TPU v7x, 32 devices: a whole 2x2x4 slice. The times are simulated.
32 devices in a mesh: dp: 16 (over z, y, x), mod: 2 (over core).
Axes of the slice: x: 2, y: 2, z: 4, core: 2. Of those that a mesh axis runs over, the one named last changes fastest.
Arguments:
- vision_feats: bfloat16 [2048, 2, 64, 512], P('dp', None, None, 'mod'), may hold values from -6 to 6
- vision_grid: int32 [2048, 2, 2], P(('dp', 'mod')), may hold values from 5 to 8
- proprio: bfloat16 [2048, 2, 16, 32], P(('dp', 'mod')), may hold values from -6 to 6
- proprio_mask: int32 [2048, 2, 16], P(('dp', 'mod')), may hold values from 0 to 1, as said below
- token_valid: int32 [2048, 64], P(('dp', 'mod')), may hold values from 0 to 1, as said below
- mix_weight: int32 [2048], P(('dp', 'mod')), may hold values from 1 to 4
- out_cot: bfloat16 [2048, 64, 128], P(('dp', 'mod')), may hold values from -6 to 6
- feat_proj: bfloat16 [512, 128], P('mod'), may hold values from -0.25 to 0.25
- vis_query: bfloat16 [16, 128], replicated, may hold values from -6 to 6
- vis_wq: bfloat16 [128, 128], replicated, may hold values from -0.5 to 0.5
- vis_kv: bfloat16 [128, 256], replicated, may hold values from -0.5 to 0.5
- vis_wo: bfloat16 [128, 128], replicated, may hold values from -1.5 to 1.5
- prop_w1: bfloat16 [32, 128], replicated, may hold values from -1 to 1
- prop_w2: bfloat16 [128, 128], replicated, may hold values from -0.5 to 0.5
- prop_query: bfloat16 [16, 128], replicated, may hold values from -6 to 6
- prop_wq: bfloat16 [128, 128], replicated, may hold values from -0.5 to 0.5
- prop_kv: bfloat16 [128, 256], replicated, may hold values from -0.5 to 0.5
- prop_wo: bfloat16 [128, 128], replicated, may hold values from -1.5 to 1.5
- ln1_gain: bfloat16 [128], replicated, may hold values from 0.099609375 to 1.8984375
- ln1_bias: bfloat16 [128], replicated, may hold values from -3 to 3
- qkv_weight: bfloat16 [128, 384], replicated, may hold values from -0.5 to 0.5
- attn_out: bfloat16 [128, 128], replicated, may hold values from -1.5 to 1.5
- ln2_gain: bfloat16 [128], replicated, may hold values from 0.099609375 to 1.8984375
- ln2_bias: bfloat16 [128], replicated, may hold values from -3 to 3
- mlp_in: bfloat16 [128, 512], replicated, may hold values from -0.5 to 0.5
- mlp_out: bfloat16 [512, 128], replicated, may hold values from -0.25 to 0.25
Outputs:
- output: bfloat16 [2048, 64, 128], P(('dp', 'mod'))
- grad_vision: bfloat16 [2048, 2, 64, 512], P('dp', None, None, 'mod')
- grad_proprio: bfloat16 [2048, 2, 16, 32], P(('dp', 'mod'))
- grad_feat_proj: float32 [512, 128], P('mod')
- grad_vis_query: float32 [16, 128], replicated
- grad_vis_wq: float32 [128, 128], replicated
- grad_vis_kv: float32 [128, 256], replicated
- grad_vis_wo: float32 [128, 128], replicated
- grad_prop_w1: float32 [32, 128], replicated
- grad_prop_w2: float32 [128, 128], replicated
- grad_prop_query: float32 [16, 128], replicated
- grad_prop_wq: float32 [128, 128], replicated
- grad_prop_kv: float32 [128, 256], replicated
- grad_prop_wo: float32 [128, 128], replicated
- grad_ln1_gain: float32 [128], replicated
- grad_ln1_bias: float32 [128], replicated
- grad_qkv_weight: float32 [128, 384], replicated
- grad_attn_out: float32 [128, 128], replicated
- grad_ln2_gain: float32 [128], replicated
- grad_ln2_bias: float32 [128], replicated
- grad_mlp_in: float32 [128, 512], replicated
- grad_mlp_out: float32 [512, 128], replicated
- rms: float32 [3], replicated
Inputs may be any that keep to these rules, and one draw needn't show every extreme that they name: `proprio_mask`: frame 0 of every step is real. `token_valid`: token 0 of every sample is valid.
All inputs are finite; a program needn't handle non-finite values.
Results may differ from a plain program's by a relative error of at most 0.02.
The roundings to bfloat16 on the way count: a program that leaves them out, or rounds other values in their place, can miss the bound.
Values may be sent and summed in bfloat16 or wider, within the bound.
A program may use at most 256 MiB of HBM per device.

v0:
```python
import functools
import math

import jax
import jax.numpy as jnp
from jax import lax
from jax.sharding import PartitionSpec as P

HEADS = 8
HEAD = 16


def round_value(v):
    return lax.optimization_barrier(v.astype(jnp.bfloat16)).astype(jnp.float32)


def pass_value(v):
    return v


def keep_rounded(v):
    return (round_value(v), None)


def pass_grad(kept, grad):
    return (grad,)


def keep_plain(v):
    return (v, None)


def round_grad(kept, grad):
    return (round_value(grad),)


def rounders():
    value_round = jax.custom_vjp(round_value)
    grad_round = jax.custom_vjp(pass_value)
    value_round.defvjp(keep_rounded, pass_grad)
    grad_round.defvjp(keep_plain, round_grad)
    return (value_round, grad_round)


def low(v):
    return rounders()[0](v)


def low_back(v):
    return rounders()[1](v)


def product(left, right):
    return jnp.matmul(left, right, precision=lax.Precision.HIGHEST)


def attend(query, keys, values, key_keep):
    full_shape = query.shape
    query_heads = query.reshape(query.shape[:-1] + (HEADS, HEAD))
    key_heads = keys.reshape(keys.shape[:-1] + (HEADS, HEAD))
    value_heads = values.reshape(values.shape[:-1] + (HEADS, HEAD))
    scores = jnp.einsum(
        "...qhd,...khd->...hqk", query_heads, key_heads, precision=lax.Precision.HIGHEST
    ) / math.sqrt(HEAD)
    scores = jnp.where(key_keep[..., None, None, :] > 0, scores, -1e30)
    peak_score = jnp.max(scores, axis=-1, keepdims=True)
    weights = jnp.exp(scores - peak_score)
    weights = low(weights / jnp.sum(weights, axis=-1, keepdims=True))
    mixed = jnp.einsum(
        "...hqk,...khd->...qhd", weights, value_heads, precision=lax.Precision.HIGHEST
    )
    return mixed.reshape(full_shape)


def layer_norm(values, gain, shift):
    centered = values - jnp.mean(values, axis=-1, keepdims=True)
    spread = jnp.mean(centered * centered, axis=-1, keepdims=True)
    return centered * lax.rsqrt(spread + 1e-05) * gain + shift


def cross_stem(tokens, learned, w_query, w_kv, w_out, key_keep):
    width = learned.shape[1]
    query = low_back(low(product(learned, w_query)))
    key_value = low_back(low(product(tokens, w_kv)))
    query = jnp.broadcast_to(query, tokens.shape[:-2] + query.shape)
    mixed = attend(query, key_value[..., :width], key_value[..., width:], key_keep)
    return low_back(product(low(mixed), w_out))


def vision_stem(tok_sum, vis_weights, vis_keep):
    vis_query, vis_wq, vis_kv, vis_wo = vis_weights
    tokens = low_back(low(tok_sum))
    return cross_stem(tokens, vis_query, vis_wq, vis_kv, vis_wo, vis_keep)


def trunk_pass(vision_lat, prop_frames, rest_weights, prop_keep, tok_keep):
    (
        prop_w1,
        prop_w2,
        prop_query,
        prop_wq,
        prop_kv,
        prop_wo,
        ln1_gain,
        ln1_bias,
        qkv_weight,
        attn_out,
        ln2_gain,
        ln2_bias,
        mlp_in,
        mlp_out,
    ) = rest_weights
    width = prop_query.shape[1]
    hidden = low(jax.nn.silu(product(prop_frames, prop_w1)))
    prop_tokens = low_back(low(product(hidden, prop_w2)))
    prop_lat = cross_stem(prop_tokens, prop_query, prop_wq, prop_kv, prop_wo, prop_keep)
    samples = vision_lat.shape[0]
    stream = jnp.stack([vision_lat, prop_lat], axis=2).reshape(samples, -1, width)
    normed = low(layer_norm(stream, ln1_gain, ln1_bias))
    qkv_all = low_back(low(product(normed, qkv_weight)))
    mixed = attend(
        qkv_all[..., :width], qkv_all[..., width : 2 * width], qkv_all[..., 2 * width :], tok_keep
    )
    attn_branch = low_back(product(low(mixed), attn_out))
    middle = stream + attn_branch
    normed_two = low(layer_norm(middle, ln2_gain, ln2_bias))
    up_proj = low_back(product(normed_two, mlp_in))
    activated = low(jax.nn.gelu(up_proj))
    mlp_branch = low_back(product(activated, mlp_out))
    output = middle + mlp_branch
    valid = tok_keep[..., None]
    statistics = jnp.stack(
        [
            jnp.sum(output * output * valid),
            jnp.sum(attn_branch * attn_branch * valid),
            jnp.sum(mlp_branch * mlp_branch * valid),
            jnp.sum(tok_keep),
        ]
    )
    return (output, statistics)


def grid_mask(grid_sizes, slot_count):
    side = math.isqrt(slot_count)
    slots = jnp.arange(slot_count, dtype=jnp.int32)
    rows_ok = (slots // side)[None, None, :] < grid_sizes[..., 0:1]
    cols_ok = (slots % side)[None, None, :] < grid_sizes[..., 1:2]
    return (rows_ok & cols_ok).astype(jnp.float32)


def pack_flat(items):
    return jnp.concatenate([jnp.ravel(item) for item in items])


def unpack_flat(flat, shapes):
    pieces = []
    offset = 0
    for shape in shapes:
        count = math.prod(shape)
        pieces.append(flat[offset : offset + count].reshape(shape))
        offset = offset + count
    return pieces


def per_device(
    vision_feats,
    vision_grid,
    proprio,
    proprio_mask,
    token_valid,
    mix_weight,
    out_cot,
    feat_proj,
    vis_query,
    vis_wq,
    vis_kv,
    vis_wo,
    prop_w1,
    prop_w2,
    prop_query,
    prop_wq,
    prop_kv,
    prop_wo,
    ln1_gain,
    ln1_bias,
    qkv_weight,
    attn_out,
    ln2_gain,
    ln2_bias,
    mlp_in,
    mlp_out,
):
    slot_count = vision_feats.shape[2]
    prop_keep = proprio_mask.astype(jnp.float32)
    tok_keep = token_valid.astype(jnp.float32)
    vis_weights = tuple((item.astype(jnp.float32) for item in (vis_query, vis_wq, vis_kv, vis_wo)))
    rest_weights = tuple(
        (
            item.astype(jnp.float32)
            for item in (
                prop_w1,
                prop_w2,
                prop_query,
                prop_wq,
                prop_kv,
                prop_wo,
                ln1_gain,
                ln1_bias,
                qkv_weight,
                attn_out,
                ln2_gain,
                ln2_bias,
                mlp_in,
                mlp_out,
            )
        )
    )
    partial_terms = jnp.einsum(
        "stvf,fd->stvd", vision_feats, feat_proj, preferred_element_type=jnp.float32
    )
    partial_terms = partial_terms.astype(jnp.bfloat16).astype(jnp.float32)
    tok_sum = lax.psum_scatter(
        partial_terms.astype(jnp.bfloat16), "mod", scatter_dimension=0, tiled=True
    ).astype(jnp.float32)
    vis_keep = grid_mask(vision_grid, slot_count)
    vision_lat, vis_pull = jax.vjp(
        functools.partial(vision_stem, vis_keep=vis_keep), tok_sum, vis_weights
    )
    trunk_local = functools.partial(trunk_pass, prop_keep=prop_keep, tok_keep=tok_keep)
    output, trunk_pull, statistics = jax.vjp(
        trunk_local, vision_lat, proprio.astype(jnp.float32), rest_weights, has_aux=True
    )
    cot_seed = out_cot.astype(jnp.float32) * mix_weight.astype(jnp.float32)[:, None, None]
    grad_lat, grad_frames, grad_rest = trunk_pull(cot_seed)
    grad_tokens, grad_vis = vis_pull(grad_lat)
    token_grads = lax.all_gather(grad_tokens.astype(jnp.bfloat16), "mod", axis=0, tiled=True)
    grad_weights = tuple(grad_vis) + tuple(grad_rest)
    grad_vision = jnp.einsum(
        "stvd,fd->stvf", token_grads, feat_proj, preferred_element_type=jnp.float32
    ).astype(jnp.bfloat16)
    grad_block = jnp.einsum(
        "stvf,stvd->fd", vision_feats, token_grads, preferred_element_type=jnp.float32
    )
    shapes = [item.shape for item in grad_weights] + [statistics.shape]
    flat_local = pack_flat(list(grad_weights) + [statistics])
    flat_total = lax.psum(flat_local, ("dp", "mod"))
    pieces = unpack_flat(flat_total, shapes)
    grad_block = lax.psum(grad_block, "dp")
    grads = pieces[:-1]
    totals = pieces[-1]
    width = output.shape[2]
    rms = jnp.sqrt(totals[:3] / (totals[3] * width))
    return (
        output.astype(jnp.bfloat16),
        grad_vision,
        grad_frames.astype(jnp.bfloat16),
        grad_block,
        grads[0],
        grads[1],
        grads[2],
        grads[3],
        grads[4],
        grads[5],
        grads[6],
        grads[7],
        grads[8],
        grads[9],
        grads[10],
        grads[11],
        grads[12],
        grads[13],
        grads[14],
        grads[15],
        grads[16],
        grads[17],
        rms,
    )


def solution(mesh):
    return jax.shard_map(
        per_device,
        mesh=mesh,
        in_specs=(
            P("dp", None, None, "mod"),
            P(("dp", "mod"), None, None),
            P(("dp", "mod"), None, None, None),
            P(("dp", "mod"), None, None),
            P(("dp", "mod"), None),
            P(("dp", "mod")),
            P(("dp", "mod"), None, None),
            P("mod", None),
            P(),
            P(),
            P(),
            P(),
            P(),
            P(),
            P(),
            P(),
            P(),
            P(),
            P(),
            P(),
            P(),
            P(),
            P(),
            P(),
            P(),
            P(),
        ),
        out_specs=(
            P(("dp", "mod"), None, None),
            P("dp", None, None, "mod"),
            P(("dp", "mod"), None, None, None),
            P("mod", None),
            P(),
            P(),
            P(),
            P(),
            P(),
            P(),
            P(),
            P(),
            P(),
            P(),
            P(),
            P(),
            P(),
            P(),
            P(),
            P(),
            P(),
            P(),
            P(),
        ),
        check_vma=False,
    )
```

profile of v0, /device:TPU:25, one launch (start us, length us, event | category | flops | bytes accessed | tf_op | source)
XLA Modules:
  0.0 813.0 jit_solution(15733467935543915362)
XLA Ops:
  7.3 14.8 %fusion.51 = bf16[128,2,64,128]{3,0,2,1:T(8,128)(2,1)} fusion(bf16[128,2,64,256]{3,2,1,0:T(8,128)(2,1)} %param.26, bf16[256,128]{1,0:T(8,128)(2,1)} %param.33), kind=kOutput, calls=%fused_computation.81 | convolution fusion | flops 1075838976 | bytes 12648448 | tf_op jit(solution)/shard_map/stvf,fd->stvd/dot_general | solution.py:218
  52.2 8.8 %fusion.26 = (f32[64,2,8,16]{3,2,1,0:T(8,128)S(1)}, f32[64,2,8,16,16]{3,4,2,1,0:T(8,128)S(1)}) fusion(pred[64,2,16]{2,1,0:T(4,128)(4,1)S(1)} %copy.270, bf16[64,2,16,8,16]{4,2,3,1,0:T(8,128)(2,1)} %copy.273, f32[16,8,16]{2,0,1:T(8,128)S(1)} %copy.271), kind=kOutput, calls=%fused_computation.52 | convolution fusion | flops 51101696 | bytes 1648640 | tf_op jit(solution)/shard_map/jvp(...qhd,...khd->...hqk)/dot_general | solution.py:62
  89.9 10.7 %fusion.24 = (f32[64,2,8,16]{3,2,1,0:T(8,128)S(1)}, f32[64,2,8,16,64]{4,3,2,1,0:T(8,128)S(1)}) fusion(pred[64,2,64]{2,1,0:T(4,128)(4,1)S(1)} %fusion.92, bf16[64,2,64,8,16]{2,4,3,1,0:T(8,128)(2,1)} %bitcast.360, f32[16,8,16]{0,2,1:T(8,128)S(1)} %bitcast.382), kind=kOutput, calls=%fused_computation.50 | convolution fusion | flops 204455936 | bytes 6373376 | tf_op jit(solution)/shard_map/jvp(...qhd,...khd->...hqk)/dot_general | solution.py:62
  106.9 9.1 %convert_reduce_fusion.2 = (f32[64,2,8,16]{3,2,1,0:T(8,128)}, pred[64,2,8,16,64]{4,3,2,1,0:T(8,128)(4,1)}, bf16[64,2,8,16,64]{4,3,2,1,0:T(8,128)(2,1)}) fusion(f32[64,2,8,16]{3,2,1,0:T(8,128)S(1)} %get-tuple-element.180, f32[64,2,8,16,64]{4,3,2,1,0:T(8,128)S(1)} %get-tuple-element.181, pred[64,2,64]{2,1,0:T(4,128)(4,1)S(1)} %fusion.92, ...), kind=kLoop, calls=%fused_computation.31 | loop fusion | flops 8372224 | bytes 7544832 | tf_op jit(solution)/shard_map/jvp()/reduce_sum | solution.py:66
  163.2 12.7 %convert_reduce_fusion = (f32[64,8,64]{2,1,0:T(8,128)}, pred[64,8,64,64]{2,3,1,0:T(32,128)(4,1)}, bf16[64,8,64,64]{2,3,1,0:T(8,128)(2,1)}) fusion(f32[64,8,64]{2,1,0:T(8,128)S(1)} %get-tuple-element.182, f32[64,8,64,64]{2,3,1,0:T(8,128)S(1)} %get-tuple-element.183, pred[64,64]{1,0:T(8,128)(4,1)S(1)} %broadcast_compare_fusion, f32[64,8,64]{2,1,0:T(8,128)S(1)} %fusion.29), kind=kLoop, calls=%fused_computation.1 | loop fusion | flops 16744448 | bytes 15077376 | tf_op jit(solution)/shard_map/jvp()/reduce_sum | solution.py:66
  213.8 14.6 %fusion.138 = f32[64,8,16,64]{3,2,1,0:T(8,128)} fusion(f32[64,8,16,64]{3,2,1,0:T(8,128)S(1)} %bitcast.353, bf16[64,8,64,64]{2,3,1,0:T(8,128)(2,1)S(1)} %bitcast.342), kind=kOutput, calls=%fused_computation.236 | convolution fusion | flops 402653184 | bytes 8388608 | tf_op jit(solution)/shard_map/transpose(jvp(...hqk,...khd->...qhd))/dot_general | solution.py:69
  228.3 20.5 %multiply_reduce_fusion = (f32[64,8,64]{2,1,0:T(8,128)}, f32[64,8,64,64]{2,3,1,0:T(8,128)}) fusion(f32[64,8,64]{2,1,0:T(8,128)S(1)} %copy-done.49, f32[64,8,64]{2,1,0:T(8,128)S(1)} %get-tuple-element.182, f32[64,8,64,64]{2,3,1,0:T(8,128)} %copy-done.2, pred[64,64]{1,0:T(8,128)(4,1)S(1)} %broadcast_compare_fusion, f32[64,8,16,64]{3,2,1,0:T(8,128)S(1)} %bitcast.354, ...), kind=kOutput, calls=%fused_computation.3 | convolution fusion | flops 415203328 | bytes 20320256 | tf_op jit(solution)/shard_map/transpose(jvp(...hqk,...khd->...qhd))/dot_general | solution.py:69
  249.9 19.5 %fusion.128 = (f32[64,8,64]{2,1,0:T(8,128)S(1)}, f32[64,8,64,64]{2,3,1,0:T(8,128)}) fusion(f32[64,8,64]{2,1,0:T(8,128)S(1)} %get-tuple-element.182, f32[64,8,64,64]{2,3,1,0:T(8,128)} %copy-done.2, pred[64,64]{1,0:T(8,128)(4,1)S(1)} %broadcast_compare_fusion, f32[64,8,64]{2,1,0:T(8,128)S(1)} %neg.39, f32[64,8,64,64]{2,3,1,0:T(8,128)} %get-tuple-element.188, ...), kind=kLoop, calls=%fused_computation.227 | loop fusion | flops 14647296 | bytes 25694208 | tf_op jit(solution)/shard_map/transpose(jvp())/reduce_sum | solution.py:67
  269.4 16.0 %fusion.2 = f32[64,8,64,16]{2,3,1,0:T(8,128)} fusion(bf16[64,64,8,16]{1,3,2,0:T(8,128)(2,1)S(1)} %bitcast.370, f32[64,8,64,64]{2,3,1,0:T(8,128)} %get-tuple-element.136, pred[64,8,64,64]{2,3,1,0:T(32,128)(4,1)S(1)} %copy-done.37, f32[64,8,64]{2,1,0:T(8,128)S(1)} %negate_divide_fusion.2, pred[64,64]{1,0:T(8,128)(4,1)S(1)} %broadcast_compare_fusion), kind=kOutput, calls=%fused_computation.11 | convolution fusion | flops 411041792 | bytes 13766656 | tf_op jit(solution)/shard_map/transpose(jvp(...qhd,...khd->...hqk))/dot_general | solution.py:62
  285.5 21.1 %fusion.3 = f32[64,8,64,16]{2,3,1,0:T(8,128)} fusion(bf16[64,64,8,16]{1,3,2,0:T(8,128)(2,1)S(1)} %bitcast.368, f32[64,8,64,64]{2,3,1,0:T(8,128)} %get-tuple-element.136, pred[64,8,64,64]{2,3,1,0:T(32,128)(4,1)S(1)} %copy-done.37, f32[64,8,64]{2,1,0:T(8,128)S(1)} %negate_divide_fusion.2, pred[64,64]{1,0:T(8,128)(4,1)S(1)} %broadcast_compare_fusion), kind=kOutput, calls=%fused_computation.12 | convolution fusion | flops 411041792 | bytes 13766656 | tf_op jit(solution)/shard_map/transpose(jvp(...qhd,...khd->...hqk))/dot_general | solution.py:62
  347.1 14.7 %fusion.140 = f32[64,2,8,16,16]{4,3,2,1,0:T(8,128)} fusion(f32[64,2,8,16,16]{4,3,2,1,0:T(8,128)} %copy.306, bf16[64,2,8,16,16]{3,4,2,1,0:T(8,128)(2,1)} %copy-done.6), kind=kOutput, calls=%fused_computation.238 | convolution fusion | flops 50331648 | bytes 2621440 | tf_op jit(solution)/shard_map/transpose(jvp(...hqk,...khd->...qhd))/dot_general | solution.py:69
  361.8 15.3 %multiply_reduce_fusion.1 = (f32[64,2,8,16]{3,2,1,0:T(8,128)}, f32[64,2,8,16,16]{3,4,2,1,0:T(8,128)}) fusion(f32[64,2,8,16]{3,2,1,0:T(8,128)} %multiply_divide_fusion, f32[64,2,8,16]{3,2,1,0:T(8,128)S(1)} %copy-done.26, f32[64,2,8,16,16]{3,4,2,1,0:T(8,128)} %copy-done.4, pred[64,2,16]{2,1,0:T(4,128)(4,1)S(1)} %copy-done.47, ...), kind=kOutput, calls=%fused_computation.28 | convolution fusion | flops 51888128 | bytes 3868672 | tf_op jit(solution)/shard_map/transpose(jvp(...hqk,...khd->...qhd))/dot_general | solution.py:69
  390.1 12.8 %fusion.71 = bf16[16,8,16]{2,0,1:T(8,128)(2,1)S(1)} fusion(f32[64,2,8,16,16]{3,4,2,1,0:T(8,128)S(1)} %select_multiply_fusion.3, bf16[64,2,16,8,16]{0,4,3,2,1:T(8,128)(2,1)S(1)} %bitcast.365), kind=kOutput, calls=%fused_computation.130 | convolution fusion | flops 50333696 | bytes 1576960 | tf_op jit(solution)/shard_map/transpose(jvp(...qhd,...khd->...hqk))/dot_general | solution.py:62
  402.9 9.6 %fusion.48 = f32[64,2,16,8,16]{4,2,3,1,0:T(8,128)} fusion(f32[64,2,8,16,16]{3,4,2,1,0:T(8,128)S(1)} %select_multiply_fusion.3, f32[16,8,16]{2,0,1:T(8,128)S(1)} %copy-done.56), kind=kOutput, calls=%fused_computation.77 | convolution fusion | flops 50331648 | bytes 2105344 | tf_op jit(solution)/shard_map/transpose(jvp(...qhd,...khd->...hqk))/dot_general | solution.py:62
  445.0 13.0 %fusion.139 = f32[64,2,8,16,64]{4,3,2,1,0:T(8,128)} fusion(f32[64,2,8,16,16]{3,4,2,1,0:T(8,128)} %copy.300, bf16[64,2,8,16,64]{4,3,2,1,0:T(8,128)(2,1)} %get-tuple-element.145), kind=kOutput, calls=%fused_computation.237 | convolution fusion | flops 201326592 | bytes 7340032 | tf_op jit(solution)/shard_map/transpose(jvp(...hqk,...khd->...qhd))/dot_general | solution.py:69
  458.1 11.5 %multiply_reduce_fusion.2 = (f32[64,2,8,16]{3,2,1,0:T(8,128)S(1)}, f32[64,2,8,16,64]{4,3,2,1,0:T(8,128)S(1)}) fusion(f32[64,2,8,16]{3,2,1,0:T(8,128)S(1)} %copy-done.38, f32[64,2,8,16]{3,2,1,0:T(8,128)S(1)} %copy-done.18, f32[64,2,8,16,64]{4,3,2,1,0:T(8,128)} %copy-done.3, pred[64,2,64]{2,1,0:T(4,128)(4,1)S(1)} %copy-done.45, ...), kind=kOutput, calls=%fused_computation.33 | convolution fusion | flops 207601664 | bytes 11739136 | tf_op jit(solution)/shard_map/transpose(jvp(...hqk,...khd->...qhd))/dot_general | solution.py:69
  469.7 10.9 %fusion.126 = (f32[64,2,8,16]{3,2,1,0:T(8,128)S(1)}, f32[64,2,8,16,64]{4,3,2,1,0:T(8,128)S(1)}) fusion(f32[64,2,8,16]{3,2,1,0:T(8,128)S(1)} %copy-done.18, f32[64,2,8,16,64]{4,3,2,1,0:T(8,128)S(1)} %bitcast.338, pred[64,2,64]{2,1,0:T(4,128)(4,1)S(1)} %copy-done.45, f32[64,2,8,16]{3,2,1,0:T(8,128)S(1)} %neg.42, ...), kind=kLoop, calls=%fused_computation.226 | loop fusion | flops 7323648 | bytes 12853248 | tf_op jit(solution)/shard_map/transpose(jvp())/reduce_sum | solution.py:67
  480.7 8.8 %fusion.70 = bf16[16,8,16]{2,0,1:T(8,128)(2,1)S(1)} fusion(bf16[64,2,64,8,16]{2,4,3,1,0:T(8,128)(2,1)S(1)} %bitcast.361, f32[64,2,8,16,64]{4,3,2,1,0:T(8,128)S(1)} %get-tuple-element.132, pred[64,2,8,16,64]{4,3,2,1,0:T(8,128)(4,1)} %get-tuple-element.134, f32[64,2,8,16]{3,2,1,0:T(8,128)S(1)} %negate_divide_fusion.1, pred[64,2,64]{2,1,0:T(4,128)(4,1)S(1)} %copy-done.45), kind=kOutput, calls=%fused_computation.129 | convolution fusion | flops 205522944 | bytes 7417856 | tf_op jit(solution)/shard_map/transpose(jvp(...qhd,...khd->...hqk))/dot_general | solution.py:62
  489.7 11.2 %fusion.28 = f32[64,2,8,64,16]{3,4,2,1,0:T(8,128)} fusion(f32[64,2,8,16,64]{4,3,2,1,0:T(8,128)S(1)} %get-tuple-element.132, pred[64,2,8,16,64]{4,3,2,1,0:T(8,128)(4,1)S(1)} %copy-done.43, f32[64,2,8,16]{3,2,1,0:T(8,128)S(1)} %negate_divide_fusion.1, f32[16,8,16]{0,2,1:T(8,128)S(1)} %bitcast.383, pred[64,2,64]{2,1,0:T(4,128)(4,1)S(1)} %copy-done.45), kind=kOutput, calls=%fused_computation.56 | convolution fusion | flops 205520896 | bytes 9519104 | tf_op jit(solution)/shard_map/transpose(jvp(...qhd,...khd->...hqk))/dot_general | solution.py:62
  527.2 20.6 %concatenate.3 = f32[352772]{0:T(1024)} concatenate(f32[2048]{0:T(1024)S(1)} %convolution_bitcast_fusion.16, f32[16384]{0:T(1024)S(1)} %bitcast.385, f32[32768]{0:T(1024)S(1)} %bitcast.380, f32[16384]{0:T(1024)S(1)} %copy-done.68, f32[4096]{0:T(1024)S(1)} %convolution_bitcast_fusion.14, f32[16384]{0:T(1024)S(1)} %convolution_bitcast_fusion.3, ...), dimensions={0} | concatenate | bytes 2822176 | tf_op jit(solution)/shard_map/concatenate | solution.py:152
  558.3 119.7 %all-reduce.12.cloned.1.call-done = f32[352772]{0:T(1024)} async-done(((f32[352772]{0:T(1024)}), f32[352772]{0:T(1024)}) %all-reduce.12.cloned.1.call-update) | async-done | bytes 1411104 | tf_op jit(solution)/shard_map/psum | solution.py:246
  702.8 13.8 %convolution_convert_fusion = bf16[128,2,64,256]{3,0,2,1:T(8,128)(2,1)} fusion(bf16[128,2,64,128]{3,2,1,0:T(8,128)(2,1)} %all-gather.2.cloned.1.call-done, bf16[256,128]{1,0:T(8,128)(2,1)S(1)} %copy-done.89), kind=kOutput, calls=%fused_computation.54 | convolution fusion | flops 1077936128 | bytes 12648448 | tf_op jit(solution)/shard_map/stvd,fd->stvf/dot_general | solution.py:238
  716.6 11.8 %copy.324 = bf16[128,2,64,256]{3,2,1,0:T(8,128)(2,1)} copy(bf16[128,2,64,256]{3,0,2,1:T(8,128)(2,1)} %convolution_convert_fusion) | data formatting | bytes 16777216
  728.4 76.2 %all-reduce.10.cloned.1.call-done = f32[256,128]{0,1:T(8,128)} async-done(((f32[256,128]{0,1:T(8,128)}), f32[256,128]{0,1:T(8,128)}) %all-reduce.10.cloned.1.call-update) | async-done | bytes 131088 | tf_op jit(solution)/shard_map/psum | solution.py:248
  (405 shorter events, 298.8 us)
Async XLA Ops:
  7.2 181.7 %copy-start = (bf16[128,512]{1,0:T(8,128)(2,1)S(1)}, bf16[128,512]{1,0:T(8,128)(2,1)}, u32[]{:S(2)}) copy-start(bf16[128,512]{1,0:T(8,128)(2,1)} %param.50) | copy-start | bytes 393220
  7.2 70.6 %reduce-scatter.2.cloned.1.call-start = ((), (), s32[]{:S(2)}) async-start(), calls=%async_computation.1 | async-start | bytes 6291456 | tf_op jit(solution)/shard_map/reduce_scatter | solution.py:222
  22.1 655.9 %all-reduce.12.cloned.1.call-start = ((), (), s32[]{:S(2)}) async-start(), calls=%async_computation.4 | async-start | bytes 2826240 | tf_op jit(solution)/shard_map/psum | solution.py:246
  34.3 30.0 %copy-start.46 = (pred[64,2,16]{2,1,0:T(4,128)(4,1)}, pred[64,2,16]{2,1,0:T(4,128)(4,1)S(1)}, u32[]{:S(2)}) copy-start(pred[64,2,16]{2,1,0:T(4,128)(4,1)S(1)} %copy.270) | copy-start | bytes 6148
  35.3 16.9 %copy-start.55 = (f32[16,8,16]{2,0,1:T(8,128)}, f32[16,8,16]{2,0,1:T(8,128)S(1)}, u32[]{:S(2)}) copy-start(f32[16,8,16]{2,0,1:T(8,128)S(1)} %copy.271) | copy-start | bytes 24580
  35.4 54.5 %copy-start.70 = (f32[16,128]{0,1:T(8,128)}, f32[16,128]{0,1:T(8,128)S(1)}, u32[]{:S(2)}) copy-start(f32[16,128]{0,1:T(8,128)S(1)} %copy.361) | copy-start | bytes 24580
  38.4 13.8 %copy-start.20 = (bf16[64,2,16,128]{0,3,2,1:T(8,128)(2,1)}, bf16[64,2,16,128]{0,3,2,1:T(8,128)(2,1)S(1)}, u32[]{:S(2)}) copy-start(bf16[64,2,16,128]{0,3,2,1:T(8,128)(2,1)S(1)} %copy.272) | copy-start | bytes 1572868
  75.3 31.6 %copy-start.44 = (pred[64,2,64]{2,1,0:T(4,128)(4,1)}, pred[64,2,64]{2,1,0:T(4,128)(4,1)S(1)}, u32[]{:S(2)}) copy-start(pred[64,2,64]{2,1,0:T(4,128)(4,1)S(1)} %fusion.92) | copy-start | bytes 24580
  213.8 14.6 %copy-start.49 = (f32[64,8,64]{2,1,0:T(8,128)S(1)}, f32[64,8,64]{2,1,0:T(8,128)}, u32[]{:S(2)}) copy-start(f32[64,8,64]{2,1,0:T(8,128)} %multiply_divide_fusion.2) | copy-start | bytes 393220
  228.3 21.5 %copy-start.36 = (f32[64,8,64]{2,1,0:T(8,128)S(1)}, f32[64,8,64]{2,1,0:T(8,128)}, u32[]{:S(2)}) copy-start(f32[64,8,64]{2,1,0:T(8,128)} %copy-done.35) | copy-start | bytes 393220
  249.8 19.5 %copy-start.48 = (f32[64,8,64]{2,1,0:T(8,128)S(1)}, f32[64,8,64]{2,1,0:T(8,128)}, u32[]{:S(2)}) copy-start(f32[64,8,64]{2,1,0:T(8,128)} %get-tuple-element.137) | copy-start | bytes 393220
  249.9 19.6 %copy-start.28 = (bf16[64,64,128]{1,2,0:T(8,128)(2,1)S(1)}, bf16[64,64,128]{1,2,0:T(8,128)(2,1)}, u32[]{:S(2)}) copy-start(bf16[64,64,128]{1,2,0:T(8,128)(2,1)} %copy.285) | copy-start | bytes 3145732
  249.9 19.6 %copy-start.37 = (pred[64,8,64,64]{2,3,1,0:T(32,128)(4,1)S(1)}, pred[64,8,64,64]{2,3,1,0:T(32,128)(4,1)}, u32[]{:S(2)}) copy-start(pred[64,8,64,64]{2,3,1,0:T(32,128)(4,1)} %get-tuple-element.138) | copy-start | bytes 6291460
  269.4 16.1 %copy-start.27 = (bf16[64,64,128]{1,2,0:T(8,128)(2,1)S(1)}, bf16[64,64,128]{1,2,0:T(8,128)(2,1)}, u32[]{:S(2)}) copy-start(bf16[64,64,128]{1,2,0:T(8,128)(2,1)} %copy.284) | copy-start | bytes 3145732
  347.1 14.7 %copy-start.26 = (f32[64,2,8,16]{3,2,1,0:T(8,128)S(1)}, f32[64,2,8,16]{3,2,1,0:T(8,128)}, u32[]{:S(2)}) copy-start(f32[64,2,8,16]{3,2,1,0:T(8,128)} %copy-done.25) | copy-start | bytes 196612
  347.1 14.7 %copy-start.47 = (pred[64,2,16]{2,1,0:T(4,128)(4,1)S(1)}, pred[64,2,16]{2,1,0:T(4,128)(4,1)}, u32[]{:S(2)}) copy-start(pred[64,2,16]{2,1,0:T(4,128)(4,1)} %copy-done.46) | copy-start | bytes 6148
  347.1 31.1 %slice-start.2 = ((s8[8388608]{0:T(1024)(128)(4,1)}), s8[4194304]{0:T(1024)(128)(4,1)S(1)}, s32[]{:S(2)}) async-start(s8[8388608]{0:T(1024)(128)(4,1)} %bitcast.339), calls=%async_computation.7 | async-start | bytes 8388608
  361.8 16.4 %slice-start.3 = ((s8[8388608]{0:T(1024)(128)(4,1)}), s8[4194304]{0:T(1024)(128)(4,1)S(1)}, s32[]{:S(2)}) async-start(s8[8388608]{0:T(1024)(128)(4,1)} %bitcast.339), calls=%async_computation.8 | async-start | bytes 8388608
  361.8 16.4 %copy-start.33 = (f32[64,2,8,16]{3,2,1,0:T(8,128)S(1)}, f32[64,2,8,16]{3,2,1,0:T(8,128)}, u32[]{:S(2)}) copy-start(f32[64,2,8,16]{3,2,1,0:T(8,128)} %copy-done.32) | copy-start | bytes 196612
  445.0 24.7 %slice-start = ((s8[8388608]{0:T(1024)(128)(4,1)}), s8[4194304]{0:T(1024)(128)(4,1)S(1)}, s32[]{:S(2)}) async-start(s8[8388608]{0:T(1024)(128)(4,1)} %bitcast.337), calls=%async_computation.5 | async-start | bytes 8388608
  526.1 21.8 %copy-start.88 = (bf16[128,256]{1,0:T(8,128)(2,1)S(1)}, bf16[128,256]{1,0:T(8,128)(2,1)}, u32[]{:S(2)}) copy-start(bf16[128,256]{1,0:T(8,128)(2,1)} %param.36) | copy-start | bytes 196612
  547.8 148.1 %all-gather.2.cloned.1.call-start = ((), (), s32[]{:S(2)}) async-start(), calls=%async_computation.2 | async-start | bytes 6291456 | tf_op jit(solution)/shard_map/all_gather | solution.py:236
  556.2 248.4 %all-reduce.10.cloned.1.call-start = ((), (), s32[]{:S(2)}) async-start(), calls=%async_computation.3 | async-start | bytes 262144 | tf_op jit(solution)/shard_map/psum | solution.py:248
  716.6 89.7 %copy-start.1 = (bf16[128,512]{1,0:T(8,128)(2,1)S(1)}, bf16[128,512]{1,0:T(8,128)(2,1)}, u32[]{:S(2)}) copy-start(bf16[128,512]{1,0:T(8,128)(2,1)} %param.50) | copy-start | bytes 393220
  (100 other events, 565.2 us)
Sparse Core Ops, SparseCore 0:
  22.2 13.7 reduce-scatter.1
  547.9 130.0 all-reduce.11
  679.6 16.1 all-gather.1
  702.9 101.6 all-reduce.9
where the time goes:
time: 826 us; the launch traced here: 813 us
  matrix products  306 us (37%)
  waiting for transfers between devices  198 us (24%)
  local copies, waits for them, and re-layouts  165 us (20%)
  other arithmetic  127 us (15%)
  between operations  16.4 us (2%)
    psum x1, waiting for transfers between devices, per_device(): flat_total = lax.psum(flat_local, ('dp', 'mod'))  120 us
    dot_general x9, matrix products, attend(): jnp.einsum('...qhd,...khd->...hqk', query_heads, key_heads, precision=lax...  107 us
    dot_general x9, matrix products, attend(): jnp.einsum('...hqk,...khd->...qhd', weights, value_heads, precision=lax.P...  104 us
    psum x1, waiting for transfers between devices, per_device(): grad_block = lax.psum(grad_block, 'dp')  76.2 us
    dot_general x36, matrix products, product(): return jnp.matmul(left, right, precision=lax.Precision.HIGHEST)  60 us
    reduce_sum x3, other arithmetic, attend(): weights = jnp.exp(scores - peak_score)  37.9 us
    reduce_sum x3, other arithmetic, attend(): peak_score = jnp.max(scores, axis=-1, keepdims=True)  29.4 us
    reshape x5, local copies, waits for them, and re-layouts, attend(): value_heads = values.reshape(values.shape[:-1] + (HEADS, HEAD))  29.3 us
  transfers between devices with their start and end apart: 4, of which 3 were waited for; matrix products, arithmetic and copies ran while one was open for 13% of the time, Pallas kernels for 0%

commit v1 on v0

v1 whole, which is shorter than its diff:
```python
import functools
import math

import jax
import jax.numpy as jnp
from jax import lax
from jax.experimental import pallas as pl
from jax.experimental.pallas import tpu as pltpu
from jax.sharding import PartitionSpec as P

HEADS = 8
HEAD = 16
WIDTH = 128
NEG = -1e30
BF = jnp.bfloat16
F32 = jnp.float32
VMEM_LIMIT = 60 * 2**20

R_WIN, R_WOUT, R_Q, R_KV, R_AO = 0, 512, 1024, 1152, 1408
R_SWO, R_VKV, R_PKV, R_W2, R_W1 = 1536, 1792, 2048, 2304, 2432
R_QV, R_QP, R_LN, R_STAT, R_END = 2464, 2480, 2496, 2500, 2560


def nn(a, b):
    return lax.dot_general(a, b, (((1,), (0,)), ((), ())), preferred_element_type=F32)


def nt(a, b):
    return lax.dot_general(a, b, (((1,), (1,)), ((), ())), preferred_element_type=F32)


def cat(items, axis):
    return jnp.concatenate(items, axis=axis)


def lane_iota(rows, lanes):
    return lax.broadcasted_iota(jnp.int32, (rows, lanes), 1)


def head_expand(value, masks):
    rows, lanes = value.shape
    out = []
    for h in range(HEADS):
        mask = cat([cat([masks[h]] * (rows // 16), 0)] * (lanes // WIDTH), 1)
        out.append(value * mask)
    return cat(out, 0)


def head_select(full):
    rows, lanes = full.shape[0] // HEADS, full.shape[1]
    head = (lane_iota(rows, lanes) & (WIDTH - 1)) >> 4
    out = full[:rows]
    for h in range(1, HEADS):
        out = jnp.where(head == h, full[h * rows : (h + 1) * rows], out)
    return out


def softmax_rows(scores):
    peak = jnp.max(scores, axis=1, keepdims=True)
    weights = jnp.exp(scores - peak)
    return weights * (1.0 / jnp.sum(weights, axis=1, keepdims=True))


def softmax_grad(weights, grad):
    return weights * (grad - jnp.sum(weights * grad, axis=1, keepdims=True))


def mean_rows(value):
    return jnp.sum(value, axis=0, keepdims=True) * (1.0 / value.shape[0])


def norm_rows(value):
    centered = value - mean_rows(value)
    scale = lax.rsqrt(mean_rows(centered * centered) + 1e-05)
    return centered * scale, scale


def norm_rows_grad(grad, hat, scale):
    return scale * (grad - mean_rows(grad) - hat * mean_rows(grad * hat))


def spread_keys(left, low_half, high_half):
    turned = cat([left[:, 64:], left[:, :64]], 1)
    zero = jnp.zeros((HEAD, WIDTH), BF)
    out = []
    for group in range(2):
        rows = []
        for s in range(2):
            for local in range(4):
                h = group * 4 + local
                part = slice(h * HEAD, (h + 1) * HEAD)
                source = left if (s == local % 2) else turned
                block = source[part] * (high_half if local % 2 else low_half)
                rows.append(cat([block, zero] if local < 2 else [zero, block], 1))
        out.append(cat(rows, 0))
    return out


def mix_keys(spread, weights, first):
    out = []
    for group in range(2):
        full = nn(spread[group], weights[group * 256 : (group + 1) * 256])
        out.append(jnp.where(first, full[:64], full[64:]))
    return cat(out, 0)


def stem_queries(query, w_query, masks):
    value = nn(query, w_query).astype(BF)
    return head_expand(value * jnp.asarray(0.25, BF), masks)


def block_kernel(
    grid_ref, po, pr, frames, aux, cot,
    vis_query, vis_wq, vis_kv, vis_wo, prop_w1, prop_w2, prop_query, prop_wq, prop_kv, prop_wo,
    ln, qkv_w, attn_out, mlp_in, mlp_out,
    out, dtok_ref, dframes, acc,
    masks_ref, qv_ref, qp_ref, wqkv_t, ao_t, win_t, wout_t, stem_t, ln_ref,
    gv_ref, gp_ref, lnacc, stat,
):
    step = pl.program_id(0)

    @pl.when(step == 0)
    def _():
        lane = lane_iota(16, WIDTH) >> 4
        for h in range(HEADS):
            masks_ref[h] = jnp.where(lane == h, 1.0, 0.0).astype(BF)
        masks = [masks_ref[h] for h in range(HEADS)]
        qv_ref[...] = stem_queries(vis_query[...], vis_wq[...], masks)
        qp_ref[...] = stem_queries(prop_query[...], prop_wq[...], masks)
        wqkv_t[...] = qkv_w[...].T
        ao_t[...] = attn_out[...].T
        win_t[...] = mlp_in[...].T
        wout_t[...] = mlp_out[...].T
        stem_t[:, :WIDTH] = vis_wo[...].T
        stem_t[:, WIDTH:] = prop_wo[...].T
        for j in range(4):
            ln_ref[j] = jnp.broadcast_to(ln[j : j + 1, :], (WIDTH, WIDTH)).T
        acc[...] = jnp.zeros_like(acc)
        gv_ref[...] = jnp.zeros_like(gv_ref)
        gp_ref[...] = jnp.zeros_like(gp_ref)
        lnacc[...] = jnp.zeros_like(lnacc)
        stat[...] = jnp.zeros_like(stat)

    masks = [masks_ref[h] for h in range(HEADS)]
    qv, qp = qv_ref[...], qp_ref[...]
    lane = lane_iota(HEAD, WIDTH)
    low_half = jnp.where(lane < 64, 1.0, 0.0).astype(BF)
    high_half = jnp.where(lane < 64, 0.0, 1.0).astype(BF)
    first = lane_iota(64, WIDTH) < 64
    low_tall = cat([low_half] * 8, 0)
    high_tall = cat([high_half] * 8, 0)

    tok = (po[...].astype(F32) + pr[...].astype(F32)).astype(BF)
    vkv = nn(tok, vis_kv[...]).astype(BF)
    vk, vv = vkv[:, :WIDTH], vkv[:, WIDTH:]
    slot = lax.broadcasted_iota(jnp.int32, (64, WIDTH), 0)
    slot_row, slot_col = slot >> 3, slot & 7
    bias = []
    for st in range(8):
        s, t = step * 4 + st // 2, st % 2
        keep = (slot_row < grid_ref[s, t, 0]) & (slot_col < grid_ref[s, t, 1])
        bias.append(jnp.where(keep, 0.0, NEG))
    vp = softmax_rows(nt(vk, qv).reshape(8, 64, WIDTH) + cat(bias, 0).reshape(8, 64, WIDTH))
    vpb = vp.reshape(512, WIDTH).astype(BF)
    vpt = vpb.T
    zero64 = jnp.zeros((64, WIDTH), BF)
    vmixed = []
    for j in range(4):
        pair = slice(128 * j, 128 * j + 128)
        block = vv[pair]
        spread = cat([cat([block[:64], zero64], 0), cat([zero64, block[64:]], 0)], 1)
        both = head_select(nn(vpt[:, pair], spread)).astype(BF)
        vmixed += [both[:, :WIDTH], both[:, WIDTH:]]

    fr = frames[...]
    pre = nn(fr, prop_w1[...])
    gate = jax.nn.sigmoid(pre)
    hidden = (pre * gate).astype(BF)
    ptok = nn(hidden, prop_w2[...]).astype(BF)
    pkv = nn(ptok, prop_kv[...]).astype(BF)
    pk, pv = pkv[:, :WIDTH], pkv[:, WIDTH:]
    pbias = jnp.broadcast_to(aux[0, 3:4, :WIDTH], (WIDTH, WIDTH)).T
    pp = softmax_rows((nt(pk, qp) + pbias).reshape(8, 16, WIDTH))
    ppb = pp.reshape(WIDTH, WIDTH).astype(BF)
    ppt = ppb.T
    zero16 = jnp.zeros((HEAD, WIDTH), BF)
    spread = cat(
        [cat([pv[16 * j : 16 * j + 16] if j == st else zero16 for j in range(8)], 0) for st in range(8)], 1
    )
    pm = head_select(nn(ppt, spread)).astype(BF)

    rows = []
    for st in range(8):
        rows.append(cat([vmixed[st], zero16], 1))
        rows.append(cat([zero16, pm[:, WIDTH * st : WIDTH * st + WIDTH]], 1))
    mixed_ext = cat(rows, 0)
    x = nt(stem_t[...], mixed_ext)
    g1, b1, g2, b2 = [cat([ln_ref[j]] * 2, 1) for j in range(4)]
    hat1, scale1 = norm_rows(x)
    n1 = (hat1 * g1 + b1).astype(BF)
    qkv = nn(wqkv_t[...], n1).astype(BF)
    qt, kt, vt = qkv[:WIDTH] * jnp.asarray(0.25, BF), qkv[WIDTH : 2 * WIDTH], qkv[2 * WIDTH :]
    kn, vn = kt.T, vt.T
    weights, weights_b, query_bd, mixed_t = [], [], [], []
    for p in range(2):
        pair = slice(128 * p, 128 * p + 128)
        column = jnp.broadcast_to(aux[0, 2:3, pair], (WIDTH, WIDTH)).T
        tbias = jnp.where(first, column[:64], column[64:])
        qbd = cat([qt[:, pair] * low_tall, qt[:, pair] * high_tall], 0)
        keys = cat([kn[128 * p : 128 * p + 64], kn[128 * p + 64 : 128 * p + 128]], 1)
        scores = nn(head_expand(keys, masks), qbd).reshape(8, 64, WIDTH) + tbias[None]
        w = softmax_rows(scores)
        wb = w.reshape(512, WIDTH).astype(BF)
        weights.append(w)
        weights_b.append(wb)
        query_bd.append(qbd)
        mixed_t.append(mix_keys(spread_keys(vt[:, pair], low_half, high_half), wb, first).astype(BF))
    mixed = cat(mixed_t, 1)
    branch = nn(ao_t[...], mixed)
    middle = x + branch
    hat2, scale2 = norm_rows(middle)
    n2 = (hat2 * g2 + b2).astype(BF)
    up = nn(win_t[...], n2)
    square = up * up
    c = math.sqrt(2.0 / math.pi)
    h = 0.5 + 0.5 * jnp.tanh(up * (c + (c * 0.044715) * square))
    act = up * h
    slope = h + act * (1.0 - h) * (2 * c + (6 * c * 0.044715) * square)
    act_b = act.astype(BF)
    mlp = nn(wout_t[...], act_b)
    final = middle + mlp
    out[...] = final.astype(BF).T
    valid, mix = aux[0, 0:1, :], aux[0, 1:2, :]
    for j, value in enumerate((final, branch, mlp)):
        stat[j : j + 1, :] += jnp.sum(value * value, axis=0, keepdims=True) * valid
    stat[3:4, :] += valid

    seed = cot[...].T.astype(F32) * mix
    dmlp = seed.astype(BF)
    acc[R_WOUT : R_WOUT + 512] += nt(act_b, dmlp)
    dup = (nn(mlp_out[...], dmlp) * slope).astype(BF)
    acc[R_WIN : R_WIN + 512] += nt(dup, n2)
    dn2 = nn(mlp_in[...], dup)
    fold = lambda v: v[:, :WIDTH] + v[:, WIDTH:]
    lnacc[2] += fold(dn2 * hat2)
    lnacc[3] += fold(dn2)
    dmid = seed + norm_rows_grad(dn2 * g2, hat2, scale2)
    dbranch = dmid.astype(BF)
    acc[R_AO : R_AO + WIDTH] += nt(mixed, dbranch)
    dmixed = nn(attn_out[...], dbranch).astype(BF)
    dq, dkv = [], []
    for p in range(2):
        pair = slice(128 * p, 128 * p + 128)
        dbd = cat([dmixed[:, pair] * low_tall, dmixed[:, pair] * high_tall], 0)
        values = cat([vn[128 * p : 128 * p + 64], vn[128 * p + 64 : 128 * p + 128]], 1)
        dw = nn(head_expand(values, masks), dbd).reshape(8, 64, WIDTH)
        ds = softmax_grad(weights[p], dw).reshape(512, WIDTH).astype(BF)
        dv = head_select(nt(weights_b[p], dbd)).astype(BF)
        dk = head_select(nt(ds, query_bd[p])).astype(BF)
        dq.append((mix_keys(spread_keys(kt[:, pair], low_half, high_half), ds, first) * 0.25).astype(BF))
        dkv.append(cat([dk[:, :WIDTH], dv[:, :WIDTH]], 1))
        dkv.append(cat([dk[:, WIDTH:], dv[:, WIDTH:]], 1))
    dq, dkv = cat(dq, 1), cat(dkv, 0)
    acc[R_Q : R_Q + WIDTH] += nt(n1, dq)
    grad = nn(n1, dkv)
    acc[R_KV : R_KV + WIDTH] += grad[:, :WIDTH]
    acc[R_KV + WIDTH : R_KV + 2 * WIDTH] += grad[:, WIDTH:]
    dn1 = nn(qkv_w[:, :WIDTH], dq) + nt(qkv_w[:, WIDTH:], dkv)
    lnacc[0] += fold(dn1 * hat1)
    lnacc[1] += fold(dn1)
    dx = (dmid + norm_rows_grad(dn1 * g1, hat1, scale1)).astype(BF)

    grad = nn(dx, mixed_ext)
    acc[R_SWO : R_SWO + WIDTH] += grad[:, :WIDTH]
    acc[R_SWO + WIDTH : R_SWO + 2 * WIDTH] += grad[:, WIDTH:]
    dstem = nn(dx.T, stem_t[...]).astype(BF)
    dw, dv, pdw, pdv = [], [], [], []
    for st in range(8):
        spread = head_expand(dstem[32 * st : 32 * st + 16, :WIDTH], masks)
        dw.append(nt(vv[64 * st : 64 * st + 64], spread))
        dv.append(nn(vpb[64 * st : 64 * st + 64], spread))
        spread = head_expand(dstem[32 * st + 16 : 32 * st + 32, WIDTH:], masks)
        pdw.append(nt(pv[16 * st : 16 * st + 16], spread))
        pdv.append(nn(ppb[16 * st : 16 * st + 16], spread))
    ds = softmax_grad(vp, cat(dw, 0).reshape(8, 64, WIDTH)).reshape(512, WIDTH).astype(BF)
    dkv = cat([nn(ds, qv).astype(BF), cat(dv, 0).astype(BF)], 1)
    dtok_ref[...] = nt(dkv, vis_kv[...]).astype(BF)
    grad = nn(tok.T, dkv)
    acc[R_VKV : R_VKV + WIDTH] += grad[:, :WIDTH]
    acc[R_VKV + WIDTH : R_VKV + 2 * WIDTH] += grad[:, WIDTH:]
    gv_ref[...] += nn(ds.T, vk)

    ds = softmax_grad(pp, cat(pdw, 0).reshape(8, 16, WIDTH)).reshape(WIDTH, WIDTH).astype(BF)
    dkv = cat([nn(ds, qp).astype(BF), cat(pdv, 0).astype(BF)], 1)
    dptok = nt(dkv, prop_kv[...]).astype(BF)
    grad = nn(ptok.T, dkv)
    acc[R_PKV : R_PKV + WIDTH] += grad[:, :WIDTH]
    acc[R_PKV + WIDTH : R_PKV + 2 * WIDTH] += grad[:, WIDTH:]
    gp_ref[...] += nn(ds.T, pk)
    acc[R_W2 : R_W2 + WIDTH] += nn(hidden.T, dptok)
    dhidden = nt(dptok, prop_w2[...])
    dpre = (dhidden * (gate * (1.0 + pre * (1.0 - gate)))).astype(BF)
    acc[R_W1 : R_W1 + 32] += nn(fr.T, dpre)
    dframes[...] = nt(dpre, prop_w1[...]).astype(BF)

    @pl.when(step == pl.num_programs(0) - 1)
    def _():
        acc[R_QV : R_QV + 16] = head_select(gv_ref[...]) * 0.25
        acc[R_QP : R_QP + 16] = head_select(gp_ref[...]) * 0.25
        for j in range(4):
            acc[R_LN + j : R_LN + j + 1] = jnp.sum(lnacc[j].T, axis=0, keepdims=True)
            acc[R_STAT + j : R_STAT + j + 1] = stat[j : j + 1, :WIDTH] + stat[j : j + 1, WIDTH:]


def whole(shape):
    return pl.BlockSpec(shape, lambda i, *_: (0,) * len(shape))


def block_call(grid_sizes, po, pr, frames, aux, cot, weights):
    steps = aux.shape[0]
    row = lambda i, *_: (i, 0)
    in_specs = [
        pl.BlockSpec(memory_space=pltpu.SMEM),
        pl.BlockSpec((512, WIDTH), row),
        pl.BlockSpec((512, WIDTH), row),
        pl.BlockSpec((128, frames.shape[1]), row),
        pl.BlockSpec((1, 8, 256), lambda i: (i, 0, 0)),
        pl.BlockSpec((256, WIDTH), row),
    ] + [whole(w.shape) for w in weights]
    out_shape = (
        jax.ShapeDtypeStruct((256 * steps, WIDTH), BF),
        jax.ShapeDtypeStruct((512 * steps, WIDTH), BF),
        jax.ShapeDtypeStruct((128 * steps, frames.shape[1]), BF),
        jax.ShapeDtypeStruct((R_END, WIDTH), F32),
    )
    out_specs = (
        pl.BlockSpec((256, WIDTH), row),
        pl.BlockSpec((512, WIDTH), row),
        pl.BlockSpec((128, frames.shape[1]), row),
        whole((R_END, WIDTH)),
    )
    scratch = [
        pltpu.VMEM((8, 16, WIDTH), BF),
        pltpu.VMEM((128, WIDTH), BF),
        pltpu.VMEM((128, WIDTH), BF),
        pltpu.VMEM((384, WIDTH), BF),
        pltpu.VMEM((128, WIDTH), BF),
        pltpu.VMEM((512, WIDTH), BF),
        pltpu.VMEM((128, 512), BF),
        pltpu.VMEM((128, 256), BF),
        pltpu.VMEM((4, WIDTH, WIDTH), F32),
        pltpu.VMEM((WIDTH, WIDTH), F32),
        pltpu.VMEM((WIDTH, WIDTH), F32),
        pltpu.VMEM((4, WIDTH, WIDTH), F32),
        pltpu.VMEM((8, 256), F32),
    ]
    return pl.pallas_call(
        block_kernel,
        grid=(steps,),
        in_specs=in_specs,
        out_specs=out_specs,
        out_shape=out_shape,
        scratch_shapes=scratch,
        compiler_params=pltpu.CompilerParams(vmem_limit_bytes=VMEM_LIMIT),
        name="stems_trunk",
    )(grid_sizes, po, pr, frames, aux, cot, *weights)


def make_aux(proprio_mask, token_valid, mix_weight):
    samples, seq = token_valid.shape
    steps = samples // 4
    valid = token_valid.reshape(steps, 1, 4 * seq).astype(F32)
    mix = jnp.broadcast_to(mix_weight.astype(F32)[:, None], (samples, seq)).reshape(steps, 1, 4 * seq)
    vbias = jnp.where(valid > 0, 0.0, NEG)
    pbias = jnp.where(proprio_mask.reshape(steps, 1, -1) > 0, 0.0, NEG)
    pbias = jnp.concatenate([pbias, jnp.zeros_like(pbias)], axis=2)
    rest = jnp.zeros((steps, 4, 4 * seq), F32)
    return jnp.concatenate([valid, mix, vbias, pbias, rest], axis=1)


def project_kernel(half, feats, proj, out):
    out[...] = nn(feats[...], proj[...]).astype(BF)


def project_call(half, feats, proj):
    rows, channels = feats.shape[0] // 2, feats.shape[1]
    steps = 8
    return pl.pallas_call(
        project_kernel,
        grid_spec=pltpu.PrefetchScalarGridSpec(
            num_scalar_prefetch=1,
            grid=(steps,),
            in_specs=[
                pl.BlockSpec((rows // steps, channels), lambda i, half: (half[0] * steps + i, 0)),
                whole(proj.shape),
            ],
            out_specs=pl.BlockSpec((rows // steps, WIDTH), lambda i, half: (i, 0)),
        ),
        out_shape=jax.ShapeDtypeStruct((rows, WIDTH), BF),
        compiler_params=pltpu.CompilerParams(vmem_limit_bytes=VMEM_LIMIT),
        cost_estimate=pl.CostEstimate(
            flops=2 * rows * channels * WIDTH, bytes_accessed=2 * rows * (channels + WIDTH), transcendentals=0
        ),
        name="project",
    )(half, feats, proj)


def feature_kernel(half, dtok, feats, proj, before, gsum_before, grad, gsum):
    @pl.when(pl.program_id(0) == 0)
    def _():
        gsum[...] = gsum_before[...]

    d = dtok[...]
    grad[...] = nt(d, proj[...]).astype(BF)
    gsum[...] += nn(d.T, feats[...])


def feature_kernel_first(half, dtok, feats, proj, grad, gsum):
    @pl.when(pl.program_id(0) == 0)
    def _():
        gsum[...] = jnp.zeros_like(gsum)

    d = dtok[...]
    grad[...] = nt(d, proj[...]).astype(BF)
    gsum[...] += nn(d.T, feats[...])


def feature_call(half, dtok, feats, proj, before=None):
    rows, channels = feats.shape[0] // 2, feats.shape[1]
    steps = 8
    in_specs = [
        pl.BlockSpec((rows // steps, WIDTH), lambda i, half: (i, 0)),
        pl.BlockSpec((rows // steps, channels), lambda i, half: (half[0] * steps + i, 0)),
        whole(proj.shape),
    ]
    args = (half, dtok, feats, proj)
    if before is not None:
        in_specs += [pl.BlockSpec(memory_space=pl.ANY), whole((WIDTH, channels))]
        args += tuple(before)
    return pl.pallas_call(
        feature_kernel_first if before is None else feature_kernel,
        grid_spec=pltpu.PrefetchScalarGridSpec(
            num_scalar_prefetch=1,
            grid=(steps,),
            in_specs=in_specs,
            out_specs=(
                pl.BlockSpec((rows // steps, channels), lambda i, half: (half[0] * steps + i, 0)),
                whole((WIDTH, channels)),
            ),
        ),
        out_shape=(
            jax.ShapeDtypeStruct((2 * rows, channels), BF),
            jax.ShapeDtypeStruct((WIDTH, channels), F32),
        ),
        input_output_aliases={} if before is None else {4: 0},
        compiler_params=pltpu.CompilerParams(vmem_limit_bytes=VMEM_LIMIT),
        cost_estimate=pl.CostEstimate(
            flops=4 * rows * channels * WIDTH, bytes_accessed=2 * rows * (2 * channels + WIDTH), transcendentals=0
        ),
        name="features",
    )(*args)


def unpack_kernel(
    total, gfeat, vis_query, vis_wq, prop_query, prop_wq,
    o_feat, o_vq, o_vwq, o_vkv, o_vwo, o_w1, o_w2, o_pq, o_pwq, o_pkv, o_pwo,
    o_g1, o_b1, o_qkv, o_ao, o_g2, o_b2, o_in, o_out, o_rms,
):
    def rows(start, count):
        return total[start : start + count]

    o_feat[...] = gfeat[...].T
    for o_query, o_w, query, w, start in (
        (o_vq, o_vwq, vis_query, vis_wq, R_QV),
        (o_pq, o_pwq, prop_query, prop_wq, R_QP),
    ):
        grad = rows(start, 16).astype(BF)
        o_query[...] = nt(grad, w[...])
        o_w[...] = lax.dot_general(
            query[...], grad, (((0,), (0,)), ((), ())), preferred_element_type=F32
        )
    for o, start in ((o_vkv, R_VKV), (o_pkv, R_PKV)):
        o[:, :WIDTH] = rows(start, WIDTH)
        o[:, WIDTH:] = rows(start + WIDTH, WIDTH)
    o_vwo[...] = rows(R_SWO, WIDTH).T
    o_pwo[...] = rows(R_SWO + WIDTH, WIDTH).T
    o_w1[...] = rows(R_W1, 32)
    o_w2[...] = rows(R_W2, WIDTH)
    for j in range(3):
        o_qkv[:, WIDTH * j : WIDTH * j + WIDTH] = rows(R_Q + WIDTH * j, WIDTH)
    o_ao[...] = rows(R_AO, WIDTH)
    o_in[...] = rows(R_WIN, 512).T
    o_out[...] = rows(R_WOUT, 512)
    for j, o in enumerate((o_g1, o_b1, o_g2, o_b2)):
        o[...] = rows(R_LN + j, 1)
    sums = jnp.sum(rows(R_STAT, 4), axis=1, keepdims=True)
    o_rms[...] = jnp.broadcast_to(jnp.sqrt(sums / (sums[3:4] * WIDTH)), (4, WIDTH))


def unpack_call(total, gfeat, vis_query, vis_wq, prop_query, prop_wq):
    shapes = [
        (gfeat.shape[1], WIDTH), (16, WIDTH), (WIDTH, WIDTH), (WIDTH, 256), (WIDTH, WIDTH), (32, WIDTH),
        (WIDTH, WIDTH), (16, WIDTH), (WIDTH, WIDTH), (WIDTH, 256), (WIDTH, WIDTH), (1, WIDTH), (1, WIDTH),
        (WIDTH, 384), (WIDTH, WIDTH), (1, WIDTH), (1, WIDTH), (WIDTH, 512), (512, WIDTH), (4, WIDTH),
    ]
    return pl.pallas_call(
        unpack_kernel,
        out_shape=[jax.ShapeDtypeStruct(s, F32) for s in shapes],
        compiler_params=pltpu.CompilerParams(vmem_limit_bytes=VMEM_LIMIT),
        name="unpack",
    )(total, gfeat, vis_query, vis_wq, prop_query, prop_wq)


def per_device(
    vision_feats, vision_grid, proprio, proprio_mask, token_valid, mix_weight, out_cot, feat_proj,
    vis_query, vis_wq, vis_kv, vis_wo, prop_w1, prop_w2, prop_query, prop_wq, prop_kv, prop_wo,
    ln1_gain, ln1_bias, qkv_weight, attn_out, ln2_gain, ln2_bias, mlp_in, mlp_out,
):
    me = lax.axis_index("mod").astype(jnp.int32)
    own, other = me.reshape(1), (1 - me).reshape(1)
    swap = [(0, 1), (1, 0)]
    feats = vision_feats.reshape(-1, vision_feats.shape[3])
    sent = project_call(other, feats, feat_proj)
    received = lax.ppermute(sent, "mod", swap)
    kept = project_call(own, feats, feat_proj)
    aux = make_aux(proprio_mask, token_valid, mix_weight)
    ln = jnp.stack([ln1_gain, ln1_bias, ln2_gain, ln2_bias]).astype(F32)
    weights = (
        vis_query, vis_wq, vis_kv, vis_wo, prop_w1, prop_w2, prop_query, prop_wq, prop_kv, prop_wo,
        ln, qkv_weight, attn_out, mlp_in, mlp_out,
    )
    frames = proprio.reshape(-1, proprio.shape[3])
    output, dtok, dframes, acc = block_call(
        vision_grid, kept, received, frames, aux, out_cot.reshape(-1, WIDTH), weights
    )
    dtok_other = lax.ppermute(dtok, "mod", swap)
    part = feature_call(own, dtok, feats, feat_proj)
    grad_vision, gfeat = feature_call(other, dtok_other, feats, feat_proj, part)
    total = lax.psum(acc, ("dp", "mod"))
    gfeat = lax.psum(gfeat, "dp")
    outs = unpack_call(total, gfeat, vis_query, vis_wq, prop_query, prop_wq)
    vectors = {11, 12, 15, 16}
    outs = [o.reshape(WIDTH) if j in vectors else o for j, o in enumerate(outs)]
    return (
        output.reshape(out_cot.shape),
        grad_vision.reshape(vision_feats.shape),
        dframes.reshape(proprio.shape),
        *outs[:-1],
        outs[-1][:3, 0],
    )


def solution(mesh):
    both = ("dp", "mod")
    return jax.shard_map(
        per_device,
        mesh=mesh,
        in_specs=(
            P("dp", None, None, "mod"),
            P(both, None, None),
            P(both, None, None, None),
            P(both, None, None),
            P(both, None),
            P(both),
            P(both, None, None),
            P("mod", None),
        ) + (P(),) * 18,
        out_specs=(
            P(both, None, None),
            P("dp", None, None, "mod"),
            P(both, None, None, None),
            P("mod", None),
        ) + (P(),) * 19,
        check_vma=False,
    )
```

time: 826 us -> 384 us (0.46)
  matrix products: 306 us -> 0 us
  local copies, waits for them, and re-layouts: 165 us -> 8.89 us
  Pallas kernels: 0 us -> 134 us
  other arithmetic: 127 us -> 0.62 us
  waiting for transfers between devices: 198 us -> 219 us
    dot_general x57 -> x0, matrix products: 306 us -> none  [the longest x9 107 us: attend(): jnp.einsum('...qhd,...khd->...hqk', query_heads, key_heads, precision=lax...]
    pallas_call x0 -> x6, Pallas kernels: none -> 134 us  [the longest x1 101 us: block_call(): pl.pallas_call(block_kernel, grid=(steps,), in_specs=in_specs, out_specs=...]
    reduce_sum x15 -> x0, other arithmetic: 93.6 us -> none  [the longest x3 37.9 us: attend(): weights = jnp.exp(scores - peak_score)]
    reshape x18 -> x0, local copies, waits for them, and re-layouts: 60.2 us -> none  [the longest x5 29.3 us: attend(): value_heads = values.reshape(values.shape[:-1] + (HEADS, HEAD))]
    slice x15 -> x1, local copies, waits for them, and re-layouts: 31 us -> 1.29 us  [per_device(): outs[-1][:3, 0]]
    psum x2, waiting for transfers between devices: 196 us -> 219 us  [the longest x1 110 us: per_device(): total = lax.psum(acc, ('dp', 'mod'))]
    transpose x5 -> x0, local copies, waits for them, and re-layouts: 21.6 us -> none  [the longest x2 15 us: attend(): jnp.einsum('...hqk,...khd->...qhd', weights, value_heads, precision=lax.P...]
    concatenate x1 -> x2, local copies, waits for them, and re-layouts: 20.6 us -> 0.79 us  [the longest x1 0.77 us: make_aux(): return jnp.concatenate([valid, mix, vbias, pbias, rest], axis=1)]
  transfers between devices with their start and end apart: 4 -> 4, of which waited for: 3 -> 2; matrix products, arithmetic and copies ran while one was open for 13% -> 1% of each run, Pallas kernels for 0% -> 6%
where the time goes in v1:
time: 384 us; the launch traced here: 378 us
  waiting for transfers between devices  219 us (57%)
  Pallas kernels  134 us (35%)
  between operations  14.2 us (4%)
  local copies, waits for them, and re-layouts  8.89 us (2%)
    psum x1, waiting for transfers between devices, per_device(): total = lax.psum(acc, ('dp', 'mod'))  110 us
    psum x1, waiting for transfers between devices, per_device(): gfeat = lax.psum(gfeat, 'dp')  109 us
    pallas_call x1, Pallas kernels, block_call(): pl.pallas_call(block_kernel, grid=(steps,), in_specs=in_specs, out_specs=...  101 us
    pallas_call x2, Pallas kernels, feature_call(): pl.pallas_call(feature_kernel_first if before is None else feature_kernel...  16.5 us
    pallas_call x2, Pallas kernels, project_call(): pl.pallas_call(project_kernel, grid_spec=pltpu.PrefetchScalarGridSpec(num...  14.3 us
  transfers between devices with their start and end apart: 4, of which 2 were waited for; matrix products, arithmetic and copies ran while one was open for 1% of the time, Pallas kernels for 6%

profile of v1, /device:TPU:25, one launch (start us, length us, event | category | flops | bytes accessed | tf_op | source)
XLA Modules:
  0.0 378.2 jit_solution(3239510796785286847)
XLA Ops:
  7.3 7.2 %project.3 = bf16[8192,128]{1,0:T(8,128)(2,1)} custom-call(s32[1]{0:T(128)} %bitcast.2.half, bf16[16384,256]{1,0:T(8,128)(2,1)} %bitcast.17, bf16[256,128]{1,0:T(8,128)(2,1)} %proj.7), custom_call_target="tpu_custom_call" | custom-call | flops 536870912 | bytes 6291456 | tf_op jit(solution)/shard_map/project/pallas_call | solution.py:388
  14.5 0.7 collective-permute-start
  15.2 0.1 broadcast_in_dim.28
  15.2 0.1 broadcast_in_dim.29
  15.3 0.1 broadcast_in_dim.30
  15.4 0.1 convert_element_type.25
  15.6 0.1 copy.55
  15.7 0.1 select_n.29
  15.8 0.7 copy.57.grid_ref
  16.5 1.5 copy.54
  18.1 0.8 concatenate.7.aux
  18.9 7.2 %project.2.po = bf16[8192,128]{1,0:T(8,128)(2,1)} custom-call(s32[1]{0:T(128)} %bitcast.half, bf16[16384,256]{1,0:T(8,128)(2,1)} %bitcast.18, bf16[256,128]{1,0:T(8,128)(2,1)} %proj.7), custom_call_target="tpu_custom_call" | custom-call | flops 536870912 | bytes 6291456 | tf_op jit(solution)/shard_map/project/pallas_call | solution.py:388
  26.1 0.6 maximum_convert_fusion.ln
  26.7 1.3 copy-done
  28.0 100.6 %stems_trunk.1 = (bf16[4096,128]{1,0:T(8,128)(2,1)}, bf16[8192,128]{1,0:T(8,128)(2,1)}, bf16[2048,32]{1,0:T(8,128)(2,1)}, f32[2560,128]{1,0:T(8,128)}) custom-call(s32[64,2,2]{2,1,0:T(2,128)} %copy.57.grid_ref, bf16[8192,128]{1,0:T(8,128)(2,1)} %project.2.po, bf16[8192,128]{1,0:T(8,128)(2,1)} %copy-done, bf16[2048,32]{1,0:T(8,128)(2,1)} %bitcast.22, ...), custom_call_target="tpu_custom_call" | custom-call | tf_op jit(solution)/shard_map/stems_trunk/pallas_call | solution.py:357
  128.6 0.1 collective-permute-start.1
  128.8 8.2 %features.2 = (bf16[16384,256]{1,0:T(8,128)(2,1)}, f32[128,256]{1,0:T(8,128)}) custom-call(s32[1]{0:T(128)} %bitcast.half, bf16[8192,128]{1,0:T(8,128)(2,1)} %get-tuple-element.52.dtok, bf16[16384,256]{1,0:T(8,128)(2,1)} %bitcast.19, bf16[256,128]{1,0:T(8,128)(2,1)} %proj.7), custom_call_target="tpu_custom_call" | custom-call | flops 1073741824 | bytes 10485760 | tf_op jit(solution)/shard_map/features/pallas_call | solution.py:440
  137.0 1.3 copy-done.1
  138.3 8.3 %features.3 = (bf16[16384,256]{1,0:T(8,128)(2,1)}, f32[128,256]{1,0:T(8,128)}) custom-call(s32[1]{0:T(128)} %bitcast.2.half, bf16[8192,128]{1,0:T(8,128)(2,1)} %copy-done.1, bf16[16384,256]{1,0:T(8,128)(2,1)} %bitcast.20, bf16[256,128]{1,0:T(8,128)(2,1)} %proj.7, bf16[16384,256]{1,0:T(8,128)(2,1)} %get-tuple-element.53.before, ...), custom_call_target="tpu_custom_call", output_to_operand_aliasing={{0}: (4, {})} | custom-call | flops 1073741824 | bytes 10485760 | tf_op jit(solution)/shard_map/features/pallas_call | solution.py:440
  146.7 1.3 copy.58
  147.9 110.3 %all-reduce.4.cloned.1.call-done.total = f32[2560,128]{1,0:T(8,128)} async-done(((f32[2560,128]{1,0:T(8,128)}), f32[2560,128]{1,0:T(8,128)}) %all-reduce.4.cloned.1.call-update) | async-done | bytes 1310736 | tf_op jit(solution)/shard_map/psum | solution.py:539
  258.3 109.1 %all-reduce.6.cloned.1.call-done.gfeat = f32[128,256]{1,0:T(8,128)} async-done(((f32[128,256]{1,0:T(8,128)}), f32[128,256]{1,0:T(8,128)}) %all-reduce.6.cloned.1.call-update) | async-done | bytes 131088 | tf_op jit(solution)/shard_map/psum | solution.py:540
  367.4 2.7 unpack.1
  370.1 1.3 slice_reduce_fusion
  (34 shorter events, 0.2 us)
Async XLA Ops:
  7.2 251.1 %all-reduce.4.cloned.1.call-start = ((), (), s32[]{:S(2)}) async-start(), calls=%async_computation | async-start | bytes 2621440 | tf_op jit(solution)/shard_map/psum | solution.py:539
  7.2 7.9 %copy-start.11 = (s32[64]{0:T(128)S(1)}, s32[64]{0:T(128)}, u32[]{:S(2)}) copy-start(s32[64]{0:T(128)} %param.31) | copy-start | bytes 772
  7.3 8.2 %copy-start.4 = (s32[64,64]{1,0:T(8,128)S(1)}, s32[64,64]{1,0:T(8,128)}, u32[]{:S(2)}) copy-start(s32[64,64]{1,0:T(8,128)} %param.30) | copy-start | bytes 49156
  7.3 8.3 %copy-start.5 = (s32[64,2,16]{0,2,1:T(8,128)S(1)}, s32[64,2,16]{0,2,1:T(8,128)}, u32[]{:S(2)}) copy-start(s32[64,2,16]{0,2,1:T(8,128)} %param.29) | copy-start | bytes 24580
  7.3 8.5 %copy-start.6 = (s32[64,2,2]{0,2,1:T(2,128)S(1)}, s32[64,2,2]{0,2,1:T(2,128)}, u32[]{:S(2)}) copy-start(s32[64,2,2]{0,2,1:T(2,128)} %param.27) | copy-start | bytes 3076
  7.3 9.3 %copy-start.3 = (bf16[64,2,16,32]{0,3,2,1:T(8,128)(2,1)S(1)}, bf16[64,2,16,32]{0,3,2,1:T(8,128)(2,1)}, u32[]{:S(2)}) copy-start(bf16[64,2,16,32]{0,3,2,1:T(8,128)(2,1)} %param.28) | copy-start | bytes 393220
  14.5 12.2 %collective-permute-start = (bf16[8192,128]{1,0:T(8,128)(2,1)}, bf16[8192,128]{1,0:T(8,128)(2,1)S(1)}, u32[]{:S(2)}, u32[]{:S(2)}) collective-permute-start(bf16[8192,128]{1,0:T(8,128)(2,1)} %project.3), channel_id=1, source_target_pairs={{0,1},{1,0},{2,3},{3,2},{4,5},{5,4},{6,7},{7,6},{8,9},{9,8},{10,11... | collective-permute-start | bytes 6291464 | tf_op jit(solution)/shard_map/ppermute | solution.py:524
  18.9 7.2 %copy-start.7 = (bf16[128]{0:T(256)(128)(2,1)S(1)}, bf16[128]{0:T(256)(128)(2,1)}, u32[]{:S(2)}) copy-start(bf16[128]{0:T(256)(128)(2,1)} %param.49) | copy-start | bytes 772
  18.9 7.2 %copy-start.8 = (bf16[128]{0:T(256)(128)(2,1)S(1)}, bf16[128]{0:T(256)(128)(2,1)}, u32[]{:S(2)}) copy-start(bf16[128]{0:T(256)(128)(2,1)} %param.48) | copy-start | bytes 772
  18.9 7.2 %copy-start.9 = (bf16[128]{0:T(256)(128)(2,1)S(1)}, bf16[128]{0:T(256)(128)(2,1)}, u32[]{:S(2)}) copy-start(bf16[128]{0:T(256)(128)(2,1)} %param.45) | copy-start | bytes 772
  18.9 7.2 %copy-start.10 = (bf16[128]{0:T(256)(128)(2,1)S(1)}, bf16[128]{0:T(256)(128)(2,1)}, u32[]{:S(2)}) copy-start(bf16[128]{0:T(256)(128)(2,1)} %param.44) | copy-start | bytes 772
  26.7 1.3 copy-start
  128.6 8.4 %collective-permute-start.1 = (bf16[8192,128]{1,0:T(8,128)(2,1)}, bf16[8192,128]{1,0:T(8,128)(2,1)S(1)}, u32[]{:S(2)}, u32[]{:S(2)}) collective-permute-start(bf16[8192,128]{1,0:T(8,128)(2,1)} %get-tuple-element.52.dtok), channel_id=1, source_target_pairs={{0,1},{1,0},{2,3},{3,2},{4,5},{5,4},{6,7},{7,6},{8,9},{9,8},{10,11... | collective-permute-start | bytes 6291464 | tf_op jit(solution)/shard_map/ppermute | solution.py:536
  128.7 238.7 %all-reduce.6.cloned.1.call-start = ((), (), s32[]{:S(2)}) async-start(), calls=%async_computation.1 | async-start | bytes 262144 | tf_op jit(solution)/shard_map/psum | solution.py:540
  137.0 1.3 copy-start.1
  138.3 8.4 %copy-start.2 = (bf16[2048,32]{1,0:T(8,128)(2,1)S(1)}, bf16[2048,32]{1,0:T(8,128)(2,1)}, u32[]{:S(2)}) copy-start(bf16[2048,32]{1,0:T(8,128)(2,1)} %get-tuple-element.56) | copy-start | bytes 393220
Sparse Core Ops, SparseCore 0:
  128.8 129.4 all-reduce.3
  264.3 103.0 all-reduce.5

commit v2 on v1

--- a/solution.py
+++ b/solution.py
@@ -467,9 +467,9 @@
     o_g1, o_b1, o_qkv, o_ao, o_g2, o_b2, o_in, o_out, o_rms,
 ):
     def rows(start, count):
-        return total[start : start + count]
-
-    o_feat[...] = gfeat[...].T
+        return total[start : start + count].astype(F32)
+
+    o_feat[...] = gfeat[...].astype(F32).T
     for o_query, o_w, query, w, start in (
         (o_vq, o_vwq, vis_query, vis_wq, R_QV),
         (o_pq, o_pwq, prop_query, prop_wq, R_QP),
@@ -491,9 +491,10 @@
     o_ao[...] = rows(R_AO, WIDTH)
     o_in[...] = rows(R_WIN, 512).T
     o_out[...] = rows(R_WOUT, 512)
+    small = rows(R_LN, 16)
     for j, o in enumerate((o_g1, o_b1, o_g2, o_b2)):
-        o[...] = rows(R_LN + j, 1)
-    sums = jnp.sum(rows(R_STAT, 4), axis=1, keepdims=True)
+        o[...] = small[j : j + 1]
+    sums = jnp.sum(small[R_STAT - R_LN : R_STAT - R_LN + 4], axis=1, keepdims=True)
     o_rms[...] = jnp.broadcast_to(jnp.sqrt(sums / (sums[3:4] * WIDTH)), (4, WIDTH))
 
 
@@ -509,6 +510,125 @@
         compiler_params=pltpu.CompilerParams(vmem_limit_bytes=VMEM_LIMIT),
         name="unpack",
     )(total, gfeat, vis_query, vis_wq, prop_query, prop_wq)
+
+
+def reduce_kernel(n, chunk, acc, gfeat, total, gsum, send_a, recv_a, send_b, recv_b, reduced, gathered, recv_d, sem_a, sem_b, sem_c, sem_d):
+    me, core = lax.axis_index("dp"), lax.axis_index("mod")
+    mesh = pl.DeviceIdType.MESH
+    partner = (me, 1 - core)
+    half = R_END // 2
+    channels = gfeat.shape[1]
+
+    barrier = pltpu.get_barrier_semaphore()
+    pl.semaphore_signal(barrier, inc=1, device_id=partner, device_id_type=mesh)
+
+    def greet(k, carry):
+        pl.semaphore_signal(barrier, inc=1, device_id=(lax.rem(me + k, n), core), device_id_type=mesh)
+        return carry
+
+    lax.fori_loop(1, n, greet, 0)
+    pl.semaphore_wait(barrier, n)
+
+    theirs = pl.ds(pl.multiple_of((1 - core) * half, 16), half)
+    mine = pl.ds(pl.multiple_of(core * half, 16), half)
+    send_a[...] = acc[theirs].astype(BF)
+    copy = pltpu.make_async_remote_copy(
+        src_ref=send_a, dst_ref=recv_a, send_sem=sem_a.at[0], recv_sem=sem_a.at[1],
+        device_id=partner, device_id_type=mesh,
+    )
+    copy.start()
+    for j in range(channels // WIDTH):
+        start = half + WIDTH * j
+        send_b[start : start + WIDTH] = gfeat[:, WIDTH * j : WIDTH * j + WIDTH].astype(BF)
+    used = half + WIDTH * (channels // WIDTH)
+    if used < n * chunk:
+        send_b[used:] = jnp.zeros((n * chunk - used, WIDTH), BF)
+    copy.wait()
+    send_b[:half] = (acc[mine] + recv_a[...].astype(F32)).astype(BF)
+
+    def scatter(k):
+        peer = lax.rem(me + k, n)
+        return pltpu.make_async_remote_copy(
+            src_ref=send_b.at[pl.ds(pl.multiple_of(peer * chunk, 16), chunk)],
+            dst_ref=recv_b.at[k - 1],
+            send_sem=sem_b.at[0, k - 1], recv_sem=sem_b.at[1, k - 1],
+            device_id=(peer, core), device_id_type=mesh,
+        )
+
+    def gather(k):
+        peer = lax.rem(me + k, n)
+        return pltpu.make_async_remote_copy(
+            src_ref=reduced,
+            dst_ref=gathered.at[pl.ds(pl.multiple_of(me * chunk, 16), chunk)],
+            send_sem=sem_c.at[0, k - 1], recv_sem=sem_c.at[1, k - 1],
+            device_id=(peer, core), device_id_type=mesh,
+        )
+
+    def start(make):
+        def body(k, carry):
+            make(k).start()
+            return carry
+
+        lax.fori_loop(1, n, body, 0)
+
+    def finish(make):
+        def body(k, carry):
+            make(k).wait()
+            return carry
+
+        lax.fori_loop(1, n, body, 0)
+
+    own = pl.ds(pl.multiple_of(me * chunk, 16), chunk)
+    start(scatter)
+    finish(scatter)
+    result = send_b[own].astype(F32)
+    result = lax.fori_loop(0, n - 1, lambda k, value: value + recv_b[k].astype(F32), result)
+    reduced[...] = result.astype(BF)
+    start(gather)
+    gathered[own] = reduced[...]
+    finish(gather)
+
+    copy = pltpu.make_async_remote_copy(
+        src_ref=gathered.at[pl.ds(0, half)], dst_ref=recv_d, send_sem=sem_d.at[0], recv_sem=sem_d.at[1],
+        device_id=partner, device_id_type=mesh,
+    )
+    copy.start()
+    total[mine] = gathered[:half]
+    for j in range(channels // WIDTH):
+        start_row = half + WIDTH * j
+        gsum[:, WIDTH * j : WIDTH * j + WIDTH] = gathered[start_row : start_row + WIDTH]
+    copy.wait()
+    total[theirs] = recv_d[...]
+
+
+def reduce_call(acc, gfeat, n):
+    half = R_END // 2
+    rows = half + WIDTH * (gfeat.shape[1] // WIDTH)
+    chunk = 16 * -(-rows // (16 * n))
+    vmem = pl.BlockSpec(memory_space=pltpu.VMEM)
+    return pl.pallas_call(
+        functools.partial(reduce_kernel, n, chunk),
+        out_shape=(jax.ShapeDtypeStruct(acc.shape, BF), jax.ShapeDtypeStruct(gfeat.shape, BF)),
+        in_specs=[vmem, vmem],
+        out_specs=(vmem, vmem),
+        scratch_shapes=[
+            pltpu.VMEM((half, WIDTH), BF),
+            pltpu.VMEM((half, WIDTH), BF),
+            pltpu.VMEM((n * chunk, WIDTH), BF),
+            pltpu.VMEM((n - 1, chunk, WIDTH), BF),
+            pltpu.VMEM((chunk, WIDTH), BF),
+            pltpu.VMEM((n * chunk, WIDTH), BF),
+            pltpu.VMEM((half, WIDTH), BF),
+            pltpu.SemaphoreType.DMA((2,)),
+            pltpu.SemaphoreType.DMA((2, n - 1)),
+            pltpu.SemaphoreType.DMA((2, n - 1)),
+            pltpu.SemaphoreType.DMA((2,)),
+        ],
+        compiler_params=pltpu.CompilerParams(
+            collective_id=0, has_side_effects=True, vmem_limit_bytes=VMEM_LIMIT
+        ),
+        name="reduce",
+    )(acc, gfeat)
 
 
 def per_device(
@@ -536,8 +656,7 @@
     dtok_other = lax.ppermute(dtok, "mod", swap)
     part = feature_call(own, dtok, feats, feat_proj)
     grad_vision, gfeat = feature_call(other, dtok_other, feats, feat_proj, part)
-    total = lax.psum(acc, ("dp", "mod"))
-    gfeat = lax.psum(gfeat, "dp")
+    total, gfeat = reduce_call(acc, gfeat, lax.axis_size("dp"))
     outs = unpack_call(total, gfeat, vis_query, vis_wq, prop_query, prop_wq)
     vectors = {11, 12, 15, 16}
     outs = [o.reshape(WIDTH) if j in vectors else o for j, o in enumerate(outs)]

time: 384 us -> 178 us (0.46); the launches traced: 378 us -> 177 us
  waiting for transfers between devices: 219 us -> 0.01 us
  Pallas kernels: 134 us -> 165 us
  between operations: 14.2 us -> 0.83 us
    psum x2 -> x0, waiting for transfers between devices: 219 us -> none  [the longest x1 110 us: per_device(): total = lax.psum(acc, ('dp', 'mod'))]
    pallas_call x0 -> x1, Pallas kernels: none -> 31.1 us  [reduce_call(): pl.pallas_call(functools.partial(reduce_kernel, n, chunk), out_shape=(jax...]
  transfers between devices with their start and end apart: 4 -> 2, of which waited for: 2 -> 0; matrix products, arithmetic and copies ran while one was open for 1% -> 4% of each run, Pallas kernels for 6% -> 9%
where the time goes in v2:
time: 178 us; the launch traced here: 177 us
  Pallas kernels  165 us (93%)
  local copies, waits for them, and re-layouts  9.89 us (6%)
    pallas_call x1, Pallas kernels, block_call(): pl.pallas_call(block_kernel, grid=(steps,), in_specs=in_specs, out_specs=...  101 us
    pallas_call x1, Pallas kernels, reduce_call(): pl.pallas_call(functools.partial(reduce_kernel, n, chunk), out_shape=(jax...  31.1 us
    pallas_call x2, Pallas kernels, feature_call(): pl.pallas_call(feature_kernel_first if before is None else feature_kernel...  16.4 us
    pallas_call x2, Pallas kernels, project_call(): pl.pallas_call(project_kernel, grid_spec=pltpu.PrefetchScalarGridSpec(num...  14.3 us
    unnamed x25, local copies, waits for them, and re-layouts  7.24 us
  transfers between devices with their start and end apart: 2, of which 0 were waited for; matrix products, arithmetic and copies ran while one was open for 4% of the time, Pallas kernels for 9%

profile of v2, /device:TPU:25, one launch (start us, length us, event | category | flops | bytes accessed | tf_op | source)
XLA Modules:
  0.0 177.0 jit_solution(9303056609031233516)
XLA Ops:
  0.7 7.2 %project.3 = bf16[8192,128]{1,0:T(8,128)(2,1)} custom-call(s32[1]{0:T(128)} %bitcast.2.half, bf16[16384,256]{1,0:T(8,128)(2,1)} %bitcast.17, bf16[256,128]{1,0:T(8,128)(2,1)} %proj.7), custom_call_target="tpu_custom_call" | custom-call | flops 536870912 | bytes 6291456 | tf_op jit(solution)/shard_map/project/pallas_call | solution.py:388
  7.9 0.7 collective-permute-start
  8.6 0.1 broadcast_in_dim.28
  8.7 0.1 broadcast_in_dim.29
  8.7 0.1 broadcast_in_dim.30
  8.9 0.1 convert_element_type.25
  9.0 0.1 copy.55
  9.1 0.1 select_n.29
  9.2 0.7 copy.57.grid_ref
  10.0 1.5 copy.54
  11.6 0.8 concatenate.7.aux
  12.3 7.1 %project.2.po = bf16[8192,128]{1,0:T(8,128)(2,1)} custom-call(s32[1]{0:T(128)} %bitcast.half, bf16[16384,256]{1,0:T(8,128)(2,1)} %bitcast.18, bf16[256,128]{1,0:T(8,128)(2,1)} %proj.7), custom_call_target="tpu_custom_call" | custom-call | flops 536870912 | bytes 6291456 | tf_op jit(solution)/shard_map/project/pallas_call | solution.py:388
  19.5 0.6 maximum_convert_fusion.ln
  20.1 0.0 collective-permute-done.pr
  20.1 1.3 copy-done
  21.4 100.6 %stems_trunk.1 = (bf16[4096,128]{1,0:T(8,128)(2,1)}, bf16[8192,128]{1,0:T(8,128)(2,1)}, bf16[2048,32]{1,0:T(8,128)(2,1)}, f32[2560,128]{1,0:T(8,128)}) custom-call(s32[64,2,2]{2,1,0:T(2,128)} %copy.57.grid_ref, bf16[8192,128]{1,0:T(8,128)(2,1)} %project.2.po, bf16[8192,128]{1,0:T(8,128)(2,1)} %copy-done, bf16[2048,32]{1,0:T(8,128)(2,1)} %bitcast.22, ...), custom_call_target="tpu_custom_call" | custom-call | tf_op jit(solution)/shard_map/stems_trunk/pallas_call | solution.py:357
  122.1 0.1 collective-permute-start.1
  122.1 2.3 %copy.58 = bf16[64,2,16,32]{0,3,2,1:T(8,128)(2,1)} copy(bf16[64,2,16,32]{3,2,1,0:T(8,128)(2,1)} %bitcast.24) | data formatting | bytes 262144
  124.4 8.2 %features.2 = (bf16[16384,256]{1,0:T(8,128)(2,1)}, f32[128,256]{1,0:T(8,128)}) custom-call(s32[1]{0:T(128)} %bitcast.half, bf16[8192,128]{1,0:T(8,128)(2,1)} %get-tuple-element.54.dtok, bf16[16384,256]{1,0:T(8,128)(2,1)} %bitcast.19, bf16[256,128]{1,0:T(8,128)(2,1)} %proj.7), custom_call_target="tpu_custom_call" | custom-call | flops 1073741824 | bytes 10485760 | tf_op jit(solution)/shard_map/features/pallas_call | solution.py:440
  132.6 1.3 copy-done.1
  133.9 8.2 %features.3 = (bf16[16384,256]{1,0:T(8,128)(2,1)}, f32[128,256]{1,0:T(8,128)}) custom-call(s32[1]{0:T(128)} %bitcast.2.half, bf16[8192,128]{1,0:T(8,128)(2,1)} %copy-done.1, bf16[16384,256]{1,0:T(8,128)(2,1)} %bitcast.20, bf16[256,128]{1,0:T(8,128)(2,1)} %proj.7, bf16[16384,256]{1,0:T(8,128)(2,1)} %get-tuple-element.55.before, ...), custom_call_target="tpu_custom_call", output_to_operand_aliasing={{0}: (4, {})} | custom-call | flops 1073741824 | bytes 10485760 | tf_op jit(solution)/shard_map/features/pallas_call | solution.py:440
  142.1 31.1 %reduce.3 = (bf16[2560,128]{1,0:T(8,128)(2,1)}, bf16[128,256]{1,0:T(8,128)(2,1)}) custom-call(f32[2560,128]{1,0:T(8,128)} %get-tuple-element.59.acc, f32[128,256]{1,0:T(8,128)} %get-tuple-element.60.gfeat), custom_call_target="tpu_custom_call" | custom-call | tf_op jit(solution)/shard_map/reduce/pallas_call | solution.py:609
  173.3 2.5 %unpack.1 = (f32[256,128]{1,0:T(8,128)}, f32[16,128]{1,0:T(8,128)}, f32[128,128]{1,0:T(8,128)}, f32[128,256]{1,0:T(8,128)}, f32[128,128]{1,0:T(8,128)}, /*index=...) custom-call(bf16[2560,128]{1,0:T(8,128)(2,1)} %get-tuple-element.61., ...), custom_call_target="tpu_custom_call" | custom-call | tf_op jit(solution)/shard_map/unpack/pallas_call | solution.py:507
  175.7 1.3 slice_reduce_fusion
  (27 shorter events, 0.1 us)
Async XLA Ops:
  0.7 7.9 %copy-start.10 = (s32[64]{0:T(128)S(1)}, s32[64]{0:T(128)}, u32[]{:S(2)}) copy-start(s32[64]{0:T(128)} %param.31) | copy-start | bytes 772
  0.7 8.2 %copy-start.3 = (s32[64,64]{1,0:T(8,128)S(1)}, s32[64,64]{1,0:T(8,128)}, u32[]{:S(2)}) copy-start(s32[64,64]{1,0:T(8,128)} %param.30) | copy-start | bytes 49156
  0.7 8.3 %copy-start.4 = (s32[64,2,16]{0,2,1:T(8,128)S(1)}, s32[64,2,16]{0,2,1:T(8,128)}, u32[]{:S(2)}) copy-start(s32[64,2,16]{0,2,1:T(8,128)} %param.29) | copy-start | bytes 24580
  0.7 8.5 %copy-start.5 = (s32[64,2,2]{0,2,1:T(2,128)S(1)}, s32[64,2,2]{0,2,1:T(2,128)}, u32[]{:S(2)}) copy-start(s32[64,2,2]{0,2,1:T(2,128)} %param.27) | copy-start | bytes 3076
  0.7 9.3 %copy-start.2 = (bf16[64,2,16,32]{0,3,2,1:T(8,128)(2,1)S(1)}, bf16[64,2,16,32]{0,3,2,1:T(8,128)(2,1)}, u32[]{:S(2)}) copy-start(bf16[64,2,16,32]{0,3,2,1:T(8,128)(2,1)} %param.28) | copy-start | bytes 393220
  7.9 12.2 %collective-permute-start = (bf16[8192,128]{1,0:T(8,128)(2,1)}, bf16[8192,128]{1,0:T(8,128)(2,1)S(1)}, u32[]{:S(2)}, u32[]{:S(2)}) collective-permute-start(bf16[8192,128]{1,0:T(8,128)(2,1)} %project.3), channel_id=1, source_target_pairs={{0,1},{1,0},{2,3},{3,2},{4,5},{5,4},{6,7},{7,6},{8,9},{9,8},{10,11... | collective-permute-start | bytes 6291464 | tf_op jit(solution)/shard_map/ppermute | solution.py:644
  12.3 7.2 %copy-start.6 = (bf16[128]{0:T(256)(128)(2,1)S(1)}, bf16[128]{0:T(256)(128)(2,1)}, u32[]{:S(2)}) copy-start(bf16[128]{0:T(256)(128)(2,1)} %param.49) | copy-start | bytes 772
  12.3 7.2 %copy-start.7 = (bf16[128]{0:T(256)(128)(2,1)S(1)}, bf16[128]{0:T(256)(128)(2,1)}, u32[]{:S(2)}) copy-start(bf16[128]{0:T(256)(128)(2,1)} %param.48) | copy-start | bytes 772
  12.3 7.2 %copy-start.8 = (bf16[128]{0:T(256)(128)(2,1)S(1)}, bf16[128]{0:T(256)(128)(2,1)}, u32[]{:S(2)}) copy-start(bf16[128]{0:T(256)(128)(2,1)} %param.45) | copy-start | bytes 772
  12.3 7.2 %copy-start.9 = (bf16[128]{0:T(256)(128)(2,1)S(1)}, bf16[128]{0:T(256)(128)(2,1)}, u32[]{:S(2)}) copy-start(bf16[128]{0:T(256)(128)(2,1)} %param.44) | copy-start | bytes 772
  20.1 1.3 copy-start
  122.1 10.5 %collective-permute-start.1 = (bf16[8192,128]{1,0:T(8,128)(2,1)}, bf16[8192,128]{1,0:T(8,128)(2,1)S(1)}, u32[]{:S(2)}, u32[]{:S(2)}) collective-permute-start(bf16[8192,128]{1,0:T(8,128)(2,1)} %get-tuple-element.54.dtok), channel_id=1, source_target_pairs={{0,1},{1,0},{2,3},{3,2},{4,5},{5,4},{6,7},{7,6},{8,9},{9,8},{10,11... | collective-permute-start | bytes 6291464 | tf_op jit(solution)/shard_map/ppermute | solution.py:656
  132.6 1.3 copy-start.1

commit v3 on v2

--- a/solution.py
+++ b/solution.py
@@ -15,6 +15,7 @@
 BF = jnp.bfloat16
 F32 = jnp.float32
 VMEM_LIMIT = 60 * 2**20
+CHAINS = 4
 
 R_WIN, R_WOUT, R_Q, R_KV, R_AO = 0, 512, 1024, 1152, 1408
 R_SWO, R_VKV, R_PKV, R_W2, R_W1 = 1536, 1792, 2048, 2304, 2432
@@ -110,10 +111,10 @@
 
 
 def block_kernel(
-    grid_ref, po, pr, frames, aux, cot,
+    half, grid_ref, feats, pr, frames, aux, cot, proj,
     vis_query, vis_wq, vis_kv, vis_wo, prop_w1, prop_w2, prop_query, prop_wq, prop_kv, prop_wo,
     ln, qkv_w, attn_out, mlp_in, mlp_out,
-    out, dtok_ref, dframes, acc,
+    out, grad_feats, dtok_ref, dframes, acc, gsum,
     masks_ref, qv_ref, qp_ref, wqkv_t, ao_t, win_t, wout_t, stem_t, ln_ref,
     gv_ref, gp_ref, lnacc, stat,
 ):
@@ -136,6 +137,7 @@
         for j in range(4):
             ln_ref[j] = jnp.broadcast_to(ln[j : j + 1, :], (WIDTH, WIDTH)).T
         acc[...] = jnp.zeros_like(acc)
+        gsum[...] = jnp.zeros_like(gsum)
         gv_ref[...] = jnp.zeros_like(gv_ref)
         gp_ref[...] = jnp.zeros_like(gp_ref)
         lnacc[...] = jnp.zeros_like(lnacc)
@@ -150,158 +152,196 @@
     low_tall = cat([low_half] * 8, 0)
     high_tall = cat([high_half] * 8, 0)
 
-    tok = (po[...].astype(F32) + pr[...].astype(F32)).astype(BF)
-    vkv = nn(tok, vis_kv[...]).astype(BF)
-    vk, vv = vkv[:, :WIDTH], vkv[:, WIDTH:]
-    slot = lax.broadcasted_iota(jnp.int32, (64, WIDTH), 0)
-    slot_row, slot_col = slot >> 3, slot & 7
-    bias = []
-    for st in range(8):
-        s, t = step * 4 + st // 2, st % 2
-        keep = (slot_row < grid_ref[s, t, 0]) & (slot_col < grid_ref[s, t, 1])
-        bias.append(jnp.where(keep, 0.0, NEG))
-    vp = softmax_rows(nt(vk, qv).reshape(8, 64, WIDTH) + cat(bias, 0).reshape(8, 64, WIDTH))
-    vpb = vp.reshape(512, WIDTH).astype(BF)
-    vpt = vpb.T
-    zero64 = jnp.zeros((64, WIDTH), BF)
-    vmixed = []
-    for j in range(4):
-        pair = slice(128 * j, 128 * j + 128)
-        block = vv[pair]
-        spread = cat([cat([block[:64], zero64], 0), cat([zero64, block[64:]], 0)], 1)
-        both = head_select(nn(vpt[:, pair], spread)).astype(BF)
-        vmixed += [both[:, :WIDTH], both[:, WIDTH:]]
-
-    fr = frames[...]
-    pre = nn(fr, prop_w1[...])
-    gate = jax.nn.sigmoid(pre)
-    hidden = (pre * gate).astype(BF)
-    ptok = nn(hidden, prop_w2[...]).astype(BF)
-    pkv = nn(ptok, prop_kv[...]).astype(BF)
-    pk, pv = pkv[:, :WIDTH], pkv[:, WIDTH:]
-    pbias = jnp.broadcast_to(aux[0, 3:4, :WIDTH], (WIDTH, WIDTH)).T
-    pp = softmax_rows((nt(pk, qp) + pbias).reshape(8, 16, WIDTH))
-    ppb = pp.reshape(WIDTH, WIDTH).astype(BF)
-    ppt = ppb.T
-    zero16 = jnp.zeros((HEAD, WIDTH), BF)
-    spread = cat(
-        [cat([pv[16 * j : 16 * j + 16] if j == st else zero16 for j in range(8)], 0) for st in range(8)], 1
-    )
-    pm = head_select(nn(ppt, spread)).astype(BF)
-
-    rows = []
-    for st in range(8):
-        rows.append(cat([vmixed[st], zero16], 1))
-        rows.append(cat([zero16, pm[:, WIDTH * st : WIDTH * st + WIDTH]], 1))
-    mixed_ext = cat(rows, 0)
-    x = nt(stem_t[...], mixed_ext)
-    g1, b1, g2, b2 = [cat([ln_ref[j]] * 2, 1) for j in range(4)]
-    hat1, scale1 = norm_rows(x)
-    n1 = (hat1 * g1 + b1).astype(BF)
-    qkv = nn(wqkv_t[...], n1).astype(BF)
-    qt, kt, vt = qkv[:WIDTH] * jnp.asarray(0.25, BF), qkv[WIDTH : 2 * WIDTH], qkv[2 * WIDTH :]
-    kn, vn = kt.T, vt.T
-    weights, weights_b, query_bd, mixed_t = [], [], [], []
-    for p in range(2):
-        pair = slice(128 * p, 128 * p + 128)
-        column = jnp.broadcast_to(aux[0, 2:3, pair], (WIDTH, WIDTH)).T
-        tbias = jnp.where(first, column[:64], column[64:])
-        qbd = cat([qt[:, pair] * low_tall, qt[:, pair] * high_tall], 0)
-        keys = cat([kn[128 * p : 128 * p + 64], kn[128 * p + 64 : 128 * p + 128]], 1)
-        scores = nn(head_expand(keys, masks), qbd).reshape(8, 64, WIDTH) + tbias[None]
-        w = softmax_rows(scores)
-        wb = w.reshape(512, WIDTH).astype(BF)
-        weights.append(w)
-        weights_b.append(wb)
-        query_bd.append(qbd)
-        mixed_t.append(mix_keys(spread_keys(vt[:, pair], low_half, high_half), wb, first).astype(BF))
-    mixed = cat(mixed_t, 1)
-    branch = nn(ao_t[...], mixed)
-    middle = x + branch
-    hat2, scale2 = norm_rows(middle)
-    n2 = (hat2 * g2 + b2).astype(BF)
-    up = nn(win_t[...], n2)
-    square = up * up
-    c = math.sqrt(2.0 / math.pi)
-    h = 0.5 + 0.5 * jnp.tanh(up * (c + (c * 0.044715) * square))
-    act = up * h
-    slope = h + act * (1.0 - h) * (2 * c + (6 * c * 0.044715) * square)
-    act_b = act.astype(BF)
-    mlp = nn(wout_t[...], act_b)
-    final = middle + mlp
-    out[...] = final.astype(BF).T
-    valid, mix = aux[0, 0:1, :], aux[0, 1:2, :]
-    for j, value in enumerate((final, branch, mlp)):
-        stat[j : j + 1, :] += jnp.sum(value * value, axis=0, keepdims=True) * valid
-    stat[3:4, :] += valid
-
-    seed = cot[...].T.astype(F32) * mix
-    dmlp = seed.astype(BF)
-    acc[R_WOUT : R_WOUT + 512] += nt(act_b, dmlp)
-    dup = (nn(mlp_out[...], dmlp) * slope).astype(BF)
-    acc[R_WIN : R_WIN + 512] += nt(dup, n2)
-    dn2 = nn(mlp_in[...], dup)
-    fold = lambda v: v[:, :WIDTH] + v[:, WIDTH:]
-    lnacc[2] += fold(dn2 * hat2)
-    lnacc[3] += fold(dn2)
-    dmid = seed + norm_rows_grad(dn2 * g2, hat2, scale2)
-    dbranch = dmid.astype(BF)
-    acc[R_AO : R_AO + WIDTH] += nt(mixed, dbranch)
-    dmixed = nn(attn_out[...], dbranch).astype(BF)
-    dq, dkv = [], []
-    for p in range(2):
-        pair = slice(128 * p, 128 * p + 128)
-        dbd = cat([dmixed[:, pair] * low_tall, dmixed[:, pair] * high_tall], 0)
-        values = cat([vn[128 * p : 128 * p + 64], vn[128 * p + 64 : 128 * p + 128]], 1)
-        dw = nn(head_expand(values, masks), dbd).reshape(8, 64, WIDTH)
-        ds = softmax_grad(weights[p], dw).reshape(512, WIDTH).astype(BF)
-        dv = head_select(nt(weights_b[p], dbd)).astype(BF)
-        dk = head_select(nt(ds, query_bd[p])).astype(BF)
-        dq.append((mix_keys(spread_keys(kt[:, pair], low_half, high_half), ds, first) * 0.25).astype(BF))
-        dkv.append(cat([dk[:, :WIDTH], dv[:, :WIDTH]], 1))
-        dkv.append(cat([dk[:, WIDTH:], dv[:, WIDTH:]], 1))
-    dq, dkv = cat(dq, 1), cat(dkv, 0)
-    acc[R_Q : R_Q + WIDTH] += nt(n1, dq)
-    grad = nn(n1, dkv)
-    acc[R_KV : R_KV + WIDTH] += grad[:, :WIDTH]
-    acc[R_KV + WIDTH : R_KV + 2 * WIDTH] += grad[:, WIDTH:]
-    dn1 = nn(qkv_w[:, :WIDTH], dq) + nt(qkv_w[:, WIDTH:], dkv)
-    lnacc[0] += fold(dn1 * hat1)
-    lnacc[1] += fold(dn1)
-    dx = (dmid + norm_rows_grad(dn1 * g1, hat1, scale1)).astype(BF)
-
-    grad = nn(dx, mixed_ext)
-    acc[R_SWO : R_SWO + WIDTH] += grad[:, :WIDTH]
-    acc[R_SWO + WIDTH : R_SWO + 2 * WIDTH] += grad[:, WIDTH:]
-    dstem = nn(dx.T, stem_t[...]).astype(BF)
-    dw, dv, pdw, pdv = [], [], [], []
-    for st in range(8):
-        spread = head_expand(dstem[32 * st : 32 * st + 16, :WIDTH], masks)
-        dw.append(nt(vv[64 * st : 64 * st + 64], spread))
-        dv.append(nn(vpb[64 * st : 64 * st + 64], spread))
-        spread = head_expand(dstem[32 * st + 16 : 32 * st + 32, WIDTH:], masks)
-        pdw.append(nt(pv[16 * st : 16 * st + 16], spread))
-        pdv.append(nn(ppb[16 * st : 16 * st + 16], spread))
-    ds = softmax_grad(vp, cat(dw, 0).reshape(8, 64, WIDTH)).reshape(512, WIDTH).astype(BF)
-    dkv = cat([nn(ds, qv).astype(BF), cat(dv, 0).astype(BF)], 1)
-    dtok_ref[...] = nt(dkv, vis_kv[...]).astype(BF)
-    grad = nn(tok.T, dkv)
-    acc[R_VKV : R_VKV + WIDTH] += grad[:, :WIDTH]
-    acc[R_VKV + WIDTH : R_VKV + 2 * WIDTH] += grad[:, WIDTH:]
-    gv_ref[...] += nn(ds.T, vk)
-
-    ds = softmax_grad(pp, cat(pdw, 0).reshape(8, 16, WIDTH)).reshape(WIDTH, WIDTH).astype(BF)
-    dkv = cat([nn(ds, qp).astype(BF), cat(pdv, 0).astype(BF)], 1)
-    dptok = nt(dkv, prop_kv[...]).astype(BF)
-    grad = nn(ptok.T, dkv)
-    acc[R_PKV : R_PKV + WIDTH] += grad[:, :WIDTH]
-    acc[R_PKV + WIDTH : R_PKV + 2 * WIDTH] += grad[:, WIDTH:]
-    gp_ref[...] += nn(ds.T, pk)
-    acc[R_W2 : R_W2 + WIDTH] += nn(hidden.T, dptok)
-    dhidden = nt(dptok, prop_w2[...])
-    dpre = (dhidden * (gate * (1.0 + pre * (1.0 - gate)))).astype(BF)
-    acc[R_W1 : R_W1 + 32] += nn(fr.T, dpre)
-    dframes[...] = nt(dpre, prop_w1[...]).astype(BF)
+
+    def chain(g):
+        slots = slice(512 * g, 512 * g + 512)
+        kept = nn(feats[slots], proj[...]).astype(BF)
+        tok = (kept.astype(F32) + pr[slots].astype(F32)).astype(BF)
+        vkv = nn(tok, vis_kv[...]).astype(BF)
+        vk, vv = vkv[:, :WIDTH], vkv[:, WIDTH:]
+        slot = lax.broadcasted_iota(jnp.int32, (64, WIDTH), 0)
+        slot_row, slot_col = slot >> 3, slot & 7
+        bias = []
+        for st in range(8):
+            s, t = (step * CHAINS + g) * 4 + st // 2, st % 2
+            keep = (slot_row < grid_ref[2 * t, s]) & (slot_col < grid_ref[2 * t + 1, s])
+            bias.append(jnp.where(keep, 0.0, NEG))
+        yield
+        vp = softmax_rows(nt(vk, qv).reshape(8, 64, WIDTH) + cat(bias, 0).reshape(8, 64, WIDTH))
+        vpb = vp.reshape(512, WIDTH).astype(BF)
+        yield
+        vpt = vpb.T
+        zero64 = jnp.zeros((64, WIDTH), BF)
+        vmixed = []
+        for j in range(4):
+            pair = slice(128 * j, 128 * j + 128)
+            block = vv[pair]
+            spread = cat([cat([block[:64], zero64], 0), cat([zero64, block[64:]], 0)], 1)
+            both = head_select(nn(vpt[:, pair], spread)).astype(BF)
+            vmixed += [both[:, :WIDTH], both[:, WIDTH:]]
+
+        yield
+        fr = frames[128 * g : 128 * g + 128]
+        pre = nn(fr, prop_w1[...])
+        gate = jax.nn.sigmoid(pre)
+        hidden = (pre * gate).astype(BF)
+        ptok = nn(hidden, prop_w2[...]).astype(BF)
+        pkv = nn(ptok, prop_kv[...]).astype(BF)
+        pk, pv = pkv[:, :WIDTH], pkv[:, WIDTH:]
+        pbias = jnp.broadcast_to(aux[g, 3:4, :WIDTH], (WIDTH, WIDTH)).T
+        yield
+        pp = softmax_rows((nt(pk, qp) + pbias).reshape(8, 16, WIDTH))
+        ppb = pp.reshape(WIDTH, WIDTH).astype(BF)
+        ppt = ppb.T
+        zero16 = jnp.zeros((HEAD, WIDTH), BF)
+        spread = cat(
+            [cat([pv[16 * j : 16 * j + 16] if j == st else zero16 for j in range(8)], 0) for st in range(8)], 1
+        )
+        pm = head_select(nn(ppt, spread)).astype(BF)
+
+        yield
+        rows = []
+        for st in range(8):
+            rows.append(cat([vmixed[st], zero16], 1))
+            rows.append(cat([zero16, pm[:, WIDTH * st : WIDTH * st + WIDTH]], 1))
+        mixed_ext = cat(rows, 0)
+        x = nt(stem_t[...], mixed_ext)
+        g1, b1, g2, b2 = [cat([ln_ref[j]] * 2, 1) for j in range(4)]
+        hat1, scale1 = norm_rows(x)
+        n1 = (hat1 * g1 + b1).astype(BF)
+        yield
+        qkv = nn(wqkv_t[...], n1).astype(BF)
+        qt, kt, vt = qkv[:WIDTH] * jnp.asarray(0.25, BF), qkv[WIDTH : 2 * WIDTH], qkv[2 * WIDTH :]
+        kn, vn = kt.T, vt.T
+        yield
+        weights, weights_b, query_bd, mixed_t = [], [], [], []
+        for p in range(2):
+            pair = slice(128 * p, 128 * p + 128)
+            column = jnp.broadcast_to(aux[g, 2:3, pair], (WIDTH, WIDTH)).T
+            tbias = jnp.where(first, column[:64], column[64:])
+            qbd = cat([qt[:, pair] * low_tall, qt[:, pair] * high_tall], 0)
+            keys = cat([kn[128 * p : 128 * p + 64], kn[128 * p + 64 : 128 * p + 128]], 1)
+            scores = nn(head_expand(keys, masks), qbd).reshape(8, 64, WIDTH) + tbias[None]
+            yield
+            w = softmax_rows(scores)
+            yield
+            wb = w.reshape(512, WIDTH).astype(BF)
+            weights.append(w)
+            weights_b.append(wb)
+            query_bd.append(qbd)
+            mixed_t.append(mix_keys(spread_keys(vt[:, pair], low_half, high_half), wb, first).astype(BF))
+        mixed = cat(mixed_t, 1)
+        yield
+        branch = nn(ao_t[...], mixed)
+        middle = x + branch
+        hat2, scale2 = norm_rows(middle)
+        n2 = (hat2 * g2 + b2).astype(BF)
+        yield
+        up = nn(win_t[...], n2)
+        yield
+        square = up * up
+        c = math.sqrt(2.0 / math.pi)
+        h = 0.5 + 0.5 * jnp.tanh(up * (c + (c * 0.044715) * square))
+        act = up * h
+        slope = h + act * (1.0 - h) * (2 * c + (6 * c * 0.044715) * square)
+        act_b = act.astype(BF)
+        yield
+        mlp = nn(wout_t[...], act_b)
+        final = middle + mlp
+        out[256 * g : 256 * g + 256] = final.astype(BF).T
+        valid, mix = aux[g, 0:1, :], aux[g, 1:2, :]
+        for j, value in enumerate((final, branch, mlp)):
+            stat[j : j + 1, :] += jnp.sum(value * value, axis=0, keepdims=True) * valid
+        stat[3:4, :] += valid
+
+        yield
+        seed = cot[256 * g : 256 * g + 256].T.astype(F32) * mix
+        dmlp = seed.astype(BF)
+        acc[R_WOUT : R_WOUT + 512] += nt(act_b, dmlp)
+        dup = (nn(mlp_out[...], dmlp) * slope).astype(BF)
+        acc[R_WIN : R_WIN + 512] += nt(dup, n2)
+        yield
+        dn2 = nn(mlp_in[...], dup)
+        fold = lambda v: v[:, :WIDTH] + v[:, WIDTH:]
+        lnacc[2] += fold(dn2 * hat2)
+        lnacc[3] += fold(dn2)
+        dmid = seed + norm_rows_grad(dn2 * g2, hat2, scale2)
+        dbranch = dmid.astype(BF)
+        acc[R_AO : R_AO + WIDTH] += nt(mixed, dbranch)
+        yield
+        dmixed = nn(attn_out[...], dbranch).astype(BF)
+        yield
+        dq, dkv = [], []
+        for p in range(2):
+            pair = slice(128 * p, 128 * p + 128)
+            dbd = cat([dmixed[:, pair] * low_tall, dmixed[:, pair] * high_tall], 0)
+            values = cat([vn[128 * p : 128 * p + 64], vn[128 * p + 64 : 128 * p + 128]], 1)
+            dw = nn(head_expand(values, masks), dbd).reshape(8, 64, WIDTH)
+            yield
+            ds = softmax_grad(weights[p], dw).reshape(512, WIDTH).astype(BF)
+            dv = head_select(nt(weights_b[p], dbd)).astype(BF)
+            dk = head_select(nt(ds, query_bd[p])).astype(BF)
+            dq.append((mix_keys(spread_keys(kt[:, pair], low_half, high_half), ds, first) * 0.25).astype(BF))
+            dkv.append(cat([dk[:, :WIDTH], dv[:, :WIDTH]], 1))
+            dkv.append(cat([dk[:, WIDTH:], dv[:, WIDTH:]], 1))
+        dq, dkv = cat(dq, 1), cat(dkv, 0)
+        yield
+        acc[R_Q : R_Q + WIDTH] += nt(n1, dq)
+        grad = nn(n1, dkv)
+        acc[R_KV : R_KV + WIDTH] += grad[:, :WIDTH]
+        acc[R_KV + WIDTH : R_KV + 2 * WIDTH] += grad[:, WIDTH:]
+        dn1 = nn(qkv_w[:, :WIDTH], dq) + nt(qkv_w[:, WIDTH:], dkv)
+        lnacc[0] += fold(dn1 * hat1)
+        lnacc[1] += fold(dn1)
+        dx = (dmid + norm_rows_grad(dn1 * g1, hat1, scale1)).astype(BF)
+
+        yield
+        grad = nn(dx, mixed_ext)
+        acc[R_SWO : R_SWO + WIDTH] += grad[:, :WIDTH]
+        acc[R_SWO + WIDTH : R_SWO + 2 * WIDTH] += grad[:, WIDTH:]
+        dstem = nn(dx.T, stem_t[...]).astype(BF)
+        dw, dv, pdw, pdv = [], [], [], []
+        for st in range(8):
+            spread = head_expand(dstem[32 * st : 32 * st + 16, :WIDTH], masks)
+            dw.append(nt(vv[64 * st : 64 * st + 64], spread))
+            dv.append(nn(vpb[64 * st : 64 * st + 64], spread))
+            spread = head_expand(dstem[32 * st + 16 : 32 * st + 32, WIDTH:], masks)
+            pdw.append(nt(pv[16 * st : 16 * st + 16], spread))
+            pdv.append(nn(ppb[16 * st : 16 * st + 16], spread))
+        yield
+        ds = softmax_grad(vp, cat(dw, 0).reshape(8, 64, WIDTH)).reshape(512, WIDTH).astype(BF)
+        dkv = cat([nn(ds, qv).astype(BF), cat(dv, 0).astype(BF)], 1)
+        dtok = nt(dkv, vis_kv[...]).astype(BF)
+        dtok_ref[slots] = dtok
+        grad_feats[slots] = nt(dtok, proj[...]).astype(BF)
+        gsum[...] += nn(dtok.T, feats[slots])
+        grad = nn(tok.T, dkv)
+        acc[R_VKV : R_VKV + WIDTH] += grad[:, :WIDTH]
+        acc[R_VKV + WIDTH : R_VKV + 2 * WIDTH] += grad[:, WIDTH:]
+        gv_ref[...] += nn(ds.T, vk)
+
+        yield
+        ds = softmax_grad(pp, cat(pdw, 0).reshape(8, 16, WIDTH)).reshape(WIDTH, WIDTH).astype(BF)
+        dkv = cat([nn(ds, qp).astype(BF), cat(pdv, 0).astype(BF)], 1)
+        dptok = nt(dkv, prop_kv[...]).astype(BF)
+        grad = nn(ptok.T, dkv)
+        acc[R_PKV : R_PKV + WIDTH] += grad[:, :WIDTH]
+        acc[R_PKV + WIDTH : R_PKV + 2 * WIDTH] += grad[:, WIDTH:]
+        gp_ref[...] += nn(ds.T, pk)
+        yield
+        acc[R_W2 : R_W2 + WIDTH] += nn(hidden.T, dptok)
+        dhidden = nt(dptok, prop_w2[...])
+        dpre = (dhidden * (gate * (1.0 + pre * (1.0 - gate)))).astype(BF)
+        acc[R_W1 : R_W1 + 32] += nn(fr.T, dpre)
+        dframes[128 * g : 128 * g + 128] = nt(dpre, prop_w1[...]).astype(BF)
+
+        yield
+
+    live = [chain(g) for g in range(CHAINS)]
+    while live:
+        for one in list(live):
+            if next(one, live) is live:
+                live.remove(one)
 
     @pl.when(step == pl.num_programs(0) - 1)
     def _():
@@ -316,28 +356,34 @@
     return pl.BlockSpec(shape, lambda i, *_: (0,) * len(shape))
 
 
-def block_call(grid_sizes, po, pr, frames, aux, cot, weights):
-    steps = aux.shape[0]
+def block_call(half, grid_sizes, feats, received, frames, aux, cot, proj, weights):
+    steps = aux.shape[0] // CHAINS
+    channels = feats.shape[1]
     row = lambda i, *_: (i, 0)
+    own = lambda i, half, _: (half[0] * steps + i, 0)
     in_specs = [
-        pl.BlockSpec(memory_space=pltpu.SMEM),
-        pl.BlockSpec((512, WIDTH), row),
-        pl.BlockSpec((512, WIDTH), row),
-        pl.BlockSpec((128, frames.shape[1]), row),
-        pl.BlockSpec((1, 8, 256), lambda i: (i, 0, 0)),
-        pl.BlockSpec((256, WIDTH), row),
+        pl.BlockSpec((512 * CHAINS, channels), own),
+        pl.BlockSpec((512 * CHAINS, WIDTH), row),
+        pl.BlockSpec((128 * CHAINS, frames.shape[1]), row),
+        pl.BlockSpec((CHAINS, 8, 256), lambda i, *_: (i, 0, 0)),
+        pl.BlockSpec((256 * CHAINS, WIDTH), row),
+        whole(proj.shape),
     ] + [whole(w.shape) for w in weights]
     out_shape = (
-        jax.ShapeDtypeStruct((256 * steps, WIDTH), BF),
-        jax.ShapeDtypeStruct((512 * steps, WIDTH), BF),
-        jax.ShapeDtypeStruct((128 * steps, frames.shape[1]), BF),
+        jax.ShapeDtypeStruct((256 * CHAINS * steps, WIDTH), BF),
+        jax.ShapeDtypeStruct(feats.shape, BF),
+        jax.ShapeDtypeStruct((512 * CHAINS * steps, WIDTH), BF),
+        jax.ShapeDtypeStruct((128 * CHAINS * steps, frames.shape[1]), BF),
         jax.ShapeDtypeStruct((R_END, WIDTH), F32),
+        jax.ShapeDtypeStruct((WIDTH, channels), F32),
     )
     out_specs = (
-        pl.BlockSpec((256, WIDTH), row),
-        pl.BlockSpec((512, WIDTH), row),
-        pl.BlockSpec((128, frames.shape[1]), row),
+        pl.BlockSpec((256 * CHAINS, WIDTH), row),
+        pl.BlockSpec((512 * CHAINS, channels), own),
+        pl.BlockSpec((512 * CHAINS, WIDTH), row),
+        pl.BlockSpec((128 * CHAINS, frames.shape[1]), row),
         whole((R_END, WIDTH)),
+        whole((WIDTH, channels)),
     )
     scratch = [
         pltpu.VMEM((8, 16, WIDTH), BF),
@@ -356,14 +402,17 @@
     ]
     return pl.pallas_call(
         block_kernel,
-        grid=(steps,),
-        in_specs=in_specs,
-        out_specs=out_specs,
+        grid_spec=pltpu.PrefetchScalarGridSpec(
+            num_scalar_prefetch=2,
+            grid=(steps,),
+            in_specs=in_specs,
+            out_specs=out_specs,
+            scratch_shapes=scratch,
+        ),
         out_shape=out_shape,
-        scratch_shapes=scratch,
         compiler_params=pltpu.CompilerParams(vmem_limit_bytes=VMEM_LIMIT),
         name="stems_trunk",
-    )(grid_sizes, po, pr, frames, aux, cot, *weights)
+    )(half, grid_sizes, feats, received, frames, aux, cot, proj, *weights)
 
 
 def make_aux(proprio_mask, token_valid, mix_weight):
@@ -377,6 +426,9 @@
     rest = jnp.zeros((steps, 4, 4 * seq), F32)
     return jnp.concatenate([valid, mix, vbias, pbias, rest], axis=1)
 
+PROJECT_STEPS = 4
+FEATURE_STEPS = 4
+
 
 def project_kernel(half, feats, proj, out):
     out[...] = nn(feats[...], proj[...]).astype(BF)
@@ -384,7 +436,7 @@
 
 def project_call(half, feats, proj):
     rows, channels = feats.shape[0] // 2, feats.shape[1]
-    steps = 8
+    steps = PROJECT_STEPS
     return pl.pallas_call(
         project_kernel,
         grid_spec=pltpu.PrefetchScalarGridSpec(
@@ -415,34 +467,21 @@
     gsum[...] += nn(d.T, feats[...])
 
 
-def feature_kernel_first(half, dtok, feats, proj, grad, gsum):
-    @pl.when(pl.program_id(0) == 0)
-    def _():
-        gsum[...] = jnp.zeros_like(gsum)
-
-    d = dtok[...]
-    grad[...] = nt(d, proj[...]).astype(BF)
-    gsum[...] += nn(d.T, feats[...])
-
-
-def feature_call(half, dtok, feats, proj, before=None):
+def feature_call(half, dtok, feats, proj, grad, gsum):
     rows, channels = feats.shape[0] // 2, feats.shape[1]
-    steps = 8
-    in_specs = [
-        pl.BlockSpec((rows // steps, WIDTH), lambda i, half: (i, 0)),
-        pl.BlockSpec((rows // steps, channels), lambda i, half: (half[0] * steps + i, 0)),
-        whole(proj.shape),
-    ]
-    args = (half, dtok, feats, proj)
-    if before is not None:
-        in_specs += [pl.BlockSpec(memory_space=pl.ANY), whole((WIDTH, channels))]
-        args += tuple(before)
+    steps = FEATURE_STEPS
     return pl.pallas_call(
-        feature_kernel_first if before is None else feature_kernel,
+        feature_kernel,
         grid_spec=pltpu.PrefetchScalarGridSpec(
             num_scalar_prefetch=1,
             grid=(steps,),
-            in_specs=in_specs,
+            in_specs=[
+                pl.BlockSpec((rows // steps, WIDTH), lambda i, half: (i, 0)),
+                pl.BlockSpec((rows // steps, channels), lambda i, half: (half[0] * steps + i, 0)),
+                whole(proj.shape),
+                pl.BlockSpec(memory_space=pl.ANY),
+                whole((WIDTH, channels)),
+            ],
             out_specs=(
                 pl.BlockSpec((rows // steps, channels), lambda i, half: (half[0] * steps + i, 0)),
                 whole((WIDTH, channels)),
@@ -452,13 +491,10 @@
             jax.ShapeDtypeStruct((2 * rows, channels), BF),
             jax.ShapeDtypeStruct((WIDTH, channels), F32),
         ),
-        input_output_aliases={} if before is None else {4: 0},
+        input_output_aliases={4: 0},
         compiler_params=pltpu.CompilerParams(vmem_limit_bytes=VMEM_LIMIT),
-        cost_estimate=pl.CostEstimate(
-            flops=4 * rows * channels * WIDTH, bytes_accessed=2 * rows * (2 * channels + WIDTH), transcendentals=0
-        ),
         name="features",
-    )(*args)
+    )(half, dtok, feats, proj, grad, gsum)
 
 
 def unpack_kernel(
@@ -642,7 +678,6 @@
     feats = vision_feats.reshape(-1, vision_feats.shape[3])
     sent = project_call(other, feats, feat_proj)
     received = lax.ppermute(sent, "mod", swap)
-    kept = project_call(own, feats, feat_proj)
     aux = make_aux(proprio_mask, token_valid, mix_weight)
     ln = jnp.stack([ln1_gain, ln1_bias, ln2_gain, ln2_bias]).astype(F32)
     weights = (
@@ -650,12 +685,12 @@
         ln, qkv_weight, attn_out, mlp_in, mlp_out,
     )
     frames = proprio.reshape(-1, proprio.shape[3])
-    output, dtok, dframes, acc = block_call(
-        vision_grid, kept, received, frames, aux, out_cot.reshape(-1, WIDTH), weights
+    grid_sizes = jnp.transpose(vision_grid, (1, 2, 0)).reshape(4, -1)
+    output, grad_vision, dtok, dframes, acc, gfeat = block_call(
+        own, grid_sizes, feats, received, frames, aux, out_cot.reshape(-1, WIDTH), feat_proj, weights
     )
     dtok_other = lax.ppermute(dtok, "mod", swap)
-    part = feature_call(own, dtok, feats, feat_proj)
-    grad_vision, gfeat = feature_call(other, dtok_other, feats, feat_proj, part)
+    grad_vision, gfeat = feature_call(other, dtok_other, feats, feat_proj, grad_vision, gfeat)
     total, gfeat = reduce_call(acc, gfeat, lax.axis_size("dp"))
     outs = unpack_call(total, gfeat, vis_query, vis_wq, prop_query, prop_wq)
     vectors = {11, 12, 15, 16}

time: 178 us -> 126 us (0.71)
  Pallas kernels: 165 us -> 111 us
  waiting for transfers between devices: 0.01 us -> 2.13 us
    pallas_call x3 -> x2, Pallas kernels: 117 us -> 72.9 us  [the longest x1 66.6 us: block_call(): pl.pallas_call(block_kernel, grid_spec=pltpu.PrefetchScalarGridSpec(num_s...]
    pallas_call x2 -> x1, Pallas kernels: 14.3 us -> 5.09 us  [project_call(): pl.pallas_call(project_kernel, grid_spec=pltpu.PrefetchScalarGridSpec(num...]
    unnamed x25 -> x22, local copies, waits for them, and re-layouts: 7.24 us -> 6.47 us
  transfers between devices with their start and end apart: 2 -> 2, of which waited for: 0 -> 2; matrix products, arithmetic and copies ran while one was open for 4% -> 5% of each run, Pallas kernels for 9% -> 0%
where the time goes in v3:
time: 126 us; the launch traced here: 125 us
  Pallas kernels  111 us (88%)
  local copies, waits for them, and re-layouts  9.13 us (7%)
  waiting for transfers between devices  2.13 us (2%)
    pallas_call x1, Pallas kernels, block_call(): pl.pallas_call(block_kernel, grid_spec=pltpu.PrefetchScalarGridSpec(num_s...  66.6 us
    pallas_call x1, Pallas kernels, reduce_call(): pl.pallas_call(functools.partial(reduce_kernel, n, chunk), out_shape=(jax...  31 us
    unnamed x22, local copies, waits for them, and re-layouts  6.47 us
    pallas_call x1, Pallas kernels, feature_call(): pl.pallas_call(feature_kernel, grid_spec=pltpu.PrefetchScalarGridSpec(num...  6.34 us
    pallas_call x1, Pallas kernels, project_call(): pl.pallas_call(project_kernel, grid_spec=pltpu.PrefetchScalarGridSpec(num...  5.09 us
  transfers between devices with their start and end apart: 2, of which 2 were waited for; matrix products, arithmetic and copies ran while one was open for 5% of the time, Pallas kernels for 0%

profile of v3, /device:TPU:25, one launch (start us, length us, event | category | flops | bytes accessed | tf_op | source)
XLA Modules:
  0.0 125.3 jit_solution(248109135654477324)
XLA Ops:
  0.7 5.1 %project.1 = bf16[8192,128]{1,0:T(8,128)(2,1)} custom-call(s32[1]{0:T(128)} %bitcast.4.half, bf16[16384,256]{1,0:T(8,128)(2,1)} %bitcast.20, bf16[256,128]{1,0:T(8,128)(2,1)} %proj.5), custom_call_target="tpu_custom_call" | custom-call | flops 536870912 | bytes 6291456 | tf_op jit(solution)/shard_map/project/pallas_call | solution.py:440
  5.8 0.7 collective-permute-start
  6.5 0.1 broadcast_in_dim.28
  6.6 0.1 broadcast_in_dim.29
  6.7 0.1 broadcast_in_dim.30
  6.8 0.0 copy-done.3
  6.8 0.1 convert_element_type.25
  6.9 0.1 copy.54
  7.0 0.1 select_n.29
  7.2 1.5 %copy.53 = bf16[64,2,16,32]{3,2,1,0:T(8,128)(2,1)} copy(bf16[64,2,16,32]{0,3,2,1:T(8,128)(2,1)S(1)} %copy-done.2) | data formatting | bytes 262144 | tf_op args[2]
  8.7 0.8 concatenate.7.aux
  9.5 0.0 copy-done.7
  9.5 0.6 maximum_convert_fusion.ln
  10.1 0.4 collective-permute-done.pr
  10.5 1.3 %copy-done = bf16[8192,128]{1,0:T(8,128)(2,1)} copy-done((bf16[8192,128]{1,0:T(8,128)(2,1)}, bf16[8192,128]{1,0:T(8,128)(2,1)S(1)}, u32[]{:S(2)}) %copy-start) | copy-done | bytes 2097176
  11.8 66.6 %stems_trunk.1 = (bf16[4096,128]{1,0:T(8,128)(2,1)}, bf16[16384,256]{1,0:T(8,128)(2,1)}, bf16[8192,128]{1,0:T(8,128)(2,1)}, bf16[2048,32]{1,0:T(8,128)(2,1)}, f32[2560,128]{1,0:T(8,128)}, /*index=5*/f32[128,256]{1,0:T(8,128)}) custom-call(s32[1]{0:T(128)} %bitcast.half, s32[4,64]{1,0:T(4,128)} %bitcast.28, bf16[16384,256]{1,0:T(8,128)(2,1)} %bitcast.21, ...), custom_call_target="tpu_custom_call" | custom-call | tf_op jit(solution)/shard_map/stems_trunk/pallas_call | solution.py:403
  78.4 0.4 collective-permute-start.1
  78.8 2.3 %copy.56 = bf16[64,2,16,32]{0,3,2,1:T(8,128)(2,1)} copy(bf16[64,2,16,32]{3,2,1,0:T(8,128)(2,1)} %bitcast.26) | data formatting | bytes 262144
  81.1 1.7 %collective-permute-done.1.dtok = bf16[8192,128]{1,0:T(8,128)(2,1)S(1)} collective-permute-done((bf16[8192,128]{1,0:T(8,128)(2,1)}, bf16[8192,128]{1,0:T(8,128)(2,1)S(1)}, u32[]{:S(2)}, u32[]{:S(2)}) %collective-permute-start.1) | collective-permute-done | bytes 2097184 | tf_op jit(solution)/shard_map/ppermute | solution.py:692
  82.8 1.3 %copy-done.1 = bf16[8192,128]{1,0:T(8,128)(2,1)} copy-done((bf16[8192,128]{1,0:T(8,128)(2,1)}, bf16[8192,128]{1,0:T(8,128)(2,1)S(1)}, u32[]{:S(2)}) %copy-start.1) | copy-done | bytes 2097176
  84.2 6.3 %features.1 = (bf16[16384,256]{1,0:T(8,128)(2,1)}, f32[128,256]{1,0:T(8,128)}) custom-call(s32[1]{0:T(128)} %bitcast.4.half, bf16[8192,128]{1,0:T(8,128)(2,1)} %copy-done.1, bf16[16384,256]{1,0:T(8,128)(2,1)} %bitcast.22, bf16[256,128]{1,0:T(8,128)(2,1)} %proj.5, bf16[16384,256]{1,0:T(8,128)(2,1)} %get-tuple-element.55.before, ...), custom_call_target="tpu_custom_call", output_to_operand_aliasing={{0}: (4, {})} | custom-call | tf_op jit(solution)/shard_map/features/pallas_call | solution.py:473
  90.5 31.0 %reduce.3 = (bf16[2560,128]{1,0:T(8,128)(2,1)}, bf16[128,256]{1,0:T(8,128)(2,1)}) custom-call(f32[2560,128]{1,0:T(8,128)} %get-tuple-element.59.acc, f32[128,256]{1,0:T(8,128)} %get-tuple-element.60.gfeat), custom_call_target="tpu_custom_call" | custom-call | tf_op jit(solution)/shard_map/reduce/pallas_call | solution.py:645
  121.6 2.5 %unpack.1 = (f32[256,128]{1,0:T(8,128)}, f32[16,128]{1,0:T(8,128)}, f32[128,128]{1,0:T(8,128)}, f32[128,256]{1,0:T(8,128)}, f32[128,128]{1,0:T(8,128)}, /*index=...) custom-call(bf16[2560,128]{1,0:T(8,128)(2,1)} %get-tuple-element.61., ...), custom_call_target="tpu_custom_call" | custom-call | tf_op jit(solution)/shard_map/unpack/pallas_call | solution.py:543
  124.0 1.3 %slice_reduce_fusion = f32[3]{0:T(128)} fusion(f32[4,128]{1,0:T(4,128)} %get-tuple-element.82), kind=kLoop, calls=%fused_computation.2 | loop fusion | bytes 24 | tf_op jit(solution)/shard_map/slice | solution.py:703
  (22 shorter events, 0.1 us)
Async XLA Ops:
  0.7 5.8 %copy-start.9 = (s32[64]{0:T(128)S(1)}, s32[64]{0:T(128)}, u32[]{:S(2)}) copy-start(s32[64]{0:T(128)} %param.31) | copy-start | bytes 772
  0.7 6.1 %copy-start.3 = (s32[64,64]{1,0:T(8,128)S(1)}, s32[64,64]{1,0:T(8,128)}, u32[]{:S(2)}) copy-start(s32[64,64]{1,0:T(8,128)} %param.30) | copy-start | bytes 49156
  0.7 6.2 %copy-start.4 = (s32[64,2,16]{0,2,1:T(8,128)S(1)}, s32[64,2,16]{0,2,1:T(8,128)}, u32[]{:S(2)}) copy-start(s32[64,2,16]{0,2,1:T(8,128)} %param.29) | copy-start | bytes 24580
  0.7 6.5 %copy-start.2 = (bf16[64,2,16,32]{0,3,2,1:T(8,128)(2,1)S(1)}, bf16[64,2,16,32]{0,3,2,1:T(8,128)(2,1)}, u32[]{:S(2)}) copy-start(bf16[64,2,16,32]{0,3,2,1:T(8,128)(2,1)} %param.28) | copy-start | bytes 393220
  0.7 8.8 %copy-start.5 = (bf16[128]{0:T(256)(128)(2,1)S(1)}, bf16[128]{0:T(256)(128)(2,1)}, u32[]{:S(2)}) copy-start(bf16[128]{0:T(256)(128)(2,1)} %param.49) | copy-start | bytes 772
  0.7 8.8 %copy-start.6 = (bf16[128]{0:T(256)(128)(2,1)S(1)}, bf16[128]{0:T(256)(128)(2,1)}, u32[]{:S(2)}) copy-start(bf16[128]{0:T(256)(128)(2,1)} %param.48) | copy-start | bytes 772
  0.7 8.8 %copy-start.7 = (bf16[128]{0:T(256)(128)(2,1)S(1)}, bf16[128]{0:T(256)(128)(2,1)}, u32[]{:S(2)}) copy-start(bf16[128]{0:T(256)(128)(2,1)} %param.45) | copy-start | bytes 772
  0.7 8.8 %copy-start.8 = (bf16[128]{0:T(256)(128)(2,1)S(1)}, bf16[128]{0:T(256)(128)(2,1)}, u32[]{:S(2)}) copy-start(bf16[128]{0:T(256)(128)(2,1)} %param.44) | copy-start | bytes 772
  5.8 4.7 %collective-permute-start = (bf16[8192,128]{1,0:T(8,128)(2,1)}, bf16[8192,128]{1,0:T(8,128)(2,1)S(1)}, u32[]{:S(2)}, u32[]{:S(2)}) collective-permute-start(bf16[8192,128]{1,0:T(8,128)(2,1)} %project.1), channel_id=1, source_target_pairs={{0,1},{1,0},{2,3},{3,2},{4,5},{5,4},{6,7},{7,6},{8,9},{9,8},{10,11... | collective-permute-start | bytes 6291464 | tf_op jit(solution)/shard_map/ppermute | solution.py:680
  10.5 1.3 %copy-start = (bf16[8192,128]{1,0:T(8,128)(2,1)}, bf16[8192,128]{1,0:T(8,128)(2,1)S(1)}, u32[]{:S(2)}) copy-start(bf16[8192,128]{1,0:T(8,128)(2,1)S(1)} %collective-permute-done.pr) | copy-start | bytes 6291460
  78.4 4.4 %collective-permute-start.1 = (bf16[8192,128]{1,0:T(8,128)(2,1)}, bf16[8192,128]{1,0:T(8,128)(2,1)S(1)}, u32[]{:S(2)}, u32[]{:S(2)}) collective-permute-start(bf16[8192,128]{1,0:T(8,128)(2,1)} %get-tuple-element.54), channel_id=1, source_target_pairs={{0,1},{1,0},{2,3},{3,2},{4,5},{5,4},{6,7},{7,6},{8,9},{9,8},{10,11... | collective-permute-start | bytes 6291464 | tf_op jit(solution)/shard_map/ppermute | solution.py:692
  82.8 1.3 %copy-start.1 = (bf16[8192,128]{1,0:T(8,128)(2,1)}, bf16[8192,128]{1,0:T(8,128)(2,1)S(1)}, u32[]{:S(2)}) copy-start(bf16[8192,128]{1,0:T(8,128)(2,1)S(1)} %collective-permute-done.1.dtok) | copy-start | bytes 6291460

commit v4 on v3

v4 whole, which is shorter than its diff:
```python
import functools
import math

import jax
import jax.numpy as jnp
from jax import lax
from jax.experimental import pallas as pl
from jax.experimental.pallas import tpu as pltpu
from jax.sharding import PartitionSpec as P

HEADS = 8
HEAD = 16
WIDTH = 128
NEG = -1e30
BF = jnp.bfloat16
F32 = jnp.float32
VMEM_LIMIT = 60 * 2**20
CHAINS = 4

R_WIN, R_WOUT, R_Q, R_KV, R_AO = 0, 512, 1024, 1152, 1408
R_SWO, R_VKV, R_PKV, R_W2, R_W1 = 1536, 1792, 2048, 2304, 2432
R_QV, R_QP, R_LN, R_STAT, R_END = 2464, 2480, 2496, 2500, 2560


def nn(a, b):
    return lax.dot_general(a, b, (((1,), (0,)), ((), ())), preferred_element_type=F32)


def nt(a, b):
    return lax.dot_general(a, b, (((1,), (1,)), ((), ())), preferred_element_type=F32)


def cat(items, axis):
    return jnp.concatenate(items, axis=axis)


def lane_iota(rows, lanes):
    return lax.broadcasted_iota(jnp.int32, (rows, lanes), 1)


def tile_to(mask, rows, lanes):
    return cat([cat([mask] * (rows // mask.shape[0]), 0)] * (lanes // mask.shape[1]), 1)


def head_expand(value, masks):
    return cat([value * tile_to(mask, *value.shape) for mask in masks], 0)


def head_select(full, heads, period):
    rows, lanes = full.shape[0] // heads, full.shape[1]
    head = (lane_iota(rows, lanes) & (period - 1)) >> 4
    out = full[:rows]
    for h in range(1, heads):
        out = jnp.where(head == h, full[h * rows : (h + 1) * rows], out)
    return out


def turn(value):
    out = []
    for j in range(0, value.shape[1], WIDTH):
        out += [value[:, j + 64 : j + 128], value[:, j : j + 64]]
    return cat(out, 1)


def diagonal(blocks):
    out = []
    for j, block in enumerate(blocks):
        row = [block if k == j else jnp.zeros((block.shape[0], other.shape[1]), BF) for k, other in enumerate(blocks)]
        out.append(cat(row, 1))
    return cat(out, 0)


def pair_up(parts):
    return cat([cat(parts[j : j + 2], 1) for j in range(0, 8, 2)], 0)


def unpair(value, rows):
    out = []
    for j in range(4):
        part = value[rows * j : rows * j + rows]
        out += [part[:, :WIDTH], part[:, WIDTH:]]
    return cat(out, 0)


def softmax_rows(scores):
    peak = jnp.max(scores, axis=1, keepdims=True)
    weights = jnp.exp(scores - peak)
    return weights * (1.0 / jnp.sum(weights, axis=1, keepdims=True))


def softmax_grad(weights, grad):
    return weights * (grad - jnp.sum(weights * grad, axis=1, keepdims=True))


def mean_rows(value):
    return jnp.sum(value, axis=0, keepdims=True) * (1.0 / value.shape[0])


def norm_rows(value):
    centered = value - mean_rows(value)
    scale = lax.rsqrt(mean_rows(centered * centered) + 1e-05)
    return centered * scale, scale


def norm_rows_grad(grad, hat, scale):
    return scale * (grad - mean_rows(grad) - hat * mean_rows(grad * hat))


def split_samples(value, low_half, high_half):
    out = []
    for s in range(4):
        half = tile_to(high_half if s % 2 else low_half, 64, WIDTH)
        block = value[:, WIDTH * (s // 2) : WIDTH * (s // 2) + WIDTH] * half
        zero = jnp.zeros((64, WIDTH), BF)
        out.append(cat([block, zero] if s < 2 else [zero, block], 1))
    return cat(out, 0)


def gather_heads(value, turned, group, low_half, high_half):
    low_tall, high_tall = tile_to(low_half, 64, WIDTH), tile_to(high_half, 64, WIDTH)
    out = []
    for s in (0, 2):
        even, odd = slice(64 * s, 64 * s + 64), slice(64 * s + 64, 64 * s + 128)
        left, right = (value[even], turned[odd]) if group == 0 else (turned[even], value[odd])
        out.append(left * low_tall + right * high_tall)
    return cat(out, 1)


def scatter_heads(parts, low_half, high_half):
    low_tall, high_tall = tile_to(low_half, 64, WIDTH), tile_to(high_half, 64, WIDTH)
    turned = [turn(part) for part in parts]
    out = []
    for s in range(4):
        lanes = slice(WIDTH * (s // 2), WIDTH * (s // 2) + WIDTH)
        left = (turned if s % 2 else parts)[0][:, lanes]
        right = (parts if s % 2 else turned)[1][:, lanes]
        out.append(left * low_tall + right * high_tall)
    return cat(out, 0)


def spread_keys(value, turned, group, low_half, high_half):
    zero = jnp.zeros((HEAD, WIDTH), BF)
    rows = []
    for s in range(4):
        lanes = slice(WIDTH * (s // 2), WIDTH * (s // 2) + WIDTH)
        for local in range(4):
            h = group * 4 + local
            source = value if s % 2 == local % 2 else turned
            block = source[h * HEAD : (h + 1) * HEAD, lanes] * (high_half if local % 2 else low_half)
            rows.append(cat([block, zero] if local < 2 else [zero, block], 1))
    return cat(rows, 0)


def mix_keys(value, weights, low_half, high_half, first):
    turned = turn(value)
    out = []
    for group in range(2):
        full = nn(spread_keys(value, turned, group, low_half, high_half), weights[group])
        left = jnp.where(first, full[:64, :WIDTH], full[64:128, :WIDTH])
        right = jnp.where(first, full[128:192, WIDTH:], full[192:, WIDTH:])
        out.append(cat([left, right], 1))
    return cat(out, 0)


def stem_queries(query, w_query, masks):
    value = nn(query, w_query).astype(BF)
    return head_expand(value * jnp.asarray(0.25, BF), masks)


def block_kernel(
    half, grid_ref, feats, pr, frames, aux, cot, proj,
    vis_query, vis_wq, vis_kv, vis_wo, prop_w1, prop_w2, prop_query, prop_wq, prop_kv, prop_wo,
    ln, qkv_w, attn_out, mlp_in, mlp_out,
    out, grad_feats, dtok_ref, dframes, acc, gsum,
    masks_ref, qv_ref, qp_ref, wqkv_t, ao_t, win_t, wout_t, stem_t, ln_ref,
    gv_ref, gp_ref, lnacc, stat,
):
    step = pl.program_id(0)

    @pl.when(step == 0)
    def _():
        lane = lane_iota(16, WIDTH) >> 4
        for h in range(HEADS):
            masks_ref[h] = jnp.where(lane == h, 1.0, 0.0).astype(BF)
        for h in range(4):
            masks_ref[HEADS + h] = jnp.where((lane & 3) == h, 1.0, 0.0).astype(BF)
        masks = [masks_ref[h] for h in range(HEADS)]
        qv_ref[...] = diagonal([stem_queries(vis_query[...], vis_wq[...], masks)] * 2)
        qp_ref[...] = diagonal([stem_queries(prop_query[...], prop_wq[...], masks)] * 2)
        wqkv_t[...] = qkv_w[...].T
        ao_t[...] = attn_out[...].T
        win_t[...] = mlp_in[...].T
        wout_t[...] = mlp_out[...].T
        stem_t[:, :WIDTH] = vis_wo[...].T
        stem_t[:, WIDTH:] = prop_wo[...].T
        for j in range(4):
            ln_ref[j] = jnp.broadcast_to(ln[j : j + 1, :], (WIDTH, WIDTH)).T
        acc[...] = jnp.zeros_like(acc)
        gsum[...] = jnp.zeros_like(gsum)
        gv_ref[...] = jnp.zeros_like(gv_ref)
        gp_ref[...] = jnp.zeros_like(gp_ref)
        lnacc[...] = jnp.zeros_like(lnacc)
        stat[...] = jnp.zeros_like(stat)

    masks = [masks_ref[h] for h in range(HEADS)]
    masks_group = [masks_ref[HEADS + h] for h in range(4)]
    qv, qp = qv_ref[...], qp_ref[...]
    lane = lane_iota(HEAD, WIDTH)
    low_half = jnp.where(lane < 64, 1.0, 0.0).astype(BF)
    high_half = jnp.where(lane < 64, 0.0, 1.0).astype(BF)
    first = lane_iota(64, WIDTH) < 64


    def chain(g):
        slots = slice(512 * g, 512 * g + 512)
        kept = nn(feats[slots], proj[...]).astype(BF)
        tok = (kept.astype(F32) + pr[slots].astype(F32)).astype(BF)
        vkv = nn(tok, vis_kv[...]).astype(BF)
        vk, vv = vkv[:, :WIDTH], vkv[:, WIDTH:]
        slot = lax.broadcasted_iota(jnp.int32, (64, WIDTH), 0)
        slot_row, slot_col = slot >> 3, slot & 7
        bias = []
        for st in range(8):
            s, t = (step * CHAINS + g) * 4 + st // 2, st % 2
            keep = (slot_row < grid_ref[2 * t, s]) & (slot_col < grid_ref[2 * t + 1, s])
            bias.append(jnp.where(keep, 0.0, NEG))
        bias = pair_up(bias).reshape(4, 64, 256)
        vk2 = pair_up([vk[64 * st : 64 * st + 64] for st in range(8)])
        vv2 = pair_up([vv[64 * st : 64 * st + 64] for st in range(8)])
        yield
        vp = softmax_rows(nt(vk2, qv).reshape(4, 64, 256) + bias)
        vpb = vp.reshape(256, 256).astype(BF)
        yield
        vpt = vpb.T
        vmixed = [None] * 8
        for e in range(2):
            for m in range(2):
                one, two = 4 * m + e, 4 * m + 2 + e
                spread = diagonal([vv[64 * one : 64 * one + 64], vv[64 * two : 64 * two + 64]])
                lhs = vpt[WIDTH * e : WIDTH * e + WIDTH, WIDTH * m : WIDTH * m + WIDTH]
                both = head_select(nn(lhs, spread), HEADS, WIDTH).astype(BF)
                vmixed[one], vmixed[two] = both[:, :WIDTH], both[:, WIDTH:]

        yield
        fr = frames[128 * g : 128 * g + 128]
        pre = nn(fr, prop_w1[...])
        gate = jax.nn.sigmoid(pre)
        hidden = (pre * gate).astype(BF)
        ptok = nn(hidden, prop_w2[...]).astype(BF)
        pkv = nn(ptok, prop_kv[...]).astype(BF)
        pk, pv = pkv[:, :WIDTH], pkv[:, WIDTH:]
        column = jnp.broadcast_to(aux[g, 3:4, :WIDTH], (WIDTH, WIDTH)).T
        parts = lambda v: [v[HEAD * st : HEAD * st + HEAD] for st in range(8)]
        pbias = pair_up(parts(column))
        pk2, pv2 = pair_up(parts(pk)), pair_up(parts(pv))
        yield
        pp = softmax_rows((nt(pk2, qp) + pbias).reshape(4, HEAD, 256))
        ppb = pp.reshape(64, 256).astype(BF)
        ppt = ppb.T
        pmixed = [None] * 8
        for e in range(2):
            spread = diagonal([pv[HEAD * st : HEAD * st + HEAD] for st in range(e, 8, 2)])
            both = head_select(nn(ppt[WIDTH * e : WIDTH * e + WIDTH], spread), HEADS, WIDTH).astype(BF)
            for j in range(4):
                pmixed[2 * j + e] = both[:, WIDTH * j : WIDTH * j + WIDTH]

        yield
        zero16 = jnp.zeros((HEAD, WIDTH), BF)
        rows = []
        for st in range(8):
            rows.append(cat([vmixed[st], zero16], 1))
            rows.append(cat([zero16, pmixed[st]], 1))
        mixed_ext = cat(rows, 0)
        x = nt(stem_t[...], mixed_ext)
        g1, b1, g2, b2 = [cat([ln_ref[j]] * 2, 1) for j in range(4)]
        hat1, scale1 = norm_rows(x)
        n1 = (hat1 * g1 + b1).astype(BF)
        yield
        qkv = nn(wqkv_t[...], n1).astype(BF)
        qt, kt, vt = qkv[:WIDTH] * jnp.asarray(0.25, BF), qkv[WIDTH : 2 * WIDTH], qkv[2 * WIDTH :]
        kn, vn = kt.T, vt.T
        kn_turned, vn_turned = turn(kn), turn(vn)
        yield
        weights, weights_b, query_bd = [], [], []
        tbias = []
        for p in range(2):
            column = jnp.broadcast_to(aux[g, 2:3, 128 * p : 128 * p + 128], (WIDTH, WIDTH)).T
            tbias.append(jnp.where(first, column[:64], column[64:]))
        tbias = cat(tbias, 1)[None]
        for group in range(2):
            part = slice(64 * group, 64 * group + 64)
            qbd = split_samples(qt[part], low_half, high_half)
            keys = head_expand(gather_heads(kn, kn_turned, group, low_half, high_half), masks_group)
            scores = nn(keys, qbd).reshape(4, 64, 256) + tbias
            yield
            w = softmax_rows(scores)
            weights.append(w)
            weights_b.append(w.reshape(256, 256).astype(BF))
            query_bd.append(qbd)
            yield
        mixed = mix_keys(vt, weights_b, low_half, high_half, first).astype(BF)
        yield
        branch = nn(ao_t[...], mixed)
        middle = x + branch
        hat2, scale2 = norm_rows(middle)
        n2 = (hat2 * g2 + b2).astype(BF)
        yield
        up = nn(win_t[...], n2)
        yield
        square = up * up
        c = math.sqrt(2.0 / math.pi)
        h = 0.5 + 0.5 * jnp.tanh(up * (c + (c * 0.044715) * square))
        act = up * h
        slope = h + act * (1.0 - h) * (2 * c + (6 * c * 0.044715) * square)
        act_b = act.astype(BF)
        yield
        mlp = nn(wout_t[...], act_b)
        final = middle + mlp
        out[256 * g : 256 * g + 256] = final.astype(BF).T
        valid, mix = aux[g, 0:1, :], aux[g, 1:2, :]
        for j, value in enumerate((final, branch, mlp)):
            stat[j : j + 1, :] += jnp.sum(value * value, axis=0, keepdims=True) * valid
        stat[3:4, :] += valid

        yield
        seed = cot[256 * g : 256 * g + 256].T.astype(F32) * mix
        dmlp = seed.astype(BF)
        acc[R_WOUT : R_WOUT + 512] += nt(act_b, dmlp)
        dup = (nn(mlp_out[...], dmlp) * slope).astype(BF)
        acc[R_WIN : R_WIN + 512] += nt(dup, n2)
        yield
        dn2 = nn(mlp_in[...], dup)
        fold = lambda v: v[:, :WIDTH] + v[:, WIDTH:]
        lnacc[2] += fold(dn2 * hat2)
        lnacc[3] += fold(dn2)
        dmid = seed + norm_rows_grad(dn2 * g2, hat2, scale2)
        dbranch = dmid.astype(BF)
        acc[R_AO : R_AO + WIDTH] += nt(mixed, dbranch)
        yield
        dmixed = nn(attn_out[...], dbranch).astype(BF)
        yield
        ds_all, dk, dv = [], [], []
        for group in range(2):
            part = slice(64 * group, 64 * group + 64)
            dbd = split_samples(dmixed[part], low_half, high_half)
            values = head_expand(gather_heads(vn, vn_turned, group, low_half, high_half), masks_group)
            dw = nn(values, dbd).reshape(4, 64, 256)
            yield
            ds = softmax_grad(weights[group], dw).reshape(256, 256).astype(BF)
            dv.append(head_select(nt(weights_b[group], dbd), 4, 64).astype(BF))
            dk.append(head_select(nt(ds, query_bd[group]), 4, 64).astype(BF))
            ds_all.append(ds)
        dq = (mix_keys(kt, ds_all, low_half, high_half, first) * 0.25).astype(BF)
        dkv = cat([scatter_heads(dk, low_half, high_half), scatter_heads(dv, low_half, high_half)], 1)
        yield
        acc[R_Q : R_Q + WIDTH] += nt(n1, dq)
        grad = nn(n1, dkv)
        acc[R_KV : R_KV + WIDTH] += grad[:, :WIDTH]
        acc[R_KV + WIDTH : R_KV + 2 * WIDTH] += grad[:, WIDTH:]
        dn1 = nn(qkv_w[:, :WIDTH], dq) + nt(qkv_w[:, WIDTH:], dkv)
        lnacc[0] += fold(dn1 * hat1)
        lnacc[1] += fold(dn1)
        dx = (dmid + norm_rows_grad(dn1 * g1, hat1, scale1)).astype(BF)

        yield
        grad = nn(dx, mixed_ext)
        acc[R_SWO : R_SWO + WIDTH] += grad[:, :WIDTH]
        acc[R_SWO + WIDTH : R_SWO + 2 * WIDTH] += grad[:, WIDTH:]
        dstem = nn(dx.T, stem_t[...]).astype(BF)
        dw, dv, pdw, pdv = [], [], [], []
        for st in range(8):
            j, e, r = st // 2, st % 2, 32 * st
            tall, short, lanes = slice(64 * j, 64 * j + 64), slice(HEAD * j, HEAD * j + HEAD), slice(WIDTH * e, WIDTH * e + WIDTH)
            spread = head_expand(cat([dstem[r : r + 16, :WIDTH], dstem[r + 16 : r + 32, WIDTH:]], 1), masks)
            full = nt(diagonal([vv2[tall, lanes], pv2[short, lanes]]), spread)
            dw.append(full[:64])
            pdw.append(full[64:])
            full = nn(
                diagonal([vpb[tall, lanes], ppb[short, lanes]]), cat([spread[:, :WIDTH], spread[:, WIDTH:]], 0)
            ).astype(BF)
            dv.append(full[:64])
            pdv.append(full[64:])
        yield
        ds = softmax_grad(vp, pair_up(dw).reshape(4, 64, 256)).reshape(256, 256).astype(BF)
        dkv = cat([unpair(nn(ds, qv).astype(BF), 64), cat(dv, 0)], 1)
        dtok = nt(dkv, vis_kv[...]).astype(BF)
        dtok_ref[slots] = dtok
        grad_feats[slots] = nt(dtok, proj[...]).astype(BF)
        gsum[...] += nn(dtok.T, feats[slots])
        grad = nn(tok.T, dkv)
        acc[R_VKV : R_VKV + WIDTH] += grad[:, :WIDTH]
        acc[R_VKV + WIDTH : R_VKV + 2 * WIDTH] += grad[:, WIDTH:]
        full = nn(ds.T, vk2)
        gv_ref[...] += full[:WIDTH, :WIDTH] + full[WIDTH:, WIDTH:]

        yield
        ds = softmax_grad(pp, pair_up(pdw).reshape(4, HEAD, 256)).reshape(64, 256).astype(BF)
        dkv = cat([unpair(nn(ds, qp).astype(BF), HEAD), cat(pdv, 0)], 1)
        dptok = nt(dkv, prop_kv[...]).astype(BF)
        grad = nn(ptok.T, dkv)
        acc[R_PKV : R_PKV + WIDTH] += grad[:, :WIDTH]
        acc[R_PKV + WIDTH : R_PKV + 2 * WIDTH] += grad[:, WIDTH:]
        full = nn(ds.T, pk2)
        gp_ref[...] += full[:WIDTH, :WIDTH] + full[WIDTH:, WIDTH:]
        yield
        acc[R_W2 : R_W2 + WIDTH] += nn(hidden.T, dptok)
        dhidden = nt(dptok, prop_w2[...])
        dpre = (dhidden * (gate * (1.0 + pre * (1.0 - gate)))).astype(BF)
        acc[R_W1 : R_W1 + 32] += nn(fr.T, dpre)
        dframes[128 * g : 128 * g + 128] = nt(dpre, prop_w1[...]).astype(BF)

        yield

    live = [chain(g) for g in range(CHAINS)]
    while live:
        for one in list(live):
            if next(one, live) is live:
                live.remove(one)

    @pl.when(step == pl.num_programs(0) - 1)
    def _():
        acc[R_QV : R_QV + 16] = head_select(gv_ref[...], HEADS, WIDTH) * 0.25
        acc[R_QP : R_QP + 16] = head_select(gp_ref[...], HEADS, WIDTH) * 0.25
        for j in range(4):
            acc[R_LN + j : R_LN + j + 1] = jnp.sum(lnacc[j].T, axis=0, keepdims=True)
            acc[R_STAT + j : R_STAT + j + 1] = stat[j : j + 1, :WIDTH] + stat[j : j + 1, WIDTH:]


def whole(shape):
    return pl.BlockSpec(shape, lambda i, *_: (0,) * len(shape))


def block_call(half, grid_sizes, feats, received, frames, aux, cot, proj, weights):
    steps = aux.shape[0] // CHAINS
    channels = feats.shape[1]
    row = lambda i, *_: (i, 0)
    own = lambda i, half, _: (half[0] * steps + i, 0)
    in_specs = [
        pl.BlockSpec((512 * CHAINS, channels), own),
        pl.BlockSpec((512 * CHAINS, WIDTH), row),
        pl.BlockSpec((128 * CHAINS, frames.shape[1]), row),
        pl.BlockSpec((CHAINS, 8, 256), lambda i, *_: (i, 0, 0)),
        pl.BlockSpec((256 * CHAINS, WIDTH), row),
        whole(proj.shape),
    ] + [whole(w.shape) for w in weights]
    out_shape = (
        jax.ShapeDtypeStruct((256 * CHAINS * steps, WIDTH), BF),
        jax.ShapeDtypeStruct(feats.shape, BF),
        jax.ShapeDtypeStruct((512 * CHAINS * steps, WIDTH), BF),
        jax.ShapeDtypeStruct((128 * CHAINS * steps, frames.shape[1]), BF),
        jax.ShapeDtypeStruct((R_END, WIDTH), F32),
        jax.ShapeDtypeStruct((WIDTH, channels), F32),
    )
    out_specs = (
        pl.BlockSpec((256 * CHAINS, WIDTH), row),
        pl.BlockSpec((512 * CHAINS, channels), own),
        pl.BlockSpec((512 * CHAINS, WIDTH), row),
        pl.BlockSpec((128 * CHAINS, frames.shape[1]), row),
        whole((R_END, WIDTH)),
        whole((WIDTH, channels)),
    )
    scratch = [
        pltpu.VMEM((12, 16, WIDTH), BF),
        pltpu.VMEM((256, 256), BF),
        pltpu.VMEM((256, 256), BF),
        pltpu.VMEM((384, WIDTH), BF),
        pltpu.VMEM((128, WIDTH), BF),
        pltpu.VMEM((512, WIDTH), BF),
        pltpu.VMEM((128, 512), BF),
        pltpu.VMEM((128, 256), BF),
        pltpu.VMEM((4, WIDTH, WIDTH), F32),
        pltpu.VMEM((WIDTH, WIDTH), F32),
        pltpu.VMEM((WIDTH, WIDTH), F32),
        pltpu.VMEM((4, WIDTH, WIDTH), F32),
        pltpu.VMEM((8, 256), F32),
    ]
    return pl.pallas_call(
        block_kernel,
        grid_spec=pltpu.PrefetchScalarGridSpec(
            num_scalar_prefetch=2,
            grid=(steps,),
            in_specs=in_specs,
            out_specs=out_specs,
            scratch_shapes=scratch,
        ),
        out_shape=out_shape,
        compiler_params=pltpu.CompilerParams(vmem_limit_bytes=VMEM_LIMIT),
        name="stems_trunk",
    )(half, grid_sizes, feats, received, frames, aux, cot, proj, *weights)


def make_aux(proprio_mask, token_valid, mix_weight):
    samples, seq = token_valid.shape
    steps = samples // 4
    valid = token_valid.reshape(steps, 1, 4 * seq).astype(F32)
    mix = jnp.broadcast_to(mix_weight.astype(F32)[:, None], (samples, seq)).reshape(steps, 1, 4 * seq)
    vbias = jnp.where(valid > 0, 0.0, NEG)
    pbias = jnp.where(proprio_mask.reshape(steps, 1, -1) > 0, 0.0, NEG)
    pbias = jnp.concatenate([pbias, jnp.zeros_like(pbias)], axis=2)
    rest = jnp.zeros((steps, 4, 4 * seq), F32)
    return jnp.concatenate([valid, mix, vbias, pbias, rest], axis=1)

PROJECT_STEPS = 4
FEATURE_STEPS = 4


def project_kernel(half, feats, proj, out):
    out[...] = nn(feats[...], proj[...]).astype(BF)


def project_call(half, feats, proj):
    rows, channels = feats.shape[0] // 2, feats.shape[1]
    steps = PROJECT_STEPS
    return pl.pallas_call(
        project_kernel,
        grid_spec=pltpu.PrefetchScalarGridSpec(
            num_scalar_prefetch=1,
            grid=(steps,),
            in_specs=[
                pl.BlockSpec((rows // steps, channels), lambda i, half: (half[0] * steps + i, 0)),
                whole(proj.shape),
            ],
            out_specs=pl.BlockSpec((rows // steps, WIDTH), lambda i, half: (i, 0)),
        ),
        out_shape=jax.ShapeDtypeStruct((rows, WIDTH), BF),
        compiler_params=pltpu.CompilerParams(vmem_limit_bytes=VMEM_LIMIT),
        cost_estimate=pl.CostEstimate(
            flops=2 * rows * channels * WIDTH, bytes_accessed=2 * rows * (channels + WIDTH), transcendentals=0
        ),
        name="project",
    )(half, feats, proj)


def unpack_kernel(
    half, dother, proj, before, total, gfeat, vis_query, vis_wq, prop_query, prop_wq,
    o_vision, o_feat, o_vq, o_vwq, o_vkv, o_vwo, o_w1, o_w2, o_pq, o_pwq, o_pkv, o_pwo,
    o_g1, o_b1, o_qkv, o_ao, o_g2, o_b2, o_in, o_out, o_rms,
):
    o_vision[...] = nt(dother[...], proj[...]).astype(BF)

    @pl.when(pl.program_id(0) == 0)
    def _():
        def rows(start, count):
            return total[start : start + count].astype(F32)

        o_feat[...] = gfeat[...].astype(F32).T
        for o_query, o_w, query, w, start in (
            (o_vq, o_vwq, vis_query, vis_wq, R_QV),
            (o_pq, o_pwq, prop_query, prop_wq, R_QP),
        ):
            grad = rows(start, 16).astype(BF)
            o_query[...] = nt(grad, w[...])
            o_w[...] = lax.dot_general(
                query[...], grad, (((0,), (0,)), ((), ())), preferred_element_type=F32
            )
        for o, start in ((o_vkv, R_VKV), (o_pkv, R_PKV)):
            o[:, :WIDTH] = rows(start, WIDTH)
            o[:, WIDTH:] = rows(start + WIDTH, WIDTH)
        o_vwo[...] = rows(R_SWO, WIDTH).T
        o_pwo[...] = rows(R_SWO + WIDTH, WIDTH).T
        o_w1[...] = rows(R_W1, 32)
        o_w2[...] = rows(R_W2, WIDTH)
        for j in range(3):
            o_qkv[:, WIDTH * j : WIDTH * j + WIDTH] = rows(R_Q + WIDTH * j, WIDTH)
        o_ao[...] = rows(R_AO, WIDTH)
        o_in[...] = rows(R_WIN, 512).T
        o_out[...] = rows(R_WOUT, 512)
        small = rows(R_LN, 16)
        for j, o in enumerate((o_g1, o_b1, o_g2, o_b2)):
            o[...] = small[j : j + 1]
        sums = jnp.sum(small[R_STAT - R_LN : R_STAT - R_LN + 4], axis=1, keepdims=True)
        o_rms[...] = jnp.broadcast_to(jnp.sqrt(sums / (sums[3:4] * WIDTH)), (4, WIDTH))


def unpack_call(half, dother, proj, grad_vision, total, gfeat, vis_query, vis_wq, prop_query, prop_wq):
    rows, channels = dother.shape[0], proj.shape[0]
    steps = FEATURE_STEPS
    shapes = [
        (gfeat.shape[1], WIDTH), (16, WIDTH), (WIDTH, WIDTH), (WIDTH, 256), (WIDTH, WIDTH), (32, WIDTH),
        (WIDTH, WIDTH), (16, WIDTH), (WIDTH, WIDTH), (WIDTH, 256), (WIDTH, WIDTH), (1, WIDTH), (1, WIDTH),
        (WIDTH, 384), (WIDTH, WIDTH), (1, WIDTH), (1, WIDTH), (WIDTH, 512), (512, WIDTH), (4, WIDTH),
    ]
    args = (proj, grad_vision, total, gfeat, vis_query, vis_wq, prop_query, prop_wq)
    return pl.pallas_call(
        unpack_kernel,
        grid_spec=pltpu.PrefetchScalarGridSpec(
            num_scalar_prefetch=1,
            grid=(steps,),
            in_specs=[pl.BlockSpec((rows // steps, WIDTH), lambda i, half: (i, 0)), whole(proj.shape)]
            + [pl.BlockSpec(memory_space=pl.ANY)]
            + [whole(a.shape) for a in args[2:]],
            out_specs=[pl.BlockSpec((rows // steps, channels), lambda i, half: (half[0] * steps + i, 0))]
            + [whole(s) for s in shapes],
        ),
        out_shape=[jax.ShapeDtypeStruct(grad_vision.shape, BF)] + [jax.ShapeDtypeStruct(s, F32) for s in shapes],
        input_output_aliases={3: 0},
        compiler_params=pltpu.CompilerParams(vmem_limit_bytes=VMEM_LIMIT),
        name="unpack",
    )(half, dother, *args)


def finish_kernel(
    n, chunk, gchunk, acc, gsum, dtok, feats, total, gout, dother,
    fbuf, send_a, recv_a, send_b, recv_b, reduced, gathered, recv_d, send_g, recv_g, reduced_g, gathered_g,
    sem_t, sem_f, sem_a, sem_b, sem_c, sem_d, sem_bg, sem_cg,
):
    me, core = lax.axis_index("dp"), lax.axis_index("mod")
    mesh = pl.DeviceIdType.MESH
    partner = (me, 1 - core)
    half = R_END // 2
    slots, channels = fbuf.shape
    piece = slots // FEATURE_STEPS

    def remote(src, dst, send_sem, recv_sem, device):
        return pltpu.make_async_remote_copy(
            src_ref=src, dst_ref=dst, send_sem=send_sem, recv_sem=recv_sem, device_id=device, device_id_type=mesh
        )

    def rows(index, count):
        return pl.ds(pl.multiple_of(index * count, 16), count)

    barrier = pltpu.get_barrier_semaphore()
    pl.semaphore_signal(barrier, inc=1, device_id=partner, device_id_type=mesh)

    def greet(k, carry):
        pl.semaphore_signal(barrier, inc=1, device_id=(lax.rem(me + k, n), core), device_id_type=mesh)
        return carry

    lax.fori_loop(1, n, greet, 0)
    pl.semaphore_wait(barrier, n)

    send_a[...] = acc[rows(1 - core, half)].astype(BF)
    copy_a = remote(send_a, recv_a, sem_a.at[0], sem_a.at[1], partner)
    copy_a.start()
    tokens, features = [], []
    for j in range(FEATURE_STEPS):
        part = pl.ds(piece * j, piece)
        tokens.append(remote(dtok.at[part], dother.at[part], sem_t.at[0, j], sem_t.at[1, j], partner))
        tokens[j].start()
        start_row = pl.multiple_of((1 - core) * slots + piece * j, 16)
        features.append(pltpu.make_async_copy(feats.at[pl.ds(start_row, piece)], fbuf.at[part], sem_f.at[j]))
        features[j].start()
    if half < n * chunk:
        send_b[half:] = jnp.zeros((n * chunk - half, WIDTH), BF)
    copy_a.wait()
    send_b[:half] = (acc[rows(core, half)] + recv_a[...].astype(F32)).astype(BF)

    def scatter(k):
        peer = lax.rem(me + k, n)
        return remote(
            send_b.at[rows(peer, chunk)], recv_b.at[k - 1], sem_b.at[0, k - 1], sem_b.at[1, k - 1], (peer, core)
        )

    def gather(k):
        peer = lax.rem(me + k, n)
        return remote(
            reduced, gathered.at[rows(me, chunk)], sem_c.at[0, k - 1], sem_c.at[1, k - 1], (peer, core)
        )

    def scatter_g(k):
        peer = lax.rem(me + k, n)
        return remote(
            send_g.at[rows(peer, gchunk)], recv_g.at[k - 1], sem_bg.at[0, k - 1], sem_bg.at[1, k - 1], (peer, core)
        )

    def gather_g(k):
        peer = lax.rem(me + k, n)
        return remote(
            reduced_g, gathered_g.at[rows(me, gchunk)], sem_cg.at[0, k - 1], sem_cg.at[1, k - 1], (peer, core)
        )

    def forward(k):
        owner = rows(lax.rem(me + n - k, n), chunk)
        return remote(gathered.at[owner], recv_d.at[owner], sem_d.at[0, k], sem_d.at[1, k], partner)

    def each(first, step):
        def body(k, carry):
            step(k)
            return carry

        lax.fori_loop(first, n, body, 0)

    each(1, lambda k: scatter(k).start())

    grad = gsum[...]
    for j in range(FEATURE_STEPS):
        tokens[j].wait()
        features[j].wait()
        part = slice(piece * j, piece * j + piece)
        grad = grad + nn(dother[part].T, fbuf[part])
    used = WIDTH * (channels // WIDTH)
    for j in range(channels // WIDTH):
        send_g[WIDTH * j : WIDTH * j + WIDTH] = grad[:, WIDTH * j : WIDTH * j + WIDTH].astype(BF)
    if used < n * gchunk:
        send_g[used:] = jnp.zeros((n * gchunk - used, WIDTH), BF)
    each(1, lambda k: scatter_g(k).start())

    each(1, lambda k: scatter(k).wait())
    value = send_b[rows(me, chunk)].astype(F32)
    value = lax.fori_loop(0, n - 1, lambda k, v: v + recv_b[k].astype(F32), value)
    reduced[...] = value.astype(BF)
    gathered[rows(me, chunk)] = reduced[...]
    each(1, lambda k: gather(k).start())
    forward(0).start()

    each(1, lambda k: scatter_g(k).wait())
    value = send_g[rows(me, gchunk)].astype(F32)
    value = lax.fori_loop(0, n - 1, lambda k, v: v + recv_g[k].astype(F32), value)
    reduced_g[...] = value.astype(BF)
    gathered_g[rows(me, gchunk)] = reduced_g[...]
    each(1, lambda k: gather_g(k).start())

    def pass_on(k):
        gather(k).wait()
        forward(k).start()

    each(1, pass_on)
    total[rows(core, half)] = gathered[:half]
    each(1, lambda k: gather_g(k).wait())
    for j in range(channels // WIDTH):
        gout[:, WIDTH * j : WIDTH * j + WIDTH] = gathered_g[WIDTH * j : WIDTH * j + WIDTH]
    each(0, lambda k: forward(k).wait())
    total[rows(1 - core, half)] = recv_d[:half]


def finish_call(acc, gsum, dtok, feats, n):
    slots, channels = dtok.shape[0], feats.shape[1]
    half = R_END // 2
    chunk = 16 * -(-half // (16 * n))
    gchunk = 16 * -(-channels // (16 * n))
    vmem = pl.BlockSpec(memory_space=pltpu.VMEM)
    hbm = pl.BlockSpec(memory_space=pl.ANY)
    dma = pltpu.SemaphoreType.DMA
    return pl.pallas_call(
        functools.partial(finish_kernel, n, chunk, gchunk),
        out_shape=(
            jax.ShapeDtypeStruct(acc.shape, BF),
            jax.ShapeDtypeStruct(gsum.shape, BF),
            jax.ShapeDtypeStruct(dtok.shape, BF),
        ),
        in_specs=[vmem, vmem, hbm, hbm],
        out_specs=(vmem, vmem, vmem),
        scratch_shapes=[
            pltpu.VMEM((slots, channels), BF),
            pltpu.VMEM((half, WIDTH), BF),
            pltpu.VMEM((half, WIDTH), BF),
            pltpu.VMEM((n * chunk, WIDTH), BF),
            pltpu.VMEM((n - 1, chunk, WIDTH), BF),
            pltpu.VMEM((chunk, WIDTH), BF),
            pltpu.VMEM((n * chunk, WIDTH), BF),
            pltpu.VMEM((n * chunk, WIDTH), BF),
            pltpu.VMEM((n * gchunk, WIDTH), BF),
            pltpu.VMEM((n - 1, gchunk, WIDTH), BF),
            pltpu.VMEM((gchunk, WIDTH), BF),
            pltpu.VMEM((n * gchunk, WIDTH), BF),
            dma((2, FEATURE_STEPS)),
            dma((FEATURE_STEPS,)),
            dma((2,)),
            dma((2, n - 1)),
            dma((2, n - 1)),
            dma((2, n)),
            dma((2, n - 1)),
            dma((2, n - 1)),
        ],
        compiler_params=pltpu.CompilerParams(
            collective_id=0, has_side_effects=True, vmem_limit_bytes=VMEM_LIMIT
        ),
        name="finish",
    )(acc, gsum, dtok, feats)


def per_device(
    vision_feats, vision_grid, proprio, proprio_mask, token_valid, mix_weight, out_cot, feat_proj,
    vis_query, vis_wq, vis_kv, vis_wo, prop_w1, prop_w2, prop_query, prop_wq, prop_kv, prop_wo,
    ln1_gain, ln1_bias, qkv_weight, attn_out, ln2_gain, ln2_bias, mlp_in, mlp_out,
):
    me = lax.axis_index("mod").astype(jnp.int32)
    own, other = me.reshape(1), (1 - me).reshape(1)
    swap = [(0, 1), (1, 0)]
    feats = vision_feats.reshape(-1, vision_feats.shape[3])
    sent = project_call(other, feats, feat_proj)
    received = lax.ppermute(sent, "mod", swap)
    aux = make_aux(proprio_mask, token_valid, mix_weight)
    ln = jnp.stack([ln1_gain, ln1_bias, ln2_gain, ln2_bias]).astype(F32)
    weights = (
        vis_query, vis_wq, vis_kv, vis_wo, prop_w1, prop_w2, prop_query, prop_wq, prop_kv, prop_wo,
        ln, qkv_weight, attn_out, mlp_in, mlp_out,
    )
    frames = proprio.reshape(-1, proprio.shape[3])
    grid_sizes = jnp.transpose(vision_grid, (1, 2, 0)).reshape(4, -1)
    output, grad_vision, dtok, dframes, acc, gfeat = block_call(
        own, grid_sizes, feats, received, frames, aux, out_cot.reshape(-1, WIDTH), feat_proj, weights
    )
    total, gfeat, dother = finish_call(acc, gfeat, dtok, feats, lax.axis_size("dp"))
    grad_vision, *outs = unpack_call(
        other, dother, feat_proj, grad_vision, total, gfeat, vis_query, vis_wq, prop_query, prop_wq
    )
    vectors = {11, 12, 15, 16}
    outs = [o.reshape(WIDTH) if j in vectors else o for j, o in enumerate(outs)]
    return (
        output.reshape(out_cot.shape),
        grad_vision.reshape(vision_feats.shape),
        dframes.reshape(proprio.shape),
        *outs[:-1],
        outs[-1][:3, 0],
    )


def solution(mesh):
    both = ("dp", "mod")
    return jax.shard_map(
        per_device,
        mesh=mesh,
        in_specs=(
            P("dp", None, None, "mod"),
            P(both, None, None),
            P(both, None, None, None),
            P(both, None, None),
            P(both, None),
            P(both),
            P(both, None, None),
            P("mod", None),
        ) + (P(),) * 18,
        out_specs=(
            P(both, None, None),
            P("dp", None, None, "mod"),
            P(both, None, None, None),
            P("mod", None),
        ) + (P(),) * 19,
        check_vma=False,
    )
```

time: 126 us -> 118 us (0.937)
  Pallas kernels: 111 us -> 106 us
  waiting for transfers between devices: 2.13 us -> 0.39 us
  local copies, waits for them, and re-layouts: 9.13 us -> 7.82 us
    pallas_call x1, Pallas kernels: 66.6 us -> 63.4 us  [block_call(): pl.pallas_call(block_kernel, grid_spec=pltpu.PrefetchScalarGridSpec(num_s...]
    pallas_call x3 -> x2, Pallas kernels: 39.8 us -> 37.5 us  [the longest x1 31.6 us: finish_call(): pl.pallas_call(functools.partial(finish_kernel, n, chunk, gchunk), out_sh...]
    ppermute x1 -> x0, waiting for transfers between devices: 1.74 us -> none  [per_device(): dtok_other = lax.ppermute(dtok, 'mod', swap)]
    unnamed x22 -> x20, local copies, waits for them, and re-layouts: 6.47 us -> 5.15 us
  transfers between devices with their start and end apart: 2 -> 1, of which waited for: 2 -> 1; matrix products, arithmetic and copies ran while one was open for 5% -> 3% of each run, Pallas kernels for 0% -> 0%
where the time goes in v4:
time: 118 us; the launch traced here: 116 us
  Pallas kernels  106 us (90%)
  local copies, waits for them, and re-layouts  7.82 us (7%)
    pallas_call x1, Pallas kernels, block_call(): pl.pallas_call(block_kernel, grid_spec=pltpu.PrefetchScalarGridSpec(num_s...  63.4 us
    pallas_call x1, Pallas kernels, finish_call(): pl.pallas_call(functools.partial(finish_kernel, n, chunk, gchunk), out_sh...  31.6 us
    pallas_call x1, Pallas kernels, unpack_call(): pl.pallas_call(unpack_kernel, grid_spec=pltpu.PrefetchScalarGridSpec(num_...  5.98 us
    unnamed x20, local copies, waits for them, and re-layouts  5.15 us
    pallas_call x1, Pallas kernels, project_call(): pl.pallas_call(project_kernel, grid_spec=pltpu.PrefetchScalarGridSpec(num...  5.09 us
  transfers between devices with their start and end apart: 1, of which 1 were waited for; matrix products, arithmetic and copies ran while one was open for 3% of the time, Pallas kernels for 0%

profile of v4, /device:TPU:25, one launch (start us, length us, event | category | flops | bytes accessed | tf_op | source)
XLA Modules:
  0.0 116.3 jit_solution(1193495909089243252)
XLA Ops:
  0.7 0.0 copy-start.8
  0.7 0.0 copy-start.2
  0.7 0.0 copy-start.3
  0.7 5.1 %project.1 = bf16[8192,128]{1,0:T(8,128)(2,1)} custom-call(s32[1]{0:T(128)} %bitcast.4.half, bf16[16384,256]{1,0:T(8,128)(2,1)} %bitcast.20, bf16[256,128]{1,0:T(8,128)(2,1)} %proj.5), custom_call_target="tpu_custom_call" | custom-call | flops 536870912 | bytes 6291456 | tf_op jit(solution)/shard_map/project/pallas_call | solution.py:514
  5.8 0.7 collective-permute-start
  6.5 0.0 copy-done.8
  6.5 0.1 broadcast_in_dim.28
  6.6 0.1 broadcast_in_dim.29
  6.7 0.1 broadcast_in_dim.30
  6.8 0.1 convert_element_type.25
  6.9 0.0 copy-done.3
  6.9 0.1 copy.54
  7.0 0.1 select_n.29
  7.1 1.5 %copy.53 = bf16[64,2,16,32]{3,2,1,0:T(8,128)(2,1)} copy(bf16[64,2,16,32]{0,3,2,1:T(8,128)(2,1)S(1)} %copy-done.1) | data formatting | bytes 262144 | tf_op args[2]
  8.7 0.8 concatenate.7.aux
  9.5 0.0 copy-done.4
  9.5 0.6 maximum_convert_fusion.ln
  10.1 0.4 collective-permute-done.pr
  10.5 1.3 %copy-done = bf16[8192,128]{1,0:T(8,128)(2,1)} copy-done((bf16[8192,128]{1,0:T(8,128)(2,1)}, bf16[8192,128]{1,0:T(8,128)(2,1)S(1)}, u32[]{:S(2)}) %copy-start) | copy-done | bytes 2097176
  11.8 63.4 %stems_trunk.1 = (bf16[4096,128]{1,0:T(8,128)(2,1)}, bf16[16384,256]{1,0:T(8,128)(2,1)}, bf16[8192,128]{1,0:T(8,128)(2,1)}, bf16[2048,32]{1,0:T(8,128)(2,1)}, f32[2560,128]{1,0:T(8,128)}, /*index=5*/f32[128,256]{1,0:T(8,128)}) custom-call(s32[1]{0:T(128)} %bitcast.half, s32[4,64]{1,0:T(4,128)} %bitcast.28, bf16[16384,256]{1,0:T(8,128)(2,1)} %bitcast.21, ...), custom_call_target="tpu_custom_call" | custom-call | tf_op jit(solution)/shard_map/stems_trunk/pallas_call | solution.py:477
  75.2 2.3 %copy.56 = bf16[64,2,16,32]{0,3,2,1:T(8,128)(2,1)} copy(bf16[64,2,16,32]{3,2,1,0:T(8,128)(2,1)} %bitcast.26) | data formatting | bytes 262144
  77.5 31.6 %finish.1 = (bf16[2560,128]{1,0:T(8,128)(2,1)}, bf16[128,256]{1,0:T(8,128)(2,1)}, bf16[8192,128]{1,0:T(8,128)(2,1)}) custom-call(f32[2560,128]{1,0:T(8,128)} %get-tuple-element.54.acc, f32[128,256]{1,0:T(8,128)} %get-tuple-element.55.gsum, bf16[8192,128]{1,0:T(8,128)(2,1)} %get-tuple-element.56.dtok, bf16[16384,256]{1,0:T(8,128)(2,1)} %bitcast.22), custom_call_target="tpu_custom_call" | custom-call | tf_op jit(solution)/shard_map/finish/pallas_call | solution.py:734
  109.1 6.0 %unpack.1 = (bf16[16384,256]{1,0:T(8,128)(2,1)}, f32[256,128]{1,0:T(8,128)}, f32[16,128]{1,0:T(8,128)}, f32[128,128]{1,0:T(8,128)}, f32[128,256]{1,0:T(8,128)}, ...) custom-call(s32[1]{0:T(128)} %bitcast.4.half, ...), custom_call_target="tpu_custom_call", output_to_operand_aliasing={{0}: (3, {})} | custom-call | tf_op jit(solution)/shard_map/unpack/pallas_call | solution.py:584
  115.0 1.3 %slice_reduce_fusion = f32[3]{0:T(128)} fusion(f32[4,128]{1,0:T(4,128)} %get-tuple-element.82), kind=kLoop, calls=%fused_computation.2 | loop fusion | bytes 24 | tf_op jit(solution)/shard_map/slice | solution.py:805
  (17 shorter events, 0.1 us)
Async XLA Ops:
  0.7 5.8 %copy-start.8 = (s32[64]{0:T(128)S(1)}, s32[64]{0:T(128)}, u32[]{:S(2)}) copy-start(s32[64]{0:T(128)} %param.31) | copy-start | bytes 772
  0.7 6.1 %copy-start.2 = (s32[64,64]{1,0:T(8,128)S(1)}, s32[64,64]{1,0:T(8,128)}, u32[]{:S(2)}) copy-start(s32[64,64]{1,0:T(8,128)} %param.30) | copy-start | bytes 49156
  0.7 6.2 %copy-start.3 = (s32[64,2,16]{0,2,1:T(8,128)S(1)}, s32[64,2,16]{0,2,1:T(8,128)}, u32[]{:S(2)}) copy-start(s32[64,2,16]{0,2,1:T(8,128)} %param.29) | copy-start | bytes 24580
  0.7 6.5 %copy-start.1 = (bf16[64,2,16,32]{0,3,2,1:T(8,128)(2,1)S(1)}, bf16[64,2,16,32]{0,3,2,1:T(8,128)(2,1)}, u32[]{:S(2)}) copy-start(bf16[64,2,16,32]{0,3,2,1:T(8,128)(2,1)} %param.28) | copy-start | bytes 393220
  0.7 8.8 %copy-start.4 = (bf16[128]{0:T(256)(128)(2,1)S(1)}, bf16[128]{0:T(256)(128)(2,1)}, u32[]{:S(2)}) copy-start(bf16[128]{0:T(256)(128)(2,1)} %param.49) | copy-start | bytes 772
  0.7 8.8 %copy-start.5 = (bf16[128]{0:T(256)(128)(2,1)S(1)}, bf16[128]{0:T(256)(128)(2,1)}, u32[]{:S(2)}) copy-start(bf16[128]{0:T(256)(128)(2,1)} %param.48) | copy-start | bytes 772
  0.7 8.8 %copy-start.6 = (bf16[128]{0:T(256)(128)(2,1)S(1)}, bf16[128]{0:T(256)(128)(2,1)}, u32[]{:S(2)}) copy-start(bf16[128]{0:T(256)(128)(2,1)} %param.45) | copy-start | bytes 772
  0.7 8.8 %copy-start.7 = (bf16[128]{0:T(256)(128)(2,1)S(1)}, bf16[128]{0:T(256)(128)(2,1)}, u32[]{:S(2)}) copy-start(bf16[128]{0:T(256)(128)(2,1)} %param.44) | copy-start | bytes 772
  5.8 4.7 %collective-permute-start = (bf16[8192,128]{1,0:T(8,128)(2,1)}, bf16[8192,128]{1,0:T(8,128)(2,1)S(1)}, u32[]{:S(2)}, u32[]{:S(2)}) collective-permute-start(bf16[8192,128]{1,0:T(8,128)(2,1)} %project.1), channel_id=1, source_target_pairs={{0,1},{1,0},{2,3},{3,2},{4,5},{5,4},{6,7},{7,6},{8,9},{9,8},{10,11... | collective-permute-start | bytes 6291464 | tf_op jit(solution)/shard_map/ppermute | solution.py:782
  10.5 1.3 %copy-start = (bf16[8192,128]{1,0:T(8,128)(2,1)}, bf16[8192,128]{1,0:T(8,128)(2,1)S(1)}, u32[]{:S(2)}) copy-start(bf16[8192,128]{1,0:T(8,128)(2,1)S(1)} %collective-permute-done.pr) | copy-start | bytes 6291460

commit v5 on v4

--- a/solution.py
+++ b/solution.py
@@ -11,11 +11,13 @@
 HEADS = 8
 HEAD = 16
 WIDTH = 128
+PROP = 32
 NEG = -1e30
 BF = jnp.bfloat16
 F32 = jnp.float32
 VMEM_LIMIT = 60 * 2**20
-CHAINS = 4
+CHAINS = 8
+FF_PART = 256
 
 R_WIN, R_WOUT, R_Q, R_KV, R_AO = 0, 512, 1024, 1152, 1408
 R_SWO, R_VKV, R_PKV, R_W2, R_W1 = 1536, 1792, 2048, 2304, 2432
@@ -171,9 +173,9 @@
     half, grid_ref, feats, pr, frames, aux, cot, proj,
     vis_query, vis_wq, vis_kv, vis_wo, prop_w1, prop_w2, prop_query, prop_wq, prop_kv, prop_wo,
     ln, qkv_w, attn_out, mlp_in, mlp_out,
-    out, grad_feats, dtok_ref, dframes, acc, gsum,
+    out, grad_feats, dtok_ref, dframes, acc_out, gsum,
     masks_ref, qv_ref, qp_ref, wqkv_t, ao_t, win_t, wout_t, stem_t, ln_ref,
-    gv_ref, gp_ref, lnacc, stat,
+    gv_ref, gp_ref, lnacc, stat, acc, fr_ref, df_ref,
 ):
     step = pl.program_id(0)
 
@@ -195,6 +197,9 @@
         stem_t[:, WIDTH:] = prop_wo[...].T
         for j in range(4):
             ln_ref[j] = jnp.broadcast_to(ln[j : j + 1, :], (WIDTH, WIDTH)).T
+        for j in range(frames.shape[0] // PROP):
+            block = frames[PROP * j : PROP * j + PROP].astype(F32).T
+            fr_ref[pl.ds(j, block.shape[0], stride=frames.shape[0] // PROP)] = block
         acc[...] = jnp.zeros_like(acc)
         gsum[...] = jnp.zeros_like(gsum)
         gv_ref[...] = jnp.zeros_like(gv_ref)
@@ -242,7 +247,8 @@
                 vmixed[one], vmixed[two] = both[:, :WIDTH], both[:, WIDTH:]
 
         yield
-        fr = frames[128 * g : 128 * g + 128]
+        fr_rows = pl.ds(pl.multiple_of((step * CHAINS + g) * 128, 128), 128)
+        fr = fr_ref[fr_rows].astype(BF)
         pre = nn(fr, prop_w1[...])
         gate = jax.nn.sigmoid(pre)
         hidden = (pre * gate).astype(BF)
@@ -305,31 +311,34 @@
         hat2, scale2 = norm_rows(middle)
         n2 = (hat2 * g2 + b2).astype(BF)
         yield
-        up = nn(win_t[...], n2)
-        yield
-        square = up * up
         c = math.sqrt(2.0 / math.pi)
-        h = 0.5 + 0.5 * jnp.tanh(up * (c + (c * 0.044715) * square))
-        act = up * h
-        slope = h + act * (1.0 - h) * (2 * c + (6 * c * 0.044715) * square)
-        act_b = act.astype(BF)
-        yield
-        mlp = nn(wout_t[...], act_b)
+        seed = cot[256 * g : 256 * g + 256].T.astype(F32) * aux[g, 1:2, :]
+        dmlp = seed.astype(BF)
+        mlp, dn2, act_all, dup_all = 0.0, 0.0, [], []
+        for j in range(512 // FF_PART):
+            part = slice(FF_PART * j, FF_PART * j + FF_PART)
+            up = nn(win_t[part], n2)
+            yield
+            square = up * up
+            h = 0.5 + 0.5 * jnp.tanh(up * (c + (c * 0.044715) * square))
+            act = up * h
+            slope = h + act * (1.0 - h) * (2 * c + (6 * c * 0.044715) * square)
+            act_b = act.astype(BF)
+            mlp = mlp + nn(wout_t[:, part], act_b)
+            dup = (nn(mlp_out[part], dmlp) * slope).astype(BF)
+            yield
+            dn2 = dn2 + nn(mlp_in[:, part], dup)
+            acc[R_WOUT + FF_PART * j : R_WOUT + FF_PART * j + FF_PART] += nt(act_b, dmlp)
+            acc[R_WIN + FF_PART * j : R_WIN + FF_PART * j + FF_PART] += nt(dup, n2)
+            yield
         final = middle + mlp
         out[256 * g : 256 * g + 256] = final.astype(BF).T
-        valid, mix = aux[g, 0:1, :], aux[g, 1:2, :]
+        valid = aux[g, 0:1, :]
         for j, value in enumerate((final, branch, mlp)):
             stat[j : j + 1, :] += jnp.sum(value * value, axis=0, keepdims=True) * valid
         stat[3:4, :] += valid
 
         yield
-        seed = cot[256 * g : 256 * g + 256].T.astype(F32) * mix
-        dmlp = seed.astype(BF)
-        acc[R_WOUT : R_WOUT + 512] += nt(act_b, dmlp)
-        dup = (nn(mlp_out[...], dmlp) * slope).astype(BF)
-        acc[R_WIN : R_WIN + 512] += nt(dup, n2)
-        yield
-        dn2 = nn(mlp_in[...], dup)
         fold = lambda v: v[:, :WIDTH] + v[:, WIDTH:]
         lnacc[2] += fold(dn2 * hat2)
         lnacc[3] += fold(dn2)
@@ -407,15 +416,17 @@
         dhidden = nt(dptok, prop_w2[...])
         dpre = (dhidden * (gate * (1.0 + pre * (1.0 - gate)))).astype(BF)
         acc[R_W1 : R_W1 + 32] += nn(fr.T, dpre)
-        dframes[128 * g : 128 * g + 128] = nt(dpre, prop_w1[...]).astype(BF)
-
-        yield
-
-    live = [chain(g) for g in range(CHAINS)]
+        df_ref[fr_rows] = nt(dpre, prop_w1[...])
+
+        yield
+
+    live = [(g // 2 * 6, chain(g)) for g in range(CHAINS)]
+    tick = 0
     while live:
         for one in list(live):
-            if next(one, live) is live:
+            if tick >= one[0] and next(one[1], live) is live:
                 live.remove(one)
+        tick += 1
 
     @pl.when(step == pl.num_programs(0) - 1)
     def _():
@@ -424,6 +435,10 @@
         for j in range(4):
             acc[R_LN + j : R_LN + j + 1] = jnp.sum(lnacc[j].T, axis=0, keepdims=True)
             acc[R_STAT + j : R_STAT + j + 1] = stat[j : j + 1, :WIDTH] + stat[j : j + 1, WIDTH:]
+        acc_out[...] = acc[...].astype(BF)
+        for j in range(frames.shape[0] // PROP):
+            block = df_ref[pl.ds(j, frames.shape[1], stride=frames.shape[0] // PROP)]
+            dframes[PROP * j : PROP * j + PROP] = block.T.astype(BF)
 
 
 def whole(shape):
@@ -438,7 +453,7 @@
     in_specs = [
         pl.BlockSpec((512 * CHAINS, channels), own),
         pl.BlockSpec((512 * CHAINS, WIDTH), row),
-        pl.BlockSpec((128 * CHAINS, frames.shape[1]), row),
+        whole(frames.shape),
         pl.BlockSpec((CHAINS, 8, 256), lambda i, *_: (i, 0, 0)),
         pl.BlockSpec((256 * CHAINS, WIDTH), row),
         whole(proj.shape),
@@ -447,15 +462,15 @@
         jax.ShapeDtypeStruct((256 * CHAINS * steps, WIDTH), BF),
         jax.ShapeDtypeStruct(feats.shape, BF),
         jax.ShapeDtypeStruct((512 * CHAINS * steps, WIDTH), BF),
-        jax.ShapeDtypeStruct((128 * CHAINS * steps, frames.shape[1]), BF),
-        jax.ShapeDtypeStruct((R_END, WIDTH), F32),
+        jax.ShapeDtypeStruct(frames.shape, BF),
+        jax.ShapeDtypeStruct((R_END, WIDTH), BF),
         jax.ShapeDtypeStruct((WIDTH, channels), F32),
     )
     out_specs = (
         pl.BlockSpec((256 * CHAINS, WIDTH), row),
         pl.BlockSpec((512 * CHAINS, channels), own),
         pl.BlockSpec((512 * CHAINS, WIDTH), row),
-        pl.BlockSpec((128 * CHAINS, frames.shape[1]), row),
+        whole(frames.shape),
         whole((R_END, WIDTH)),
         whole((WIDTH, channels)),
     )
@@ -473,6 +488,9 @@
         pltpu.VMEM((WIDTH, WIDTH), F32),
         pltpu.VMEM((4, WIDTH, WIDTH), F32),
         pltpu.VMEM((8, 256), F32),
+        pltpu.VMEM((R_END, WIDTH), F32),
+        pltpu.VMEM((frames.shape[0] // PROP * frames.shape[1], PROP), F32),
+        pltpu.VMEM((frames.shape[0] // PROP * frames.shape[1], PROP), F32),
     ]
     return pl.pallas_call(
         block_kernel,
@@ -532,77 +550,87 @@
 
 
 def unpack_kernel(
-    half, dother, proj, before, total, gfeat, vis_query, vis_wq, prop_query, prop_wq,
+    chunk, dother, proj, total, vis_query, vis_wq, prop_query, prop_wq, before,
     o_vision, o_feat, o_vq, o_vwq, o_vkv, o_vwo, o_w1, o_w2, o_pq, o_pwq, o_pkv, o_pwo,
-    o_g1, o_b1, o_qkv, o_ao, o_g2, o_b2, o_in, o_out, o_rms,
+    o_g1, o_b1, o_qkv, o_ao, o_g2, o_b2, o_in, o_out, o_rms, vision, sems,
 ):
-    o_vision[...] = nt(dother[...], proj[...]).astype(BF)
-
-    @pl.when(pl.program_id(0) == 0)
-    def _():
-        def rows(start, count):
-            return total[start : start + count].astype(F32)
-
-        o_feat[...] = gfeat[...].astype(F32).T
-        for o_query, o_w, query, w, start in (
-            (o_vq, o_vwq, vis_query, vis_wq, R_QV),
-            (o_pq, o_pwq, prop_query, prop_wq, R_QP),
-        ):
-            grad = rows(start, 16).astype(BF)
-            o_query[...] = nt(grad, w[...])
-            o_w[...] = lax.dot_general(
-                query[...], grad, (((0,), (0,)), ((), ())), preferred_element_type=F32
-            )
-        for o, start in ((o_vkv, R_VKV), (o_pkv, R_PKV)):
-            o[:, :WIDTH] = rows(start, WIDTH)
-            o[:, WIDTH:] = rows(start + WIDTH, WIDTH)
-        o_vwo[...] = rows(R_SWO, WIDTH).T
-        o_pwo[...] = rows(R_SWO + WIDTH, WIDTH).T
-        o_w1[...] = rows(R_W1, 32)
-        o_w2[...] = rows(R_W2, WIDTH)
-        for j in range(3):
-            o_qkv[:, WIDTH * j : WIDTH * j + WIDTH] = rows(R_Q + WIDTH * j, WIDTH)
-        o_ao[...] = rows(R_AO, WIDTH)
-        o_in[...] = rows(R_WIN, 512).T
-        o_out[...] = rows(R_WOUT, 512)
-        small = rows(R_LN, 16)
-        for j, o in enumerate((o_g1, o_b1, o_g2, o_b2)):
-            o[...] = small[j : j + 1]
-        sums = jnp.sum(small[R_STAT - R_LN : R_STAT - R_LN + 4], axis=1, keepdims=True)
-        o_rms[...] = jnp.broadcast_to(jnp.sqrt(sums / (sums[3:4] * WIDTH)), (4, WIDTH))
-
-
-def unpack_call(half, dother, proj, grad_vision, total, gfeat, vis_query, vis_wq, prop_query, prop_wq):
-    rows, channels = dother.shape[0], proj.shape[0]
-    steps = FEATURE_STEPS
+    core = lax.axis_index("mod")
+    slots, channels = vision.shape
+    piece = slots // FEATURE_STEPS
+    copies = []
+    for j in range(FEATURE_STEPS):
+        part = pl.ds(piece * j, piece)
+        vision[part] = nt(dother[part], proj[...]).astype(BF)
+        start = pl.multiple_of((1 - core) * slots + piece * j, 16)
+        copies.append(pltpu.make_async_copy(vision.at[part], o_vision.at[pl.ds(start, piece)], sems.at[j]))
+        copies[j].start()
+
+    n = total.shape[1]
+    halves = [total[j, :, :chunk].reshape(n * chunk, WIDTH) for j in range(2)]
+    half = R_END // 2
+
+    def rows(start, count):
+        source, at = halves[start // half], start % half
+        return source[at : at + count].astype(F32)
+
+    gsum = total[core, :, chunk:].reshape(n * (total.shape[2] - chunk), WIDTH).astype(F32)
+    for j in range(channels // WIDTH):
+        o_feat[WIDTH * j : WIDTH * j + WIDTH] = gsum[WIDTH * j : WIDTH * j + WIDTH].T
+    for o_query, o_w, query, w, start in (
+        (o_vq, o_vwq, vis_query, vis_wq, R_QV),
+        (o_pq, o_pwq, prop_query, prop_wq, R_QP),
+    ):
+        grad = rows(start, 16).astype(BF)
+        o_query[...] = nt(grad, w[...])
+        o_w[...] = lax.dot_general(
+            query[...], grad, (((0,), (0,)), ((), ())), preferred_element_type=F32
+        )
+    for o, start in ((o_vkv, R_VKV), (o_pkv, R_PKV)):
+        o[:, :WIDTH] = rows(start, WIDTH)
+        o[:, WIDTH:] = rows(start + WIDTH, WIDTH)
+    o_vwo[...] = rows(R_SWO, WIDTH).T
+    o_pwo[...] = rows(R_SWO + WIDTH, WIDTH).T
+    o_w1[...] = rows(R_W1, 32)
+    o_w2[...] = rows(R_W2, WIDTH)
+    for j in range(3):
+        o_qkv[:, WIDTH * j : WIDTH * j + WIDTH] = rows(R_Q + WIDTH * j, WIDTH)
+    o_ao[...] = rows(R_AO, WIDTH)
+    o_in[...] = rows(R_WIN, 512).T
+    o_out[...] = rows(R_WOUT, 512)
+    small = rows(R_LN, 16)
+    for j, o in enumerate((o_g1, o_b1, o_g2, o_b2)):
+        o[...] = small[j : j + 1]
+    sums = [jnp.sum(small[R_STAT - R_LN + j : R_STAT - R_LN + j + 1], axis=1, keepdims=True) for j in range(4)]
+    for j in range(3):
+        o_rms[j] = jnp.sum(jnp.sqrt(sums[j] / (sums[3] * WIDTH)))
+    for copy in copies:
+        copy.wait()
+
+
+def unpack_call(chunk, dother, proj, total, vis_query, vis_wq, prop_query, prop_wq, grad_vision):
+    slots, channels = dother.shape[0], proj.shape[0]
     shapes = [
-        (gfeat.shape[1], WIDTH), (16, WIDTH), (WIDTH, WIDTH), (WIDTH, 256), (WIDTH, WIDTH), (32, WIDTH),
+        (channels, WIDTH), (16, WIDTH), (WIDTH, WIDTH), (WIDTH, 256), (WIDTH, WIDTH), (32, WIDTH),
         (WIDTH, WIDTH), (16, WIDTH), (WIDTH, WIDTH), (WIDTH, 256), (WIDTH, WIDTH), (1, WIDTH), (1, WIDTH),
-        (WIDTH, 384), (WIDTH, WIDTH), (1, WIDTH), (1, WIDTH), (WIDTH, 512), (512, WIDTH), (4, WIDTH),
+        (WIDTH, 384), (WIDTH, WIDTH), (1, WIDTH), (1, WIDTH), (WIDTH, 512), (512, WIDTH), (3,),
     ]
-    args = (proj, grad_vision, total, gfeat, vis_query, vis_wq, prop_query, prop_wq)
+    vmem, hbm = pl.BlockSpec(memory_space=pltpu.VMEM), pl.BlockSpec(memory_space=pltpu.HBM)
     return pl.pallas_call(
-        unpack_kernel,
-        grid_spec=pltpu.PrefetchScalarGridSpec(
-            num_scalar_prefetch=1,
-            grid=(steps,),
-            in_specs=[pl.BlockSpec((rows // steps, WIDTH), lambda i, half: (i, 0)), whole(proj.shape)]
-            + [pl.BlockSpec(memory_space=pl.ANY)]
-            + [whole(a.shape) for a in args[2:]],
-            out_specs=[pl.BlockSpec((rows // steps, channels), lambda i, half: (half[0] * steps + i, 0))]
-            + [whole(s) for s in shapes],
-        ),
+        functools.partial(unpack_kernel, chunk),
+        in_specs=[vmem] * 7 + [hbm],
+        out_specs=[hbm] + [vmem] * (len(shapes) - 1) + [pl.BlockSpec(memory_space=pltpu.SMEM)],
         out_shape=[jax.ShapeDtypeStruct(grad_vision.shape, BF)] + [jax.ShapeDtypeStruct(s, F32) for s in shapes],
-        input_output_aliases={3: 0},
-        compiler_params=pltpu.CompilerParams(vmem_limit_bytes=VMEM_LIMIT),
+        scratch_shapes=[pltpu.VMEM((slots, channels), BF), pltpu.SemaphoreType.DMA((FEATURE_STEPS,))],
+        input_output_aliases={7: 0},
+        compiler_params=pltpu.CompilerParams(vmem_limit_bytes=20 * 2**20),
         name="unpack",
-    )(half, dother, *args)
+    )(dother, in_hbm(proj), total, *map(in_hbm, (vis_query, vis_wq, prop_query, prop_wq)), grad_vision)
 
 
 def finish_kernel(
-    n, chunk, gchunk, acc, gsum, dtok, feats, total, gout, dother,
-    fbuf, send_a, recv_a, send_b, recv_b, reduced, gathered, recv_d, send_g, recv_g, reduced_g, gathered_g,
-    sem_t, sem_f, sem_a, sem_b, sem_c, sem_d, sem_bg, sem_cg,
+    n, chunk, gchunk, acc, gsum, dtok, feats, total, dother,
+    fbuf, gbuf, own_a, recv_a, send_b, recv_b, send_g, recv_g, reduced,
+    sem_t, sem_f, sem_a, sem_b, sem_c, sem_d, sem_g,
 ):
     me, core = lax.axis_index("dp"), lax.axis_index("mod")
     mesh = pl.DeviceIdType.MESH
@@ -627,23 +655,29 @@
         return carry
 
     lax.fori_loop(1, n, greet, 0)
+    load_a = pltpu.make_async_copy(acc.at[rows(core, half)], own_a, sem_a.at[2])
+    load_a.start()
+    load_g = pltpu.make_async_copy(gsum, gbuf, sem_a.at[3])
+    load_g.start()
+    tokens, features = [], []
+    for j in range(FEATURE_STEPS):
+        part = pl.ds(piece * j, piece)
+        start_row = pl.multiple_of((1 - core) * slots + piece * j, 16)
+        features.append(pltpu.make_async_copy(feats.at[pl.ds(start_row, piece)], fbuf.at[part], sem_f.at[j]))
+        features[j].start()
     pl.semaphore_wait(barrier, n)
 
-    send_a[...] = acc[rows(1 - core, half)].astype(BF)
-    copy_a = remote(send_a, recv_a, sem_a.at[0], sem_a.at[1], partner)
+    copy_a = remote(acc.at[rows(1 - core, half)], recv_a, sem_a.at[0], sem_a.at[1], partner)
     copy_a.start()
-    tokens, features = [], []
     for j in range(FEATURE_STEPS):
         part = pl.ds(piece * j, piece)
         tokens.append(remote(dtok.at[part], dother.at[part], sem_t.at[0, j], sem_t.at[1, j], partner))
         tokens[j].start()
-        start_row = pl.multiple_of((1 - core) * slots + piece * j, 16)
-        features.append(pltpu.make_async_copy(feats.at[pl.ds(start_row, piece)], fbuf.at[part], sem_f.at[j]))
-        features[j].start()
     if half < n * chunk:
         send_b[half:] = jnp.zeros((n * chunk - half, WIDTH), BF)
+    load_a.wait()
     copy_a.wait()
-    send_b[:half] = (acc[rows(core, half)] + recv_a[...].astype(F32)).astype(BF)
+    send_b[:half] = (own_a[...].astype(F32) + recv_a[...].astype(F32)).astype(BF)
 
     def scatter(k):
         peer = lax.rem(me + k, n)
@@ -651,27 +685,19 @@
             send_b.at[rows(peer, chunk)], recv_b.at[k - 1], sem_b.at[0, k - 1], sem_b.at[1, k - 1], (peer, core)
         )
 
-    def gather(k):
-        peer = lax.rem(me + k, n)
-        return remote(
-            reduced, gathered.at[rows(me, chunk)], sem_c.at[0, k - 1], sem_c.at[1, k - 1], (peer, core)
-        )
-
     def scatter_g(k):
         peer = lax.rem(me + k, n)
         return remote(
-            send_g.at[rows(peer, gchunk)], recv_g.at[k - 1], sem_bg.at[0, k - 1], sem_bg.at[1, k - 1], (peer, core)
+            send_g.at[rows(peer, gchunk)], recv_g.at[k - 1], sem_g.at[0, k - 1], sem_g.at[1, k - 1], (peer, core)
         )
 
-    def gather_g(k):
+    def gather(k):
         peer = lax.rem(me + k, n)
-        return remote(
-            reduced_g, gathered_g.at[rows(me, gchunk)], sem_cg.at[0, k - 1], sem_cg.at[1, k - 1], (peer, core)
-        )
+        return remote(reduced, total.at[core, me], sem_c.at[0, k - 1], sem_c.at[1, k - 1], (peer, core))
 
     def forward(k):
-        owner = rows(lax.rem(me + n - k, n), chunk)
-        return remote(gathered.at[owner], recv_d.at[owner], sem_d.at[0, k], sem_d.at[1, k], partner)
+        piece_k = total.at[core, lax.rem(me + n - k, n), pl.ds(0, chunk)]
+        return remote(piece_k, piece_k, sem_d.at[0, k], sem_d.at[1, k], partner)
 
     def each(first, step):
         def body(k, carry):
@@ -682,7 +708,8 @@
 
     each(1, lambda k: scatter(k).start())
 
-    grad = gsum[...]
+    load_g.wait()
+    grad = gbuf[...]
     for j in range(FEATURE_STEPS):
         tokens[j].wait()
         features[j].wait()
@@ -695,32 +722,30 @@
         send_g[used:] = jnp.zeros((n * gchunk - used, WIDTH), BF)
     each(1, lambda k: scatter_g(k).start())
 
-    each(1, lambda k: scatter(k).wait())
-    value = send_b[rows(me, chunk)].astype(F32)
-    value = lax.fori_loop(0, n - 1, lambda k, v: v + recv_b[k].astype(F32), value)
-    reduced[...] = value.astype(BF)
-    gathered[rows(me, chunk)] = reduced[...]
+    def add(k, value):
+        scatter(k).wait()
+        return value + recv_b[k - 1].astype(F32)
+
+    def add_g(k, value):
+        scatter_g(k).wait()
+        return value + recv_g[k - 1].astype(F32)
+
+    reduced[:chunk] = lax.fori_loop(1, n, add, send_b[rows(me, chunk)].astype(F32)).astype(BF)
+    reduced[chunk:] = lax.fori_loop(1, n, add_g, send_g[rows(me, gchunk)].astype(F32)).astype(BF)
     each(1, lambda k: gather(k).start())
+    total[core, me] = reduced[...]
     forward(0).start()
-
-    each(1, lambda k: scatter_g(k).wait())
-    value = send_g[rows(me, gchunk)].astype(F32)
-    value = lax.fori_loop(0, n - 1, lambda k, v: v + recv_g[k].astype(F32), value)
-    reduced_g[...] = value.astype(BF)
-    gathered_g[rows(me, gchunk)] = reduced_g[...]
-    each(1, lambda k: gather_g(k).start())
 
     def pass_on(k):
         gather(k).wait()
         forward(k).start()
 
     each(1, pass_on)
-    total[rows(core, half)] = gathered[:half]
-    each(1, lambda k: gather_g(k).wait())
-    for j in range(channels // WIDTH):
-        gout[:, WIDTH * j : WIDTH * j + WIDTH] = gathered_g[WIDTH * j : WIDTH * j + WIDTH]
     each(0, lambda k: forward(k).wait())
-    total[rows(1 - core, half)] = recv_d[:half]
+
+
+def in_hbm(value):
+    return pltpu.with_memory_space_constraint(value, pltpu.HBM)
 
 
 def finish_call(acc, gsum, dtok, feats, n):
@@ -729,44 +754,40 @@
     chunk = 16 * -(-half // (16 * n))
     gchunk = 16 * -(-channels // (16 * n))
     vmem = pl.BlockSpec(memory_space=pltpu.VMEM)
-    hbm = pl.BlockSpec(memory_space=pl.ANY)
+    hbm = pl.BlockSpec(memory_space=pltpu.HBM)
     dma = pltpu.SemaphoreType.DMA
-    return pl.pallas_call(
+    total, dother = pl.pallas_call(
         functools.partial(finish_kernel, n, chunk, gchunk),
         out_shape=(
-            jax.ShapeDtypeStruct(acc.shape, BF),
-            jax.ShapeDtypeStruct(gsum.shape, BF),
+            jax.ShapeDtypeStruct((2, n, chunk + gchunk, WIDTH), BF),
             jax.ShapeDtypeStruct(dtok.shape, BF),
         ),
-        in_specs=[vmem, vmem, hbm, hbm],
-        out_specs=(vmem, vmem, vmem),
+        in_specs=[hbm, hbm, hbm, hbm],
+        out_specs=(vmem, vmem),
         scratch_shapes=[
             pltpu.VMEM((slots, channels), BF),
+            pltpu.VMEM(gsum.shape, F32),
             pltpu.VMEM((half, WIDTH), BF),
             pltpu.VMEM((half, WIDTH), BF),
             pltpu.VMEM((n * chunk, WIDTH), BF),
             pltpu.VMEM((n - 1, chunk, WIDTH), BF),
-            pltpu.VMEM((chunk, WIDTH), BF),
-            pltpu.VMEM((n * chunk, WIDTH), BF),
-            pltpu.VMEM((n * chunk, WIDTH), BF),
             pltpu.VMEM((n * gchunk, WIDTH), BF),
             pltpu.VMEM((n - 1, gchunk, WIDTH), BF),
-            pltpu.VMEM((gchunk, WIDTH), BF),
-            pltpu.VMEM((n * gchunk, WIDTH), BF),
+            pltpu.VMEM((chunk + gchunk, WIDTH), BF),
             dma((2, FEATURE_STEPS)),
             dma((FEATURE_STEPS,)),
-            dma((2,)),
+            dma((4,)),
             dma((2, n - 1)),
             dma((2, n - 1)),
             dma((2, n)),
             dma((2, n - 1)),
-            dma((2, n - 1)),
         ],
         compiler_params=pltpu.CompilerParams(
-            collective_id=0, has_side_effects=True, vmem_limit_bytes=VMEM_LIMIT
+            collective_id=0, has_side_effects=True, vmem_limit_bytes=24 * 2**20
         ),
         name="finish",
-    )(acc, gsum, dtok, feats)
+    )(in_hbm(acc), in_hbm(gsum), in_hbm(dtok), in_hbm(feats))
+    return chunk, total, dother
 
 
 def per_device(
@@ -786,23 +807,22 @@
         vis_query, vis_wq, vis_kv, vis_wo, prop_w1, prop_w2, prop_query, prop_wq, prop_kv, prop_wo,
         ln, qkv_weight, attn_out, mlp_in, mlp_out,
     )
-    frames = proprio.reshape(-1, proprio.shape[3])
+    frames = jnp.transpose(proprio, (1, 2, 3, 0)).reshape(-1, proprio.shape[0])
     grid_sizes = jnp.transpose(vision_grid, (1, 2, 0)).reshape(4, -1)
     output, grad_vision, dtok, dframes, acc, gfeat = block_call(
         own, grid_sizes, feats, received, frames, aux, out_cot.reshape(-1, WIDTH), feat_proj, weights
     )
-    total, gfeat, dother = finish_call(acc, gfeat, dtok, feats, lax.axis_size("dp"))
+    chunk, total, dother = finish_call(acc, gfeat, dtok, feats, lax.axis_size("dp"))
     grad_vision, *outs = unpack_call(
-        other, dother, feat_proj, grad_vision, total, gfeat, vis_query, vis_wq, prop_query, prop_wq
+        chunk, dother, feat_proj, total, vis_query, vis_wq, prop_query, prop_wq, grad_vision
     )
     vectors = {11, 12, 15, 16}
     outs = [o.reshape(WIDTH) if j in vectors else o for j, o in enumerate(outs)]
     return (
         output.reshape(out_cot.shape),
         grad_vision.reshape(vision_feats.shape),
-        dframes.reshape(proprio.shape),
-        *outs[:-1],
-        outs[-1][:3, 0],
+        jnp.transpose(dframes.reshape(proprio.shape[1:] + proprio.shape[:1]), (3, 0, 1, 2)),
+        *outs,
     )
 
 

time: 118 us -> 106 us (0.90)
  Pallas kernels: 106 us -> 98.4 us
  local copies, waits for them, and re-layouts: 7.82 us -> 2.73 us
  waiting for transfers between devices: 0.39 us -> 1.91 us
    pallas_call x1, Pallas kernels: 63.4 us -> 59 us  [block_call(): pl.pallas_call(block_kernel, grid_spec=pltpu.PrefetchScalarGridSpec(num_s...]
    unnamed x20 -> x16, local copies, waits for them, and re-layouts: 5.15 us -> 1.36 us
    pallas_call x1, Pallas kernels: 31.6 us -> 29.5 us  [finish_call(): pl.pallas_call(functools.partial(finish_kernel, n, chunk, gchunk), out_sh...]
    ppermute x1, waiting for transfers between devices: 0.39 us -> 1.91 us  [per_device(): received = lax.ppermute(sent, 'mod', swap)]
    slice x1 -> x0, local copies, waits for them, and re-layouts: 1.3 us -> none  [per_device(): outs[-1][:3, 0]]
  transfers between devices with their start and end apart: 1 -> 1, of which waited for: 1 -> 1; matrix products, arithmetic and copies ran while one was open for 3% -> 2% of each run, Pallas kernels for 0% -> 0%
where the time goes in v5:
time: 106 us; the launch traced here: 105 us
  Pallas kernels  98.4 us (93%)
  local copies, waits for them, and re-layouts  2.73 us (3%)
  waiting for transfers between devices  1.91 us (2%)
    pallas_call x1, Pallas kernels, block_call(): pl.pallas_call(block_kernel, grid_spec=pltpu.PrefetchScalarGridSpec(num_s...  59 us
    pallas_call x1, Pallas kernels, finish_call(): pl.pallas_call(functools.partial(finish_kernel, n, chunk, gchunk), out_sh...  29.5 us
    pallas_call x1, Pallas kernels, project_call(): pl.pallas_call(project_kernel, grid_spec=pltpu.PrefetchScalarGridSpec(num...  5.02 us
    pallas_call x1, Pallas kernels, unpack_call(): pl.pallas_call(functools.partial(unpack_kernel, chunk), in_specs=[vmem] *...  4.83 us
  transfers between devices with their start and end apart: 1, of which 1 were waited for; matrix products, arithmetic and copies ran while one was open for 2% of the time, Pallas kernels for 0%

profile of v5, /device:TPU:25, one launch (start us, length us, event | category | flops | bytes accessed | tf_op | source)
XLA Modules:
  0.0 105.3 jit_solution(10921877505847333194)
XLA Ops:
  0.7 0.0 copy-start.7
  0.7 0.0 copy-start.1
  0.7 0.0 copy-start.2
  0.7 0.0 copy-start.3
  0.7 0.0 copy-start.4
  0.7 0.0 copy-start.5
  0.7 0.0 copy-start.6
  0.7 5.0 %project.1 = bf16[8192,128]{1,0:T(8,128)(2,1)} custom-call(s32[1]{0:T(128)} %bitcast.4.half, bf16[16384,256]{1,0:T(8,128)(2,1)} %bitcast.24, bf16[256,128]{1,0:T(8,128)(2,1)} %proj.5), custom_call_target="tpu_custom_call" | custom-call | flops 536870912 | bytes 6291456 | tf_op jit(solution)/shard_map/project/pallas_call | solution.py:532
  5.8 0.7 collective-permute-start
  6.4 0.0 copy-done.7
  6.4 0.1 broadcast_in_dim.28
  6.5 0.1 broadcast_in_dim.29
  6.6 0.1 broadcast_in_dim.30
  6.7 0.1 convert_element_type.25
  6.8 0.1 copy.51
  6.9 0.1 select_n.29
  7.1 0.8 concatenate.7.aux
  7.9 0.0 copy-done.6
  7.9 0.6 maximum_convert_fusion.ln
  8.5 1.9 %collective-permute-done.pr = bf16[8192,128]{1,0:T(8,128)(2,1)S(1)} collective-permute-done((bf16[8192,128]{1,0:T(8,128)(2,1)}, bf16[8192,128]{1,0:T(8,128)(2,1)S(1)}, u32[]{:S(2)}, u32[]{:S(2)}) %collective-permute-start) | collective-permute-done | bytes 2097184 | tf_op jit(solution)/shard_map/ppermute | solution.py:803
  10.4 1.3 %copy-done = bf16[8192,128]{1,0:T(8,128)(2,1)} copy-done((bf16[8192,128]{1,0:T(8,128)(2,1)}, bf16[8192,128]{1,0:T(8,128)(2,1)S(1)}, u32[]{:S(2)}) %copy-start) | copy-done | bytes 2097176
  11.8 59.0 %stems_trunk.1 = (bf16[4096,128]{1,0:T(8,128)(2,1)}, bf16[16384,256]{1,0:T(8,128)(2,1)}, bf16[8192,128]{1,0:T(8,128)(2,1)}, bf16[1024,64]{1,0:T(8,128)(2,1)}, bf...) custom-call(s32[1]{0:T(128)} %bitcast.half, s32[4,64]{1,0:T(4,128)} %bitcast.31, bf16[16384,256]{1,0:T(8,128)(2,1)} %bitcast.25, ...), custom_call_target="tpu_custom_call" | custom-call | tf_op jit(solution)/shard_map/stems_trunk/pallas_call | solution.py:495
  70.7 29.5 %finish.1 = (bf16[2,16,96,128]{3,2,1,0:T(8,128)(2,1)S(1)}, bf16[8192,128]{1,0:T(8,128)(2,1)S(1)}) custom-call(bf16[2560,128]{1,0:T(8,128)(2,1)} %get-tuple-element.53.acc, f32[128,256]{1,0:T(8,128)} %get-tuple-element.54.gsum, bf16[8192,128]{1,0:T(8,128)(2,1)} %get-tuple-element.55.dtok, bf16[16384,256]{1,0:T(8,128)(2,1)} %bitcast.26), custom_call_target="tpu_custom_call" | custom-call | tf_op jit(solution)/shard_map/finish/pallas_call | solution.py:759
  100.3 4.8 %unpack.1 = (bf16[16384,256]{1,0:T(8,128)(2,1)}, f32[256,128]{1,0:T(8,128)}, f32[16,128]{1,0:T(8,128)}, f32[128,128]{1,0:T(8,128)}, f32[128,256]{1,0:T(8,128)}, ...) custom-call(bf16[8192,128]{1,0:T(8,128)(2,1)S(1)} %get-tuple-element, ...), custom_call_target="tpu_custom_call", output_to_operand_aliasing={{0}: (7, {})} | custom-call | tf_op jit(solution)/shard_map/unpack/pallas_call | solution.py:618
  (12 shorter events, 0.1 us)
Async XLA Ops:
  0.7 5.8 %copy-start.7 = (s32[64]{0:T(128)S(1)}, s32[64]{0:T(128)}, u32[]{:S(2)}) copy-start(s32[64]{0:T(128)} %param.31) | copy-start | bytes 772
  0.7 6.0 %copy-start.1 = (s32[64,64]{1,0:T(8,128)S(1)}, s32[64,64]{1,0:T(8,128)}, u32[]{:S(2)}) copy-start(s32[64,64]{1,0:T(8,128)} %param.30) | copy-start | bytes 49156
  0.7 6.1 %copy-start.2 = (s32[64,2,16]{0,2,1:T(8,128)S(1)}, s32[64,2,16]{0,2,1:T(8,128)}, u32[]{:S(2)}) copy-start(s32[64,2,16]{0,2,1:T(8,128)} %param.29) | copy-start | bytes 24580
  0.7 7.2 %copy-start.3 = (bf16[128]{0:T(256)(128)(2,1)S(1)}, bf16[128]{0:T(256)(128)(2,1)}, u32[]{:S(2)}) copy-start(bf16[128]{0:T(256)(128)(2,1)} %param.49) | copy-start | bytes 772
  0.7 7.2 %copy-start.4 = (bf16[128]{0:T(256)(128)(2,1)S(1)}, bf16[128]{0:T(256)(128)(2,1)}, u32[]{:S(2)}) copy-start(bf16[128]{0:T(256)(128)(2,1)} %param.48) | copy-start | bytes 772
  0.7 7.2 %copy-start.5 = (bf16[128]{0:T(256)(128)(2,1)S(1)}, bf16[128]{0:T(256)(128)(2,1)}, u32[]{:S(2)}) copy-start(bf16[128]{0:T(256)(128)(2,1)} %param.45) | copy-start | bytes 772
  0.7 7.2 %copy-start.6 = (bf16[128]{0:T(256)(128)(2,1)S(1)}, bf16[128]{0:T(256)(128)(2,1)}, u32[]{:S(2)}) copy-start(bf16[128]{0:T(256)(128)(2,1)} %param.44) | copy-start | bytes 772
  5.8 4.7 %collective-permute-start = (bf16[8192,128]{1,0:T(8,128)(2,1)}, bf16[8192,128]{1,0:T(8,128)(2,1)S(1)}, u32[]{:S(2)}, u32[]{:S(2)}) collective-permute-start(bf16[8192,128]{1,0:T(8,128)(2,1)} %project.1), channel_id=1, source_target_pairs={{0,1},{1,0},{2,3},{3,2},{4,5},{5,4},{6,7},{7,6},{8,9},{9,8},{10,11... | collective-permute-start | bytes 6291464 | tf_op jit(solution)/shard_map/ppermute | solution.py:803
  10.4 1.3 %copy-start = (bf16[8192,128]{1,0:T(8,128)(2,1)}, bf16[8192,128]{1,0:T(8,128)(2,1)S(1)}, u32[]{:S(2)}) copy-start(bf16[8192,128]{1,0:T(8,128)(2,1)S(1)} %collective-permute-done.pr) | copy-start | bytes 6291460

commit v6 on v5

--- a/solution.py
+++ b/solution.py
@@ -170,13 +170,14 @@
 
 
 def block_kernel(
-    half, grid_ref, feats, pr, frames, aux, cot, proj,
+    half, grid_ref, feats, pr, frames, frame_mask, token_valid, mix_weight, cot, proj,
     vis_query, vis_wq, vis_kv, vis_wo, prop_w1, prop_w2, prop_query, prop_wq, prop_kv, prop_wo,
-    ln, qkv_w, attn_out, mlp_in, mlp_out,
+    ln1_gain, ln1_bias, ln2_gain, ln2_bias, qkv_w, attn_out, mlp_in, mlp_out,
     out, grad_feats, dtok_ref, dframes, acc_out, gsum,
     masks_ref, qv_ref, qp_ref, wqkv_t, ao_t, win_t, wout_t, stem_t, ln_ref,
-    gv_ref, gp_ref, lnacc, stat, acc, fr_ref, df_ref,
+    gv_ref, gp_ref, lnacc, stat, acc, fr_ref, df_ref, aux_ref, turn_ref,
 ):
+    blocks = token_valid.shape[0] // 4
     step = pl.program_id(0)
 
     @pl.when(step == 0)
@@ -195,8 +196,22 @@
         wout_t[...] = mlp_out[...].T
         stem_t[:, :WIDTH] = vis_wo[...].T
         stem_t[:, WIDTH:] = prop_wo[...].T
-        for j in range(4):
-            ln_ref[j] = jnp.broadcast_to(ln[j : j + 1, :], (WIDTH, WIDTH)).T
+        for j, vector in enumerate((ln1_gain, ln1_bias, ln2_gain, ln2_bias)):
+            ln_ref[j] = jnp.broadcast_to(vector[...].astype(F32), (WIDTH, WIDTH)).T
+
+        def by_block(ref):
+            return cat([ref[pl.ds(j, blocks, stride=4)].astype(F32) for j in range(4)], 1)
+
+        valid = by_block(token_valid)
+        turn_ref[...] = jnp.broadcast_to(mix_weight[...].astype(F32), turn_ref.shape).T
+        mix = by_block(turn_ref)
+        turn_ref[:, : frame_mask.shape[0]] = frame_mask[...].astype(F32).T
+        frame_keep = cat([turn_ref[pl.ds(j, blocks, stride=4)][:, : frame_mask.shape[0]] for j in range(4)], 1)
+        values = (valid, mix, jnp.where(valid > 0, 0.0, NEG), jnp.where(cat([frame_keep] * 2, 1) > 0, 0.0, NEG))
+        for i in range(blocks):
+            for j, value in enumerate(values):
+                aux_ref[i, j : j + 1] = value[i : i + 1]
+
         for j in range(frames.shape[0] // PROP):
             block = frames[PROP * j : PROP * j + PROP].astype(F32).T
             fr_ref[pl.ds(j, block.shape[0], stride=frames.shape[0] // PROP)] = block
@@ -217,6 +232,7 @@
 
 
     def chain(g):
+        block = step * CHAINS + g
         slots = slice(512 * g, 512 * g + 512)
         kept = nn(feats[slots], proj[...]).astype(BF)
         tok = (kept.astype(F32) + pr[slots].astype(F32)).astype(BF)
@@ -255,7 +271,7 @@
         ptok = nn(hidden, prop_w2[...]).astype(BF)
         pkv = nn(ptok, prop_kv[...]).astype(BF)
         pk, pv = pkv[:, :WIDTH], pkv[:, WIDTH:]
-        column = jnp.broadcast_to(aux[g, 3:4, :WIDTH], (WIDTH, WIDTH)).T
+        column = jnp.broadcast_to(aux_ref[block, 3:4, :WIDTH], (WIDTH, WIDTH)).T
         parts = lambda v: [v[HEAD * st : HEAD * st + HEAD] for st in range(8)]
         pbias = pair_up(parts(column))
         pk2, pv2 = pair_up(parts(pk)), pair_up(parts(pv))
@@ -290,7 +306,7 @@
         weights, weights_b, query_bd = [], [], []
         tbias = []
         for p in range(2):
-            column = jnp.broadcast_to(aux[g, 2:3, 128 * p : 128 * p + 128], (WIDTH, WIDTH)).T
+            column = jnp.broadcast_to(aux_ref[block, 2:3, 128 * p : 128 * p + 128], (WIDTH, WIDTH)).T
             tbias.append(jnp.where(first, column[:64], column[64:]))
         tbias = cat(tbias, 1)[None]
         for group in range(2):
@@ -312,7 +328,7 @@
         n2 = (hat2 * g2 + b2).astype(BF)
         yield
         c = math.sqrt(2.0 / math.pi)
-        seed = cot[256 * g : 256 * g + 256].T.astype(F32) * aux[g, 1:2, :]
+        seed = cot[256 * g : 256 * g + 256].T.astype(F32) * aux_ref[block, 1:2, :]
         dmlp = seed.astype(BF)
         mlp, dn2, act_all, dup_all = 0.0, 0.0, [], []
         for j in range(512 // FF_PART):
@@ -333,7 +349,7 @@
             yield
         final = middle + mlp
         out[256 * g : 256 * g + 256] = final.astype(BF).T
-        valid = aux[g, 0:1, :]
+        valid = aux_ref[block, 0:1, :]
         for j, value in enumerate((final, branch, mlp)):
             stat[j : j + 1, :] += jnp.sum(value * value, axis=0, keepdims=True) * valid
         stat[3:4, :] += valid
@@ -445,8 +461,9 @@
     return pl.BlockSpec(shape, lambda i, *_: (0,) * len(shape))
 
 
-def block_call(half, grid_sizes, feats, received, frames, aux, cot, proj, weights):
-    steps = aux.shape[0] // CHAINS
+def block_call(half, grid_sizes, feats, received, frames, frame_mask, token_valid, mix_weight, cot, proj, weights):
+    samples, seq = token_valid.shape
+    steps = samples // (4 * CHAINS)
     channels = feats.shape[1]
     row = lambda i, *_: (i, 0)
     own = lambda i, half, _: (half[0] * steps + i, 0)
@@ -454,7 +471,9 @@
         pl.BlockSpec((512 * CHAINS, channels), own),
         pl.BlockSpec((512 * CHAINS, WIDTH), row),
         whole(frames.shape),
-        pl.BlockSpec((CHAINS, 8, 256), lambda i, *_: (i, 0, 0)),
+        whole(frame_mask.shape),
+        whole(token_valid.shape),
+        whole(mix_weight.shape),
         pl.BlockSpec((256 * CHAINS, WIDTH), row),
         whole(proj.shape),
     ] + [whole(w.shape) for w in weights]
@@ -491,6 +510,8 @@
         pltpu.VMEM((R_END, WIDTH), F32),
         pltpu.VMEM((frames.shape[0] // PROP * frames.shape[1], PROP), F32),
         pltpu.VMEM((frames.shape[0] // PROP * frames.shape[1], PROP), F32),
+        pltpu.VMEM((samples // 4, 8, 4 * seq), F32),
+        pltpu.VMEM((samples, seq), F32),
     ]
     return pl.pallas_call(
         block_kernel,
@@ -504,66 +525,72 @@
         out_shape=out_shape,
         compiler_params=pltpu.CompilerParams(vmem_limit_bytes=VMEM_LIMIT),
         name="stems_trunk",
-    )(half, grid_sizes, feats, received, frames, aux, cot, proj, *weights)
-
-
-def make_aux(proprio_mask, token_valid, mix_weight):
-    samples, seq = token_valid.shape
-    steps = samples // 4
-    valid = token_valid.reshape(steps, 1, 4 * seq).astype(F32)
-    mix = jnp.broadcast_to(mix_weight.astype(F32)[:, None], (samples, seq)).reshape(steps, 1, 4 * seq)
-    vbias = jnp.where(valid > 0, 0.0, NEG)
-    pbias = jnp.where(proprio_mask.reshape(steps, 1, -1) > 0, 0.0, NEG)
-    pbias = jnp.concatenate([pbias, jnp.zeros_like(pbias)], axis=2)
-    rest = jnp.zeros((steps, 4, 4 * seq), F32)
-    return jnp.concatenate([valid, mix, vbias, pbias, rest], axis=1)
-
-PROJECT_STEPS = 4
+    )(half, grid_sizes, feats, received, frames, frame_mask, token_valid, mix_weight, cot, proj, *weights)
+
+PROJECT_STEPS = 8
 FEATURE_STEPS = 4
 
 
-def project_kernel(half, feats, proj, out):
-    out[...] = nn(feats[...], proj[...]).astype(BF)
-
-
-def project_call(half, feats, proj):
-    rows, channels = feats.shape[0] // 2, feats.shape[1]
-    steps = PROJECT_STEPS
+def project_kernel(feats, proj, out, fbuf, stage, sem_f, sem_s):
+    me, core = lax.axis_index("dp"), lax.axis_index("mod")
+    mesh = pl.DeviceIdType.MESH
+    partner = (me, 1 - core)
+    slots = fbuf.shape[0]
+    piece = slots // PROJECT_STEPS
+    loads, sends = [], []
+    for j in range(PROJECT_STEPS):
+        start = pl.multiple_of((1 - core) * slots + piece * j, 16)
+        loads.append(pltpu.make_async_copy(feats.at[pl.ds(start, piece)], fbuf.at[pl.ds(piece * j, piece)], sem_f.at[j]))
+        loads[j].start()
+    barrier = pltpu.get_barrier_semaphore()
+    pl.semaphore_signal(barrier, inc=1, device_id=partner, device_id_type=mesh)
+    pl.semaphore_wait(barrier, 1)
+    for j in range(PROJECT_STEPS):
+        part = pl.ds(piece * j, piece)
+        loads[j].wait()
+        stage[part] = nn(fbuf[part], proj[...]).astype(BF)
+        sends.append(
+            pltpu.make_async_remote_copy(
+                src_ref=stage.at[part], dst_ref=out.at[part], send_sem=sem_s.at[0, j], recv_sem=sem_s.at[1, j],
+                device_id=partner, device_id_type=mesh,
+            )
+        )
+        sends[j].start()
+    for j in range(PROJECT_STEPS):
+        sends[j].wait()
+
+
+def project_call(feats, proj):
+    slots, channels = feats.shape[0] // 2, feats.shape[1]
+    hbm = pl.BlockSpec(memory_space=pl.ANY)
     return pl.pallas_call(
         project_kernel,
-        grid_spec=pltpu.PrefetchScalarGridSpec(
-            num_scalar_prefetch=1,
-            grid=(steps,),
-            in_specs=[
-                pl.BlockSpec((rows // steps, channels), lambda i, half: (half[0] * steps + i, 0)),
-                whole(proj.shape),
-            ],
-            out_specs=pl.BlockSpec((rows // steps, WIDTH), lambda i, half: (i, 0)),
-        ),
-        out_shape=jax.ShapeDtypeStruct((rows, WIDTH), BF),
-        compiler_params=pltpu.CompilerParams(vmem_limit_bytes=VMEM_LIMIT),
-        cost_estimate=pl.CostEstimate(
-            flops=2 * rows * channels * WIDTH, bytes_accessed=2 * rows * (channels + WIDTH), transcendentals=0
+        in_specs=[hbm, pl.BlockSpec(memory_space=pltpu.VMEM)],
+        out_specs=hbm,
+        out_shape=jax.ShapeDtypeStruct((slots, WIDTH), BF),
+        scratch_shapes=[
+            pltpu.VMEM((slots, channels), BF),
+            pltpu.VMEM((slots, WIDTH), BF),
+            pltpu.SemaphoreType.DMA((PROJECT_STEPS,)),
+            pltpu.SemaphoreType.DMA((2, PROJECT_STEPS)),
+        ],
+        compiler_params=pltpu.CompilerParams(
+            collective_id=1, has_side_effects=True, vmem_limit_bytes=VMEM_LIMIT
         ),
         name="project",
-    )(half, feats, proj)
+    )(feats, proj)
 
 
 def unpack_kernel(
-    chunk, dother, proj, total, vis_query, vis_wq, prop_query, prop_wq, before,
+    chunk, vision, total, vis_query, vis_wq, prop_query, prop_wq, before,
     o_vision, o_feat, o_vq, o_vwq, o_vkv, o_vwo, o_w1, o_w2, o_pq, o_pwq, o_pkv, o_pwo,
-    o_g1, o_b1, o_qkv, o_ao, o_g2, o_b2, o_in, o_out, o_rms, vision, sems,
+    o_g1, o_b1, o_qkv, o_ao, o_g2, o_b2, o_in, o_out, o_rms, sem,
 ):
     core = lax.axis_index("mod")
     slots, channels = vision.shape
-    piece = slots // FEATURE_STEPS
-    copies = []
-    for j in range(FEATURE_STEPS):
-        part = pl.ds(piece * j, piece)
-        vision[part] = nt(dother[part], proj[...]).astype(BF)
-        start = pl.multiple_of((1 - core) * slots + piece * j, 16)
-        copies.append(pltpu.make_async_copy(vision.at[part], o_vision.at[pl.ds(start, piece)], sems.at[j]))
-        copies[j].start()
+    start = pl.multiple_of((1 - core) * slots, 16)
+    copy = pltpu.make_async_copy(vision, o_vision.at[pl.ds(start, slots)], sem)
+    copy.start()
 
     n = total.shape[1]
     halves = [total[j, :, :chunk].reshape(n * chunk, WIDTH) for j in range(2)]
@@ -603,12 +630,11 @@
     sums = [jnp.sum(small[R_STAT - R_LN + j : R_STAT - R_LN + j + 1], axis=1, keepdims=True) for j in range(4)]
     for j in range(3):
         o_rms[j] = jnp.sum(jnp.sqrt(sums[j] / (sums[3] * WIDTH)))
-    for copy in copies:
-        copy.wait()
-
-
-def unpack_call(chunk, dother, proj, total, vis_query, vis_wq, prop_query, prop_wq, grad_vision):
-    slots, channels = dother.shape[0], proj.shape[0]
+    copy.wait()
+
+
+def unpack_call(chunk, vision, total, vis_query, vis_wq, prop_query, prop_wq, grad_vision):
+    channels = vision.shape[1]
     shapes = [
         (channels, WIDTH), (16, WIDTH), (WIDTH, WIDTH), (WIDTH, 256), (WIDTH, WIDTH), (32, WIDTH),
         (WIDTH, WIDTH), (16, WIDTH), (WIDTH, WIDTH), (WIDTH, 256), (WIDTH, WIDTH), (1, WIDTH), (1, WIDTH),
@@ -617,19 +643,19 @@
     vmem, hbm = pl.BlockSpec(memory_space=pltpu.VMEM), pl.BlockSpec(memory_space=pltpu.HBM)
     return pl.pallas_call(
         functools.partial(unpack_kernel, chunk),
-        in_specs=[vmem] * 7 + [hbm],
+        in_specs=[vmem] * 6 + [hbm],
         out_specs=[hbm] + [vmem] * (len(shapes) - 1) + [pl.BlockSpec(memory_space=pltpu.SMEM)],
         out_shape=[jax.ShapeDtypeStruct(grad_vision.shape, BF)] + [jax.ShapeDtypeStruct(s, F32) for s in shapes],
-        scratch_shapes=[pltpu.VMEM((slots, channels), BF), pltpu.SemaphoreType.DMA((FEATURE_STEPS,))],
-        input_output_aliases={7: 0},
+        scratch_shapes=[pltpu.SemaphoreType.DMA],
+        input_output_aliases={6: 0},
         compiler_params=pltpu.CompilerParams(vmem_limit_bytes=20 * 2**20),
         name="unpack",
-    )(dother, in_hbm(proj), total, *map(in_hbm, (vis_query, vis_wq, prop_query, prop_wq)), grad_vision)
+    )(vision, total, *map(in_hbm, (vis_query, vis_wq, prop_query, prop_wq)), grad_vision)
 
 
 def finish_kernel(
-    n, chunk, gchunk, acc, gsum, dtok, feats, total, dother,
-    fbuf, gbuf, own_a, recv_a, send_b, recv_b, send_g, recv_g, reduced,
+    n, chunk, gchunk, acc, gsum, dtok, feats, proj, total, vision,
+    dother, pbuf, fbuf, gbuf, own_a, recv_a, send_b, recv_b, send_g, recv_g, reduced,
     sem_t, sem_f, sem_a, sem_b, sem_c, sem_d, sem_g,
 ):
     me, core = lax.axis_index("dp"), lax.axis_index("mod")
@@ -659,6 +685,8 @@
     load_a.start()
     load_g = pltpu.make_async_copy(gsum, gbuf, sem_a.at[3])
     load_g.start()
+    load_p = pltpu.make_async_copy(proj, pbuf, sem_a.at[4])
+    load_p.start()
     tokens, features = [], []
     for j in range(FEATURE_STEPS):
         part = pl.ds(piece * j, piece)
@@ -721,6 +749,10 @@
     if used < n * gchunk:
         send_g[used:] = jnp.zeros((n * gchunk - used, WIDTH), BF)
     each(1, lambda k: scatter_g(k).start())
+    load_p.wait()
+    for j in range(FEATURE_STEPS):
+        part = slice(piece * j, piece * j + piece)
+        vision[part] = nt(dother[part], pbuf[...]).astype(BF)
 
     def add(k, value):
         scatter(k).wait()
@@ -748,7 +780,7 @@
     return pltpu.with_memory_space_constraint(value, pltpu.HBM)
 
 
-def finish_call(acc, gsum, dtok, feats, n):
+def finish_call(acc, gsum, dtok, feats, proj, n):
     slots, channels = dtok.shape[0], feats.shape[1]
     half = R_END // 2
     chunk = 16 * -(-half // (16 * n))
@@ -756,15 +788,17 @@
     vmem = pl.BlockSpec(memory_space=pltpu.VMEM)
     hbm = pl.BlockSpec(memory_space=pltpu.HBM)
     dma = pltpu.SemaphoreType.DMA
-    total, dother = pl.pallas_call(
+    total, vision = pl.pallas_call(
         functools.partial(finish_kernel, n, chunk, gchunk),
         out_shape=(
             jax.ShapeDtypeStruct((2, n, chunk + gchunk, WIDTH), BF),
-            jax.ShapeDtypeStruct(dtok.shape, BF),
+            jax.ShapeDtypeStruct((slots, channels), BF),
         ),
-        in_specs=[hbm, hbm, hbm, hbm],
+        in_specs=[hbm] * 5,
         out_specs=(vmem, vmem),
         scratch_shapes=[
+            pltpu.VMEM(dtok.shape, BF),
+            pltpu.VMEM(proj.shape, BF),
             pltpu.VMEM((slots, channels), BF),
             pltpu.VMEM(gsum.shape, F32),
             pltpu.VMEM((half, WIDTH), BF),
@@ -776,18 +810,18 @@
             pltpu.VMEM((chunk + gchunk, WIDTH), BF),
             dma((2, FEATURE_STEPS)),
             dma((FEATURE_STEPS,)),
-            dma((4,)),
+            dma((5,)),
             dma((2, n - 1)),
             dma((2, n - 1)),
             dma((2, n)),
             dma((2, n - 1)),
         ],
         compiler_params=pltpu.CompilerParams(
-            collective_id=0, has_side_effects=True, vmem_limit_bytes=24 * 2**20
+            collective_id=0, has_side_effects=True, vmem_limit_bytes=28 * 2**20
         ),
         name="finish",
-    )(in_hbm(acc), in_hbm(gsum), in_hbm(dtok), in_hbm(feats))
-    return chunk, total, dother
+    )(*map(in_hbm, (acc, gsum, dtok, feats, proj)))
+    return chunk, total, vision
 
 
 def per_device(
@@ -796,25 +830,23 @@
     ln1_gain, ln1_bias, qkv_weight, attn_out, ln2_gain, ln2_bias, mlp_in, mlp_out,
 ):
     me = lax.axis_index("mod").astype(jnp.int32)
-    own, other = me.reshape(1), (1 - me).reshape(1)
-    swap = [(0, 1), (1, 0)]
+    own = me.reshape(1)
     feats = vision_feats.reshape(-1, vision_feats.shape[3])
-    sent = project_call(other, feats, feat_proj)
-    received = lax.ppermute(sent, "mod", swap)
-    aux = make_aux(proprio_mask, token_valid, mix_weight)
-    ln = jnp.stack([ln1_gain, ln1_bias, ln2_gain, ln2_bias]).astype(F32)
+    received = project_call(feats, feat_proj)
     weights = (
         vis_query, vis_wq, vis_kv, vis_wo, prop_w1, prop_w2, prop_query, prop_wq, prop_kv, prop_wo,
-        ln, qkv_weight, attn_out, mlp_in, mlp_out,
+        *(v.reshape(1, -1) for v in (ln1_gain, ln1_bias, ln2_gain, ln2_bias)), qkv_weight, attn_out, mlp_in, mlp_out,
     )
     frames = jnp.transpose(proprio, (1, 2, 3, 0)).reshape(-1, proprio.shape[0])
+    frame_mask = jnp.transpose(proprio_mask, (1, 2, 0)).reshape(-1, proprio_mask.shape[0])
     grid_sizes = jnp.transpose(vision_grid, (1, 2, 0)).reshape(4, -1)
     output, grad_vision, dtok, dframes, acc, gfeat = block_call(
-        own, grid_sizes, feats, received, frames, aux, out_cot.reshape(-1, WIDTH), feat_proj, weights
+        own, grid_sizes, feats, received, frames, frame_mask, token_valid, mix_weight.reshape(1, -1),
+        out_cot.reshape(-1, WIDTH), feat_proj, weights,
     )
-    chunk, total, dother = finish_call(acc, gfeat, dtok, feats, lax.axis_size("dp"))
+    chunk, total, vision = finish_call(acc, gfeat, dtok, feats, feat_proj, lax.axis_size("dp"))
     grad_vision, *outs = unpack_call(
-        chunk, dother, feat_proj, total, vis_query, vis_wq, prop_query, prop_wq, grad_vision
+        chunk, vision, total, vis_query, vis_wq, prop_query, prop_wq, grad_vision
     )
     vectors = {11, 12, 15, 16}
     outs = [o.reshape(WIDTH) if j in vectors else o for j, o in enumerate(outs)]

time: 106 us -> 102 us (0.962)
  local copies, waits for them, and re-layouts: 2.73 us -> 0 us
  waiting for transfers between devices: 1.91 us -> 0 us
  Pallas kernels: 98.4 us -> 100 us
    pallas_call x1, Pallas kernels: 5.02 us -> 7.29 us  [project_call(): pl.pallas_call(project_kernel, in_specs=[hbm, pl.BlockSpec(memory_space=p...]
    ppermute x1 -> x0, waiting for transfers between devices: 1.91 us -> none  [per_device(): received = lax.ppermute(sent, 'mod', swap)]
    unnamed x16 -> x0, local copies, waits for them, and re-layouts: 1.36 us -> none
  transfers between devices with their start and end apart: 1 -> 0, of which waited for: 1 -> 0; matrix products, arithmetic and copies ran while one was open for 2% -> 0% of each run, Pallas kernels for 0% -> 0%
where the time goes in v6:
time: 102 us; the launch traced here: 101 us
  Pallas kernels  100 us (98%)
    pallas_call x1, Pallas kernels, block_call(): pl.pallas_call(block_kernel, grid_spec=pltpu.PrefetchScalarGridSpec(num_s...  59.6 us
    pallas_call x1, Pallas kernels, finish_call(): pl.pallas_call(functools.partial(finish_kernel, n, chunk, gchunk), out_sh...  29.3 us
    pallas_call x1, Pallas kernels, project_call(): pl.pallas_call(project_kernel, in_specs=[hbm, pl.BlockSpec(memory_space=p...  7.29 us
    pallas_call x1, Pallas kernels, unpack_call(): pl.pallas_call(functools.partial(unpack_kernel, chunk), in_specs=[vmem] *...  4.08 us

profile of v6, /device:TPU:25, one launch (start us, length us, event | category | flops | bytes accessed | tf_op | source)
XLA Modules:
  0.0 101.1 jit_solution(1145018503382136784)
XLA Ops:
  0.7 7.3 %project.1.pr = bf16[8192,128]{1,0:T(8,128)(2,1)} custom-call(bf16[16384,256]{1,0:T(8,128)(2,1)} %bitcast.26, bf16[256,128]{1,0:T(8,128)(2,1)} %proj.5), custom_call_target="tpu_custom_call" | custom-call | tf_op jit(solution)/shard_map/project/pallas_call | solution.py:566
  8.0 59.6 %stems_trunk.1 = (bf16[4096,128]{1,0:T(8,128)(2,1)}, bf16[16384,256]{1,0:T(8,128)(2,1)}, bf16[8192,128]{1,0:T(8,128)(2,1)}, bf16[1024,64]{1,0:T(8,128)(2,1)}, bf...) custom-call(s32[1]{0:T(128)} %bitcast.half, s32[4,64]{1,0:T(4,128)} %bitcast.33, bf16[16384,256]{1,0:T(8,128)(2,1)} %bitcast.27, ...), custom_call_target="tpu_custom_call" | custom-call | tf_op jit(solution)/shard_map/stems_trunk/pallas_call | solution.py:516
  67.5 29.3 %finish.1 = (bf16[2,16,96,128]{3,2,1,0:T(8,128)(2,1)S(1)}, bf16[8192,256]{1,0:T(8,128)(2,1)S(1)}) custom-call(bf16[2560,128]{1,0:T(8,128)(2,1)} %get-tuple-element.53.acc, f32[128,256]{1,0:T(8,128)} %get-tuple-element.54.gsum, bf16[8192,128]{1,0:T(8,128)(2,1)} %get-tuple-element.55.dtok, bf16[16384,256]{1,0:T(8,128)(2,1)} %bitcast.28, bf16[256,128]{1,0:T(8,128)(2,1)} %proj.5), custom_call_target="tpu_custom_call" | custom-call | tf_op jit(solution)/shard_map/finish/pallas_call | solution.py:791
  96.9 4.1 %unpack.1 = (bf16[16384,256]{1,0:T(8,128)(2,1)}, f32[256,128]{1,0:T(8,128)}, f32[16,128]{1,0:T(8,128)}, f32[128,128]{1,0:T(8,128)}, f32[128,256]{1,0:T(8,128)}, ...) custom-call(bf16[8192,256]{1,0:T(8,128)(2,1)S(1)} %get-tuple-element, ...), custom_call_target="tpu_custom_call", output_to_operand_aliasing={{0}: (6, {})} | custom-call | tf_op jit(solution)/shard_map/unpack/pallas_call | solution.py:644

commit v7 on v6

--- a/solution.py
+++ b/solution.py
@@ -173,7 +173,7 @@
     half, grid_ref, feats, pr, frames, frame_mask, token_valid, mix_weight, cot, proj,
     vis_query, vis_wq, vis_kv, vis_wo, prop_w1, prop_w2, prop_query, prop_wq, prop_kv, prop_wo,
     ln1_gain, ln1_bias, ln2_gain, ln2_bias, qkv_w, attn_out, mlp_in, mlp_out,
-    out, grad_feats, dtok_ref, dframes, acc_out, gsum,
+    out, grad_feats, dtok_ref, dframes, acc_out,
     masks_ref, qv_ref, qp_ref, wqkv_t, ao_t, win_t, wout_t, stem_t, ln_ref,
     gv_ref, gp_ref, lnacc, stat, acc, fr_ref, df_ref, aux_ref, turn_ref,
 ):
@@ -216,7 +216,6 @@
             block = frames[PROP * j : PROP * j + PROP].astype(F32).T
             fr_ref[pl.ds(j, block.shape[0], stride=frames.shape[0] // PROP)] = block
         acc[...] = jnp.zeros_like(acc)
-        gsum[...] = jnp.zeros_like(gsum)
         gv_ref[...] = jnp.zeros_like(gv_ref)
         gp_ref[...] = jnp.zeros_like(gp_ref)
         lnacc[...] = jnp.zeros_like(lnacc)
@@ -411,7 +410,6 @@
         dtok = nt(dkv, vis_kv[...]).astype(BF)
         dtok_ref[slots] = dtok
         grad_feats[slots] = nt(dtok, proj[...]).astype(BF)
-        gsum[...] += nn(dtok.T, feats[slots])
         grad = nn(tok.T, dkv)
         acc[R_VKV : R_VKV + WIDTH] += grad[:, :WIDTH]
         acc[R_VKV + WIDTH : R_VKV + 2 * WIDTH] += grad[:, WIDTH:]
@@ -483,7 +481,6 @@
         jax.ShapeDtypeStruct((512 * CHAINS * steps, WIDTH), BF),
         jax.ShapeDtypeStruct(frames.shape, BF),
         jax.ShapeDtypeStruct((R_END, WIDTH), BF),
-        jax.ShapeDtypeStruct((WIDTH, channels), F32),
     )
     out_specs = (
         pl.BlockSpec((256 * CHAINS, WIDTH), row),
@@ -491,7 +488,6 @@
         pl.BlockSpec((512 * CHAINS, WIDTH), row),
         whole(frames.shape),
         whole((R_END, WIDTH)),
-        whole((WIDTH, channels)),
     )
     scratch = [
         pltpu.VMEM((12, 16, WIDTH), BF),
@@ -654,8 +650,8 @@
 
 
 def finish_kernel(
-    n, chunk, gchunk, acc, gsum, dtok, feats, proj, total, vision,
-    dother, pbuf, fbuf, gbuf, own_a, recv_a, send_b, recv_b, send_g, recv_g, reduced,
+    n, chunk, gchunk, acc, dtok, feats, proj, total, vision,
+    dother, pbuf, fbuf, dbuf, obuf, own_a, recv_a, send_b, recv_b, send_g, recv_g, reduced,
     sem_t, sem_f, sem_a, sem_b, sem_c, sem_d, sem_g,
 ):
     me, core = lax.axis_index("dp"), lax.axis_index("mod")
@@ -683,8 +679,10 @@
     lax.fori_loop(1, n, greet, 0)
     load_a = pltpu.make_async_copy(acc.at[rows(core, half)], own_a, sem_a.at[2])
     load_a.start()
-    load_g = pltpu.make_async_copy(gsum, gbuf, sem_a.at[3])
-    load_g.start()
+    load_d = pltpu.make_async_copy(dtok, dbuf, sem_a.at[3])
+    load_d.start()
+    load_o = pltpu.make_async_copy(feats.at[rows(core, slots)], obuf, sem_a.at[5])
+    load_o.start()
     load_p = pltpu.make_async_copy(proj, pbuf, sem_a.at[4])
     load_p.start()
     tokens, features = [], []
@@ -736,8 +734,12 @@
 
     each(1, lambda k: scatter(k).start())
 
-    load_g.wait()
-    grad = gbuf[...]
+    load_d.wait()
+    load_o.wait()
+    grad = jnp.zeros((WIDTH, channels), F32)
+    for j in range(FEATURE_STEPS):
+        part = slice(piece * j, piece * j + piece)
+        grad = grad + nn(dbuf[part].T, obuf[part])
     for j in range(FEATURE_STEPS):
         tokens[j].wait()
         features[j].wait()
@@ -780,7 +782,7 @@
     return pltpu.with_memory_space_constraint(value, pltpu.HBM)
 
 
-def finish_call(acc, gsum, dtok, feats, proj, n):
+def finish_call(acc, dtok, feats, proj, n):
     slots, channels = dtok.shape[0], feats.shape[1]
     half = R_END // 2
     chunk = 16 * -(-half // (16 * n))
@@ -794,13 +796,14 @@
             jax.ShapeDtypeStruct((2, n, chunk + gchunk, WIDTH), BF),
             jax.ShapeDtypeStruct((slots, channels), BF),
         ),
-        in_specs=[hbm] * 5,
+        in_specs=[hbm] * 4,
         out_specs=(vmem, vmem),
         scratch_shapes=[
             pltpu.VMEM(dtok.shape, BF),
             pltpu.VMEM(proj.shape, BF),
             pltpu.VMEM((slots, channels), BF),
-            pltpu.VMEM(gsum.shape, F32),
+            pltpu.VMEM(dtok.shape, BF),
+            pltpu.VMEM((slots, channels), BF),
             pltpu.VMEM((half, WIDTH), BF),
             pltpu.VMEM((half, WIDTH), BF),
             pltpu.VMEM((n * chunk, WIDTH), BF),
@@ -810,17 +813,17 @@
             pltpu.VMEM((chunk + gchunk, WIDTH), BF),
             dma((2, FEATURE_STEPS)),
             dma((FEATURE_STEPS,)),
-            dma((5,)),
+            dma((6,)),
             dma((2, n - 1)),
             dma((2, n - 1)),
             dma((2, n)),
             dma((2, n - 1)),
         ],
         compiler_params=pltpu.CompilerParams(
-            collective_id=0, has_side_effects=True, vmem_limit_bytes=28 * 2**20
+            collective_id=0, has_side_effects=True, vmem_limit_bytes=36 * 2**20
         ),
         name="finish",
-    )(*map(in_hbm, (acc, gsum, dtok, feats, proj)))
+    )(*map(in_hbm, (acc, dtok, feats, proj)))
     return chunk, total, vision
 
 
@@ -840,11 +843,11 @@
     frames = jnp.transpose(proprio, (1, 2, 3, 0)).reshape(-1, proprio.shape[0])
     frame_mask = jnp.transpose(proprio_mask, (1, 2, 0)).reshape(-1, proprio_mask.shape[0])
     grid_sizes = jnp.transpose(vision_grid, (1, 2, 0)).reshape(4, -1)
-    output, grad_vision, dtok, dframes, acc, gfeat = block_call(
+    output, grad_vision, dtok, dframes, acc = block_call(
         own, grid_sizes, feats, received, frames, frame_mask, token_valid, mix_weight.reshape(1, -1),
         out_cot.reshape(-1, WIDTH), feat_proj, weights,
     )
-    chunk, total, vision = finish_call(acc, gfeat, dtok, feats, feat_proj, lax.axis_size("dp"))
+    chunk, total, vision = finish_call(acc, dtok, feats, feat_proj, lax.axis_size("dp"))
     grad_vision, *outs = unpack_call(
         chunk, vision, total, vis_query, vis_wq, prop_query, prop_wq, grad_vision
     )

time: 102 us -> 100 us (0.980)
  Pallas kernels: 100 us -> 98.4 us
    pallas_call x1, Pallas kernels: 59.6 us -> 57.7 us  [block_call(): pl.pallas_call(block_kernel, grid_spec=pltpu.PrefetchScalarGridSpec(num_s...]
where the time goes in v7:
time: 100 us; the launch traced here: 99.3 us
  Pallas kernels  98.4 us (98%)
    pallas_call x1, Pallas kernels, block_call(): pl.pallas_call(block_kernel, grid_spec=pltpu.PrefetchScalarGridSpec(num_s...  57.7 us
    pallas_call x1, Pallas kernels, finish_call(): pl.pallas_call(functools.partial(finish_kernel, n, chunk, gchunk), out_sh...  29.3 us
    pallas_call x1, Pallas kernels, project_call(): pl.pallas_call(project_kernel, in_specs=[hbm, pl.BlockSpec(memory_space=p...  7.29 us
    pallas_call x1, Pallas kernels, unpack_call(): pl.pallas_call(functools.partial(unpack_kernel, chunk), in_specs=[vmem] *...  4.08 us

profile of v7, /device:TPU:25, one launch (start us, length us, event | category | flops | bytes accessed | tf_op | source)
XLA Modules:
  0.0 99.3 jit_solution(8689255549401809352)
XLA Ops:
  0.7 7.3 %project.1.pr = bf16[8192,128]{1,0:T(8,128)(2,1)} custom-call(bf16[16384,256]{1,0:T(8,128)(2,1)} %bitcast.26, bf16[256,128]{1,0:T(8,128)(2,1)} %proj.5), custom_call_target="tpu_custom_call" | custom-call | tf_op jit(solution)/shard_map/project/pallas_call | solution.py:562
  8.0 57.7 %stems_trunk.1 = (bf16[4096,128]{1,0:T(8,128)(2,1)}, bf16[16384,256]{1,0:T(8,128)(2,1)}, bf16[8192,128]{1,0:T(8,128)(2,1)}, bf16[1024,64]{1,0:T(8,128)(2,1)}, bf16[2560,128]{1,0:T(8,128)(2,1)}) custom-call(s32[1]{0:T(128)} %bitcast.half, s32[4,64]{1,0:T(4,128)} %bitcast.33, bf16[16384,256]{1,0:T(8,128)(2,1)} %bitcast.27, bf16[8192,128]{1,0:T(8,128)(2,1)} %project.1.pr, ...), custom_call_target="tpu_custom_call" | custom-call | tf_op jit(solution)/shard_map/stems_trunk/pallas_call | solution.py:512
  65.7 29.3 %finish.1 = (bf16[2,16,96,128]{3,2,1,0:T(8,128)(2,1)S(1)}, bf16[8192,256]{1,0:T(8,128)(2,1)S(1)}) custom-call(bf16[2560,128]{1,0:T(8,128)(2,1)} %get-tuple-element.52.acc, bf16[8192,128]{1,0:T(8,128)(2,1)} %get-tuple-element.53.dtok, bf16[16384,256]{1,0:T(8,128)(2,1)} %bitcast.28, bf16[256,128]{1,0:T(8,128)(2,1)} %proj.5), custom_call_target="tpu_custom_call" | custom-call | tf_op jit(solution)/shard_map/finish/pallas_call | solution.py:793
  95.0 4.1 %unpack.1 = (bf16[16384,256]{1,0:T(8,128)(2,1)}, f32[256,128]{1,0:T(8,128)}, f32[16,128]{1,0:T(8,128)}, f32[128,128]{1,0:T(8,128)}, f32[128,256]{1,0:T(8,128)}, ...) custom-call(bf16[8192,256]{1,0:T(8,128)(2,1)S(1)} %get-tuple-element, ...), custom_call_target="tpu_custom_call", output_to_operand_aliasing={{0}: (6, {})} | custom-call | tf_op jit(solution)/shard_map/unpack/pallas_call | solution.py:640

commit v8 on v7

--- a/solution.py
+++ b/solution.py
@@ -434,7 +434,7 @@
 
         yield
 
-    live = [(g // 2 * 6, chain(g)) for g in range(CHAINS)]
+    live = [(g // 2 * 5, chain(g)) for g in range(CHAINS)]
     tick = 0
     while live:
         for one in list(live):

time: 100 us -> 98.4 us (0.984)
  Pallas kernels: 98.4 us -> 96.9 us
    pallas_call x1, Pallas kernels: 57.7 us -> 56.1 us  [block_call(): pl.pallas_call(block_kernel, grid_spec=pltpu.PrefetchScalarGridSpec(num_s...]
where the time goes in v8:
time: 98.4 us; the launch traced here: 97.7 us
  Pallas kernels  96.9 us (98%)
    pallas_call x1, Pallas kernels, block_call(): pl.pallas_call(block_kernel, grid_spec=pltpu.PrefetchScalarGridSpec(num_s...  56.1 us
    pallas_call x1, Pallas kernels, finish_call(): pl.pallas_call(functools.partial(finish_kernel, n, chunk, gchunk), out_sh...  29.3 us
    pallas_call x1, Pallas kernels, project_call(): pl.pallas_call(project_kernel, in_specs=[hbm, pl.BlockSpec(memory_space=p...  7.29 us
    pallas_call x1, Pallas kernels, unpack_call(): pl.pallas_call(functools.partial(unpack_kernel, chunk), in_specs=[vmem] *...  4.08 us

profile of v8, /device:TPU:25, one launch (start us, length us, event | category | flops | bytes accessed | tf_op | source)
XLA Modules:
  0.0 97.7 jit_solution(11523072700844557985)
XLA Ops:
  0.7 7.3 %project.1.pr = bf16[8192,128]{1,0:T(8,128)(2,1)} custom-call(bf16[16384,256]{1,0:T(8,128)(2,1)} %bitcast.26, bf16[256,128]{1,0:T(8,128)(2,1)} %proj.5), custom_call_target="tpu_custom_call" | custom-call | tf_op jit(solution)/shard_map/project/pallas_call | solution.py:562
  8.0 56.1 %stems_trunk.1 = (bf16[4096,128]{1,0:T(8,128)(2,1)}, bf16[16384,256]{1,0:T(8,128)(2,1)}, bf16[8192,128]{1,0:T(8,128)(2,1)}, bf16[1024,64]{1,0:T(8,128)(2,1)}, bf16[2560,128]{1,0:T(8,128)(2,1)}) custom-call(s32[1]{0:T(128)} %bitcast.half, s32[4,64]{1,0:T(4,128)} %bitcast.33, bf16[16384,256]{1,0:T(8,128)(2,1)} %bitcast.27, bf16[8192,128]{1,0:T(8,128)(2,1)} %project.1.pr, ...), custom_call_target="tpu_custom_call" | custom-call | tf_op jit(solution)/shard_map/stems_trunk/pallas_call | solution.py:512
  64.1 29.3 %finish.1 = (bf16[2,16,96,128]{3,2,1,0:T(8,128)(2,1)S(1)}, bf16[8192,256]{1,0:T(8,128)(2,1)S(1)}) custom-call(bf16[2560,128]{1,0:T(8,128)(2,1)} %get-tuple-element.52.acc, bf16[8192,128]{1,0:T(8,128)(2,1)} %get-tuple-element.53.dtok, bf16[16384,256]{1,0:T(8,128)(2,1)} %bitcast.28, bf16[256,128]{1,0:T(8,128)(2,1)} %proj.5), custom_call_target="tpu_custom_call" | custom-call | tf_op jit(solution)/shard_map/finish/pallas_call | solution.py:793
  93.5 4.1 %unpack.1 = (bf16[16384,256]{1,0:T(8,128)(2,1)}, f32[256,128]{1,0:T(8,128)}, f32[16,128]{1,0:T(8,128)}, f32[128,128]{1,0:T(8,128)}, f32[128,256]{1,0:T(8,128)}, ...) custom-call(bf16[8192,256]{1,0:T(8,128)(2,1)S(1)} %get-tuple-element, ...), custom_call_target="tpu_custom_call", output_to_operand_aliasing={{0}: (6, {})} | custom-call | tf_op jit(solution)/shard_map/unpack/pallas_call | solution.py:640

commit v9 on v8

--- a/solution.py
+++ b/solution.py
@@ -584,9 +584,14 @@
 ):
     core = lax.axis_index("mod")
     slots, channels = vision.shape
-    start = pl.multiple_of((1 - core) * slots, 16)
-    copy = pltpu.make_async_copy(vision, o_vision.at[pl.ds(start, slots)], sem)
-    copy.start()
+    piece = slots // FEATURE_STEPS
+    copies = []
+    for j in range(FEATURE_STEPS):
+        start = pl.multiple_of((1 - core) * slots + piece * j, 16)
+        copies.append(
+            pltpu.make_async_copy(vision.at[pl.ds(piece * j, piece)], o_vision.at[pl.ds(start, piece)], sem.at[j])
+        )
+        copies[j].start()
 
     n = total.shape[1]
     halves = [total[j, :, :chunk].reshape(n * chunk, WIDTH) for j in range(2)]
@@ -626,7 +631,8 @@
     sums = [jnp.sum(small[R_STAT - R_LN + j : R_STAT - R_LN + j + 1], axis=1, keepdims=True) for j in range(4)]
     for j in range(3):
         o_rms[j] = jnp.sum(jnp.sqrt(sums[j] / (sums[3] * WIDTH)))
-    copy.wait()
+    for copy in copies:
+        copy.wait()
 
 
 def unpack_call(chunk, vision, total, vis_query, vis_wq, prop_query, prop_wq, grad_vision):
@@ -642,7 +648,7 @@
         in_specs=[vmem] * 6 + [hbm],
         out_specs=[hbm] + [vmem] * (len(shapes) - 1) + [pl.BlockSpec(memory_space=pltpu.SMEM)],
         out_shape=[jax.ShapeDtypeStruct(grad_vision.shape, BF)] + [jax.ShapeDtypeStruct(s, F32) for s in shapes],
-        scratch_shapes=[pltpu.SemaphoreType.DMA],
+        scratch_shapes=[pltpu.SemaphoreType.DMA((FEATURE_STEPS,))],
         input_output_aliases={6: 0},
         compiler_params=pltpu.CompilerParams(vmem_limit_bytes=20 * 2**20),
         name="unpack",
@@ -652,7 +658,7 @@
 def finish_kernel(
     n, chunk, gchunk, acc, dtok, feats, proj, total, vision,
     dother, pbuf, fbuf, dbuf, obuf, own_a, recv_a, send_b, recv_b, send_g, recv_g, reduced,
-    sem_t, sem_f, sem_a, sem_b, sem_c, sem_d, sem_g,
+    sem_t, sem_f, sem_o, sem_a, sem_b, sem_c, sem_d, sem_g,
 ):
     me, core = lax.axis_index("dp"), lax.axis_index("mod")
     mesh = pl.DeviceIdType.MESH
@@ -681,8 +687,12 @@
     load_a.start()
     load_d = pltpu.make_async_copy(dtok, dbuf, sem_a.at[3])
     load_d.start()
-    load_o = pltpu.make_async_copy(feats.at[rows(core, slots)], obuf, sem_a.at[5])
-    load_o.start()
+    own_loads = []
+    for j in range(FEATURE_STEPS):
+        start_row = pl.multiple_of(core * slots + piece * j, 16)
+        part = pl.ds(piece * j, piece)
+        own_loads.append(pltpu.make_async_copy(feats.at[pl.ds(start_row, piece)], obuf.at[part], sem_o.at[j]))
+        own_loads[j].start()
     load_p = pltpu.make_async_copy(proj, pbuf, sem_a.at[4])
     load_p.start()
     tokens, features = [], []
@@ -735,10 +745,10 @@
     each(1, lambda k: scatter(k).start())
 
     load_d.wait()
-    load_o.wait()
     grad = jnp.zeros((WIDTH, channels), F32)
     for j in range(FEATURE_STEPS):
         part = slice(piece * j, piece * j + piece)
+        own_loads[j].wait()
         grad = grad + nn(dbuf[part].T, obuf[part])
     for j in range(FEATURE_STEPS):
         tokens[j].wait()
@@ -813,7 +823,8 @@
             pltpu.VMEM((chunk + gchunk, WIDTH), BF),
             dma((2, FEATURE_STEPS)),
             dma((FEATURE_STEPS,)),
-            dma((6,)),
+            dma((FEATURE_STEPS,)),
+            dma((5,)),
             dma((2, n - 1)),
             dma((2, n - 1)),
             dma((2, n)),

time: 98.4 us -> 98.4 us (level)
  no operation moved by 1% of the time
where the time goes in v9:
time: 98.4 us; the launch traced here: 97.8 us
  Pallas kernels  96.9 us (98%)
    pallas_call x1, Pallas kernels, block_call(): pl.pallas_call(block_kernel, grid_spec=pltpu.PrefetchScalarGridSpec(num_s...  56.1 us
    pallas_call x1, Pallas kernels, finish_call(): pl.pallas_call(functools.partial(finish_kernel, n, chunk, gchunk), out_sh...  29.4 us
    pallas_call x1, Pallas kernels, project_call(): pl.pallas_call(project_kernel, in_specs=[hbm, pl.BlockSpec(memory_space=p...  7.29 us
    pallas_call x1, Pallas kernels, unpack_call(): pl.pallas_call(functools.partial(unpack_kernel, chunk), in_specs=[vmem] *...  4.1 us

profile of v9, /device:TPU:25, one launch (start us, length us, event | category | flops | bytes accessed | tf_op | source)
XLA Modules:
  0.0 97.8 jit_solution(11746946236425210739)
XLA Ops:
  0.7 7.3 %project.1.pr = bf16[8192,128]{1,0:T(8,128)(2,1)} custom-call(bf16[16384,256]{1,0:T(8,128)(2,1)} %bitcast.26, bf16[256,128]{1,0:T(8,128)(2,1)} %proj.5), custom_call_target="tpu_custom_call" | custom-call | tf_op jit(solution)/shard_map/project/pallas_call | solution.py:562
  8.0 56.1 %stems_trunk.1 = (bf16[4096,128]{1,0:T(8,128)(2,1)}, bf16[16384,256]{1,0:T(8,128)(2,1)}, bf16[8192,128]{1,0:T(8,128)(2,1)}, bf16[1024,64]{1,0:T(8,128)(2,1)}, bf16[2560,128]{1,0:T(8,128)(2,1)}) custom-call(s32[1]{0:T(128)} %bitcast.half, s32[4,64]{1,0:T(4,128)} %bitcast.33, bf16[16384,256]{1,0:T(8,128)(2,1)} %bitcast.27, bf16[8192,128]{1,0:T(8,128)(2,1)} %project.1.pr, ...), custom_call_target="tpu_custom_call" | custom-call | tf_op jit(solution)/shard_map/stems_trunk/pallas_call | solution.py:512
  64.1 29.4 %finish.1 = (bf16[2,16,96,128]{3,2,1,0:T(8,128)(2,1)S(1)}, bf16[8192,256]{1,0:T(8,128)(2,1)S(1)}) custom-call(bf16[2560,128]{1,0:T(8,128)(2,1)} %get-tuple-element.52.acc, bf16[8192,128]{1,0:T(8,128)(2,1)} %get-tuple-element.53.dtok, bf16[16384,256]{1,0:T(8,128)(2,1)} %bitcast.28, bf16[256,128]{1,0:T(8,128)(2,1)} %proj.5), custom_call_target="tpu_custom_call" | custom-call | tf_op jit(solution)/shard_map/finish/pallas_call | solution.py:803
  93.5 4.1 %unpack.1 = (bf16[16384,256]{1,0:T(8,128)(2,1)}, f32[256,128]{1,0:T(8,128)}, f32[16,128]{1,0:T(8,128)}, f32[128,128]{1,0:T(8,128)}, f32[128,256]{1,0:T(8,128)}, ...) custom-call(bf16[8192,256]{1,0:T(8,128)(2,1)S(1)} %get-tuple-element, ...), custom_call_target="tpu_custom_call", output_to_operand_aliasing={{0}: (6, {})} | custom-call | tf_op jit(solution)/shard_map/unpack/pallas_call | solution.py:646
